TPU v7x, 32 devices: a whole 2x2x4 slice. The times are simulated.
32 devices in a mesh: tm: 8 (over z, y), space: 4 (over x, core).
Axes of the slice: x: 2, y: 2, z: 4, core: 2. Of those that a mesh axis runs over, the one named last changes fastest.
Arguments:
- iterate: float32 [2, 16, 32, 4096], P(None, 'tm', 'space'), may hold values from -6 to 6
- forcing: float32 [2, 16, 32, 4096], P(None, 'tm', 'space'), may hold values from -6 to 6
Outputs:
- smoothed: float32 [2, 16, 32, 4096], P(None, 'tm', 'space')
- coarse: float32 [2, 16, 32, 4096], P(None, 'tm', 'space')
All inputs are finite; a program needn't handle non-finite values.
Results may differ from a plain program's by a relative error of at most 0.00002.
Values sent between devices are 32-bit elements; how exact they have to be, the bound alone decides.
No kernel may reach another device: no remote copies, remote signals or barrier semaphores. Data moves between devices by JAX's collectives and lax.ppermute only.
A program may use at most 320 MiB of HBM per device.

v0:
```python
import jax
import jax.numpy as jnp
from jax import lax
from jax.sharding import PartitionSpec as P

NY = 64


KAPPA_BASE = 0.25
COUPLING_BASE = 0.5
DAMPING = 0.6


def extended_2(array, sides, width):
    for axis, dim in sides:
        size, length = (lax.axis_size(axis), array.shape[dim])
        up = [(i, (i + 1) % size) for i in range(size - 1)]
        down = [(j, i) for i, j in up]
        last = lax.slice_in_dim(array, length - width, length, axis=dim)
        first = lax.slice_in_dim(array, 0, width, axis=dim)
        before = lax.ppermute(last, axis, up)
        after = lax.ppermute(first, axis, down)
        array = jnp.concatenate([before, array, after], axis=dim)
    return array


def from_behind(array, axis, by):
    size = lax.axis_size(axis)
    pairs = [(i, i + by) for i in range(size) if 0 <= i + by < size]
    return lax.ppermute(array, axis, pairs)


def swapped(value, axis, bit):
    mask = 2**bit
    pairs = [(source, source ^ mask) for source in range(lax.axis_size(axis))]
    return lax.ppermute(value, axis, pairs)


def neighbour_plane(values, row_cells):
    length = values.shape[-1]
    columns = jnp.arange(length, dtype=jnp.int32) % row_cells
    single = jnp.zeros(values.shape[:-1] + (1,), jnp.float32)
    row_zero = jnp.zeros(values.shape[:-1] + (row_cells,), jnp.float32)
    left_side = jnp.where(columns != 0, jnp.concatenate([single, values[..., :-1]], -1), 0.0)
    right_side = jnp.where(
        columns != row_cells - 1, jnp.concatenate([values[..., 1:], single], -1), 0.0
    )
    upper_side = jnp.concatenate([row_zero, values[..., :-row_cells]], -1)
    lower_side = jnp.concatenate([values[..., row_cells:], row_zero], -1)
    return left_side + right_side + upper_side + lower_side


def operate(fields, extended, prev_state, next_adjoint, diffusion, coupling):
    neighbours = extended[:, :, 2:] + extended[:, :, :-2] + neighbour_plane(fields, NY)
    centre = 1.0 + 6.0 * diffusion
    state = fields[0]
    adjoint = fields[1]
    state_before = jnp.concatenate([prev_state, state[:-1]], 0)
    adjoint_after = jnp.concatenate([adjoint[1:], next_adjoint], 0)
    image_state = centre * state - diffusion * neighbours[0] - state_before + coupling * adjoint
    image_adjoint = centre * adjoint - diffusion * neighbours[1] - adjoint_after - coupling * state
    return jnp.stack([image_state, image_adjoint])


def relax(fields, defect, diffusion, coupling):
    centre = 1.0 + 6.0 * diffusion
    determinant = centre * centre + coupling * coupling
    along = DAMPING * centre / determinant
    across = DAMPING * coupling / determinant
    update = jnp.stack(
        [along * defect[0] - across * defect[1], across * defect[0] + along * defect[1]]
    )
    return fields + update


def apply_level(fields, diffusion, coupling, stride):
    extended = extended_2(fields, (("space", 2),), 1)
    blank_plane = jnp.zeros((1,) + fields.shape[2:], jnp.float32)
    prev_state = blank_plane
    next_adjoint = blank_plane
    if stride > 0:
        prev_state = from_behind(fields[0, -1:], "tm", stride)
        next_adjoint = from_behind(fields[1, :1], "tm", -stride)
    return operate(fields, extended, prev_state, next_adjoint, diffusion, coupling)


def local(iterate, forcing):
    time_devices = lax.axis_size("tm")
    total_steps = forcing.shape[1] * time_devices
    level_count = total_steps.bit_length()
    fields = iterate
    source = forcing
    smoothed = iterate
    stride_now = 1
    pair_bit = 0
    for level_index in range(level_count):
        diffusion = KAPPA_BASE * 2.0**level_index
        coupling = COUPLING_BASE * 2.0**level_index
        steps_here = total_steps >> level_index
        stride = stride_now if steps_here > 1 else 0
        for sweep_index in range(2):
            if level_index > 0 and sweep_index == 0:
                defect = source
            else:
                defect = source - apply_level(fields, diffusion, coupling, stride)
            fields = relax(fields, defect, diffusion, coupling)
        if level_index == 0:
            smoothed = fields
        if level_index < level_count - 1:
            defect = source - apply_level(fields, diffusion, coupling, stride)
            count_now = defect.shape[1]
            if count_now >= 2:
                paired = defect.reshape(2, count_now // 2, 2, defect.shape[2], defect.shape[3])
                source = paired[:, :, 0] + paired[:, :, 1]
            else:
                partner = swapped(defect, "tm", pair_bit)
                source = defect + partner
                pair_bit = pair_bit + 1
                stride_now = stride_now * 2
            fields = jnp.zeros_like(source)
    coarse = jnp.broadcast_to(fields, iterate.shape)
    return (smoothed, coarse)


def solution(mesh):
    in_specs = (P(None, "tm", "space", None), P(None, "tm", "space", None))
    out_specs = (P(None, "tm", "space", None), P(None, "tm", "space", None))
    return jax.shard_map(local, mesh=mesh, in_specs=in_specs, out_specs=out_specs, check_vma=False)
```

profile of v0, /device:TPU:0, one launch (start us, length us, event | category | flops | bytes accessed | tf_op | source)
XLA Modules:
  0.0 197.9 jit_solution(2836485608091107849)
XLA Ops:
  3.3 3.2 %collective-permute-start.1 = (f32[2,2,1,4096]{3,2,1,0:T(1,128)S(1)}, f32[2,2,1,4096]{3,2,1,0:T(1,128)S(1)}, u32[]{:S(2)}, u32[]{:S(2)}) collective-permute-start(f32[2,2,1,4096]{3,2,1,0:T(1,128)S(1)} %get-tuple-element.57), channel_id=1, source_target_pairs={{0,1},{1,2},{2,3},{4,5},{5,6},{6,7},{8,9},{9,10},{10,11},{12,13},{... | collective-permute-start | bytes 196616 | tf_op jit(solution)/shard_map/ppermute | solution.py:21
  7.6 4.9 %collective-permute-start.2 = (f32[1,8,4096]{2,1,0:T(8,128)S(1)}, f32[1,8,4096]{2,1,0:T(8,128)S(1)}, u32[]{:S(2)}, u32[]{:S(2)}) collective-permute-start(f32[1,8,4096]{2,1,0:T(8,128)S(1)} %get-tuple-element.48), channel_id=1, source_target_pairs={{0,4},{4,8},{8,12},{12,16},{16,20},{20,24},{24,28},{1,5},{5,9},{9,... | collective-permute-start | bytes 393224 | tf_op jit(solution)/shard_map/ppermute | solution.py:30
  16.2 4.4 %collective-permute-done.3 = f32[1,8,4096]{2,1,0:T(8,128)S(1)} collective-permute-done((f32[1,8,4096]{2,1,0:T(8,128)S(1)}, f32[1,8,4096]{2,1,0:T(8,128)S(1)}, u32[]{:S(2)}, u32[]{:S(2)}) %collective-permute-start.3) | collective-permute-done | bytes 131104 | tf_op jit(solution)/shard_map/ppermute | solution.py:30
  23.7 3.0 %collective-permute-start.5 = (f32[2,2,1,4096]{3,2,1,0:T(1,128)S(1)}, f32[2,2,1,4096]{3,2,1,0:T(1,128)S(1)}, u32[]{:S(2)}, u32[]{:S(2)}) collective-permute-start(f32[2,2,1,4096]{3,2,1,0:T(1,128)S(1)} %get-tuple-element.45), channel_id=1, source_target_pairs={{0,1},{1,2},{2,3},{4,5},{5,6},{6,7},{8,9},{9,10},{10,11},{12,13},{... | collective-permute-start | bytes 196616 | tf_op jit(solution)/shard_map/ppermute | solution.py:21
  26.8 4.3 %collective-permute-start.6 = (f32[1,8,4096]{2,1,0:T(8,128)S(1)}, f32[1,8,4096]{2,1,0:T(8,128)S(1)}, u32[]{:S(2)}, u32[]{:S(2)}) collective-permute-start(f32[1,8,4096]{2,1,0:T(8,128)S(1)} %get-tuple-element.36), channel_id=1, source_target_pairs={{0,4},{4,8},{8,12},{12,16},{16,20},{20,24},{24,28},{1,5},{5,9},{9,... | collective-permute-start | bytes 393224 | tf_op jit(solution)/shard_map/ppermute | solution.py:30
  34.7 4.6 %collective-permute-done.7 = f32[1,8,4096]{2,1,0:T(8,128)S(1)} collective-permute-done((f32[1,8,4096]{2,1,0:T(8,128)S(1)}, f32[1,8,4096]{2,1,0:T(8,128)S(1)}, u32[]{:S(2)}, u32[]{:S(2)}) %collective-permute-start.7) | collective-permute-done | bytes 131104 | tf_op jit(solution)/shard_map/ppermute | solution.py:30
  41.5 3.0 %collective-permute-start.9 = (f32[2,2,1,4096]{3,2,1,0:T(1,128)S(1)}, f32[2,2,1,4096]{3,2,1,0:T(1,128)S(1)}, u32[]{:S(2)}, u32[]{:S(2)}) collective-permute-start(f32[2,2,1,4096]{3,2,1,0:T(1,128)S(1)} %get-tuple-element.33), channel_id=1, source_target_pairs={{0,1},{1,2},{2,3},{4,5},{5,6},{6,7},{8,9},{9,10},{10,11},{12,13},{... | collective-permute-start | bytes 196616 | tf_op jit(solution)/shard_map/ppermute | solution.py:21
  45.9 4.6 %collective-permute-start.10 = (f32[1,8,4096]{2,1,0:T(8,128)S(1)}, f32[1,8,4096]{2,1,0:T(8,128)S(1)}, u32[]{:S(2)}, u32[]{:S(2)}) collective-permute-start(f32[1,8,4096]{2,1,0:T(8,128)S(1)} %get-tuple-element.24), channel_id=1, source_target_pairs={{0,4},{4,8},{8,12},{12,16},{16,20},{20,24},{24,28},{1,5},{5,9},{9,... | collective-permute-start | bytes 393224 | tf_op jit(solution)/shard_map/ppermute | solution.py:30
  52.4 3.5 %collective-permute-done.10 = f32[1,8,4096]{2,1,0:T(8,128)S(1)} collective-permute-done((f32[1,8,4096]{2,1,0:T(8,128)S(1)}, f32[1,8,4096]{2,1,0:T(8,128)S(1)}, u32[]{:S(2)}, u32[]{:S(2)}) %collective-permute-start.10) | collective-permute-done | bytes 131104 | tf_op jit(solution)/shard_map/ppermute | solution.py:30
  60.9 4.4 %collective-permute-start.14 = (f32[1,8,4096]{2,1,0:T(8,128)S(1)}, f32[1,8,4096]{2,1,0:T(8,128)S(1)}, u32[]{:S(2)}, u32[]{:S(2)}) collective-permute-start(f32[1,8,4096]{2,1,0:T(8,128)S(1)} %get-tuple-element.22), channel_id=1, source_target_pairs={{0,4},{4,8},{8,12},{12,16},{16,20},{20,24},{24,28},{1,5},{5,9},{9,... | collective-permute-start | bytes 393224 | tf_op jit(solution)/shard_map/ppermute | solution.py:30
  65.6 3.3 %collective-permute-done.14 = f32[1,8,4096]{2,1,0:T(8,128)S(1)} collective-permute-done((f32[1,8,4096]{2,1,0:T(8,128)S(1)}, f32[1,8,4096]{2,1,0:T(8,128)S(1)}, u32[]{:S(2)}, u32[]{:S(2)}) %collective-permute-start.14) | collective-permute-done | bytes 131104 | tf_op jit(solution)/shard_map/ppermute | solution.py:30
  70.2 6.9 %collective-permute-done.15 = f32[1,8,4096]{2,1,0:T(8,128)S(1)} collective-permute-done((f32[1,8,4096]{2,1,0:T(8,128)S(1)}, f32[1,8,4096]{2,1,0:T(8,128)S(1)}, u32[]{:S(2)}, u32[]{:S(2)}) %collective-permute-start.15) | collective-permute-done | bytes 131104 | tf_op jit(solution)/shard_map/ppermute | solution.py:30
  82.0 4.8 %collective-permute-start.18 = (f32[1,8,4096]{2,1,0:T(8,128)S(1)}, f32[1,8,4096]{2,1,0:T(8,128)S(1)}, u32[]{:S(2)}, u32[]{:S(2)}) collective-permute-start(f32[1,8,4096]{2,1,0:T(8,128)S(1)} %get-tuple-element.102), channel_id=1, source_target_pairs={{0,4},{4,8},{8,12},{12,16},{16,20},{20,24},{24,28},{1,5},{5,9},{9,... | collective-permute-start | bytes 393224 | tf_op jit(solution)/shard_map/ppermute | solution.py:30
  90.4 4.1 %collective-permute-done.19 = f32[1,8,4096]{2,1,0:T(8,128)S(1)} collective-permute-done((f32[1,8,4096]{2,1,0:T(8,128)S(1)}, f32[1,8,4096]{2,1,0:T(8,128)S(1)}, u32[]{:S(2)}, u32[]{:S(2)}) %collective-permute-start.19) | collective-permute-done | bytes 131104 | tf_op jit(solution)/shard_map/ppermute | solution.py:30
  97.1 5.9 %collective-permute-done.20 = f32[2,1,8,4096]{3,2,1,0:T(8,128)S(1)} collective-permute-done((f32[2,1,8,4096]{3,2,1,0:T(8,128)S(1)}, f32[2,1,8,4096]{3,2,1,0:T(8,128)S(1)}, u32[]{:S(2)}, u32[]{:S(2)}) %collective-permute-start.20) | collective-permute-done | bytes 262176 | tf_op jit(solution)/shard_map/ppermute | solution.py:36
  107.7 4.0 %collective-permute-start.23 = (f32[1,8,4096]{2,1,0:T(8,128)S(1)}, f32[1,8,4096]{2,1,0:T(8,128)S(1)}, u32[]{:S(2)}, u32[]{:S(2)}) collective-permute-start(f32[1,8,4096]{2,1,0:T(8,128)S(1)} %bitcast.250), channel_id=1, source_target_pairs={{0,8},{4,12},{8,16},{12,20},{16,24},{20,28},{1,9},{5,13},{9,17},{1... | collective-permute-start | bytes 393224 | tf_op jit(solution)/shard_map/ppermute | solution.py:30
  115.1 4.1 %collective-permute-done.24 = f32[1,8,4096]{2,1,0:T(8,128)S(1)} collective-permute-done((f32[1,8,4096]{2,1,0:T(8,128)S(1)}, f32[1,8,4096]{2,1,0:T(8,128)S(1)}, u32[]{:S(2)}, u32[]{:S(2)}) %collective-permute-start.24) | collective-permute-done | bytes 131104 | tf_op jit(solution)/shard_map/ppermute | solution.py:30
  124.1 3.5 %collective-permute-start.27 = (f32[1,8,4096]{2,1,0:T(8,128)S(1)}, f32[1,8,4096]{2,1,0:T(8,128)S(1)}, u32[]{:S(2)}, u32[]{:S(2)}) collective-permute-start(f32[1,8,4096]{2,1,0:T(8,128)S(1)} %get-tuple-element.84), channel_id=1, source_target_pairs={{0,8},{4,12},{8,16},{12,20},{16,24},{20,28},{1,9},{5,13},{9,17},{1... | collective-permute-start | bytes 393224 | tf_op jit(solution)/shard_map/ppermute | solution.py:30
  131.1 4.1 %collective-permute-done.28 = f32[1,8,4096]{2,1,0:T(8,128)S(1)} collective-permute-done((f32[1,8,4096]{2,1,0:T(8,128)S(1)}, f32[1,8,4096]{2,1,0:T(8,128)S(1)}, u32[]{:S(2)}, u32[]{:S(2)}) %collective-permute-start.28) | collective-permute-done | bytes 131104 | tf_op jit(solution)/shard_map/ppermute | solution.py:30
  137.0 6.1 %collective-permute-done.29 = f32[2,1,8,4096]{3,2,1,0:T(8,128)S(1)} collective-permute-done((f32[2,1,8,4096]{3,2,1,0:T(8,128)S(1)}, f32[2,1,8,4096]{3,2,1,0:T(8,128)S(1)}, u32[]{:S(2)}, u32[]{:S(2)}) %collective-permute-start.29) | collective-permute-done | bytes 262176 | tf_op jit(solution)/shard_map/ppermute | solution.py:36
  147.9 3.5 %collective-permute-start.32 = (f32[1,8,4096]{2,1,0:T(8,128)S(1)}, f32[1,8,4096]{2,1,0:T(8,128)S(1)}, u32[]{:S(2)}, u32[]{:S(2)}) collective-permute-start(f32[1,8,4096]{2,1,0:T(8,128)S(1)} %bitcast.252), channel_id=1, source_target_pairs={{0,16},{4,20},{8,24},{12,28},{1,17},{5,21},{9,25},{13,29},{2,18},{... | collective-permute-start | bytes 393224 | tf_op jit(solution)/shard_map/ppermute | solution.py:30
  154.6 7.8 %collective-permute-done.33 = f32[1,8,4096]{2,1,0:T(8,128)S(1)} collective-permute-done((f32[1,8,4096]{2,1,0:T(8,128)S(1)}, f32[1,8,4096]{2,1,0:T(8,128)S(1)}, u32[]{:S(2)}, u32[]{:S(2)}) %collective-permute-start.33) | collective-permute-done | bytes 131104 | tf_op jit(solution)/shard_map/ppermute | solution.py:30
  172.3 6.9 %collective-permute-done.37 = f32[1,8,4096]{2,1,0:T(8,128)S(1)} collective-permute-done((f32[1,8,4096]{2,1,0:T(8,128)S(1)}, f32[1,8,4096]{2,1,0:T(8,128)S(1)}, u32[]{:S(2)}, u32[]{:S(2)}) %collective-permute-start.37) | collective-permute-done | bytes 131104 | tf_op jit(solution)/shard_map/ppermute | solution.py:30
  179.4 11.7 %collective-permute-done.38 = f32[2,1,8,4096]{3,2,1,0:T(8,128)S(1)} collective-permute-done((f32[2,1,8,4096]{3,2,1,0:T(8,128)S(1)}, f32[2,1,8,4096]{3,2,1,0:T(8,128)S(1)}, u32[]{:S(2)}, u32[]{:S(2)}) %collective-permute-start.38) | collective-permute-done | bytes 262176 | tf_op jit(solution)/shard_map/ppermute | solution.py:36
  (155 shorter events, 79.6 us)
Async XLA Ops:
  2.0 12.2 %collective-permute-start = (f32[2,2,1,4096]{3,2,1,0:T(1,128)S(1)}, f32[2,2,1,4096]{3,2,1,0:T(1,128)S(1)}, u32[]{:S(2)}, u32[]{:S(2)}) collective-permute-start(f32[2,2,1,4096]{3,2,1,0:T(1,128)S(1)} %get-tuple-element.56), channel_id=1, source_target_pairs={{1,0},{2,1},{3,2},{5,4},{6,5},{7,6},{9,8},{10,9},{11,10},{13,12},{... | collective-permute-start | bytes 196616 | tf_op jit(solution)/shard_map/ppermute | solution.py:22
  3.3 10.9 %collective-permute-start.1 = (f32[2,2,1,4096]{3,2,1,0:T(1,128)S(1)}, f32[2,2,1,4096]{3,2,1,0:T(1,128)S(1)}, u32[]{:S(2)}, u32[]{:S(2)}) collective-permute-start(f32[2,2,1,4096]{3,2,1,0:T(1,128)S(1)} %get-tuple-element.57), channel_id=1, source_target_pairs={{0,1},{1,2},{2,3},{4,5},{5,6},{6,7},{8,9},{9,10},{10,11},{12,13},{... | collective-permute-start | bytes 196616 | tf_op jit(solution)/shard_map/ppermute | solution.py:21
  7.6 8.6 %collective-permute-start.2 = (f32[1,8,4096]{2,1,0:T(8,128)S(1)}, f32[1,8,4096]{2,1,0:T(8,128)S(1)}, u32[]{:S(2)}, u32[]{:S(2)}) collective-permute-start(f32[1,8,4096]{2,1,0:T(8,128)S(1)} %get-tuple-element.48), channel_id=1, source_target_pairs={{0,4},{4,8},{8,12},{12,16},{16,20},{20,24},{24,28},{1,5},{5,9},{9,... | collective-permute-start | bytes 393224 | tf_op jit(solution)/shard_map/ppermute | solution.py:30
  12.5 8.1 %collective-permute-start.3 = (f32[1,8,4096]{2,1,0:T(8,128)S(1)}, f32[1,8,4096]{2,1,0:T(8,128)S(1)}, u32[]{:S(2)}, u32[]{:S(2)}) collective-permute-start(f32[1,8,4096]{2,1,0:T(8,128)S(1)} %get-tuple-element.51), channel_id=1, source_target_pairs={{4,0},{8,4},{12,8},{16,12},{20,16},{24,20},{28,24},{5,1},{9,5},{13... | collective-permute-start | bytes 393224 | tf_op jit(solution)/shard_map/ppermute | solution.py:30
  22.4 10.0 %collective-permute-start.4 = (f32[2,2,1,4096]{3,2,1,0:T(1,128)S(1)}, f32[2,2,1,4096]{3,2,1,0:T(1,128)S(1)}, u32[]{:S(2)}, u32[]{:S(2)}) collective-permute-start(f32[2,2,1,4096]{3,2,1,0:T(1,128)S(1)} %get-tuple-element.44), channel_id=1, source_target_pairs={{1,0},{2,1},{3,2},{5,4},{6,5},{7,6},{9,8},{10,9},{11,10},{13,12},{... | collective-permute-start | bytes 196616 | tf_op jit(solution)/shard_map/ppermute | solution.py:22
  23.7 8.7 %collective-permute-start.5 = (f32[2,2,1,4096]{3,2,1,0:T(1,128)S(1)}, f32[2,2,1,4096]{3,2,1,0:T(1,128)S(1)}, u32[]{:S(2)}, u32[]{:S(2)}) collective-permute-start(f32[2,2,1,4096]{3,2,1,0:T(1,128)S(1)} %get-tuple-element.45), channel_id=1, source_target_pairs={{0,1},{1,2},{2,3},{4,5},{5,6},{6,7},{8,9},{9,10},{10,11},{12,13},{... | collective-permute-start | bytes 196616 | tf_op jit(solution)/shard_map/ppermute | solution.py:21
  31.1 8.2 %collective-permute-start.7 = (f32[1,8,4096]{2,1,0:T(8,128)S(1)}, f32[1,8,4096]{2,1,0:T(8,128)S(1)}, u32[]{:S(2)}, u32[]{:S(2)}) collective-permute-start(f32[1,8,4096]{2,1,0:T(8,128)S(1)} %get-tuple-element.37), channel_id=1, source_target_pairs={{4,0},{8,4},{12,8},{16,12},{20,16},{24,20},{28,24},{5,1},{9,5},{13... | collective-permute-start | bytes 393224 | tf_op jit(solution)/shard_map/ppermute | solution.py:30
  40.2 10.3 %collective-permute-start.8 = (f32[2,2,1,4096]{3,2,1,0:T(1,128)S(1)}, f32[2,2,1,4096]{3,2,1,0:T(1,128)S(1)}, u32[]{:S(2)}, u32[]{:S(2)}) collective-permute-start(f32[2,2,1,4096]{3,2,1,0:T(1,128)S(1)} %get-tuple-element.32), channel_id=1, source_target_pairs={{1,0},{2,1},{3,2},{5,4},{6,5},{7,6},{9,8},{10,9},{11,10},{13,12},{... | collective-permute-start | bytes 196616 | tf_op jit(solution)/shard_map/ppermute | solution.py:22
  41.5 9.0 %collective-permute-start.9 = (f32[2,2,1,4096]{3,2,1,0:T(1,128)S(1)}, f32[2,2,1,4096]{3,2,1,0:T(1,128)S(1)}, u32[]{:S(2)}, u32[]{:S(2)}) collective-permute-start(f32[2,2,1,4096]{3,2,1,0:T(1,128)S(1)} %get-tuple-element.33), channel_id=1, source_target_pairs={{0,1},{1,2},{2,3},{4,5},{5,6},{6,7},{8,9},{9,10},{10,11},{12,13},{... | collective-permute-start | bytes 196616 | tf_op jit(solution)/shard_map/ppermute | solution.py:21
  45.9 10.0 %collective-permute-start.10 = (f32[1,8,4096]{2,1,0:T(8,128)S(1)}, f32[1,8,4096]{2,1,0:T(8,128)S(1)}, u32[]{:S(2)}, u32[]{:S(2)}) collective-permute-start(f32[1,8,4096]{2,1,0:T(8,128)S(1)} %get-tuple-element.24), channel_id=1, source_target_pairs={{0,4},{4,8},{8,12},{12,16},{16,20},{20,24},{24,28},{1,5},{5,9},{9,... | collective-permute-start | bytes 393224 | tf_op jit(solution)/shard_map/ppermute | solution.py:30
  56.4 8.9 %collective-permute-start.12 = (f32[2,1,1,4096]{3,2,1,0:T(1,128)S(1)}, f32[2,1,1,4096]{3,2,1,0:T(1,128)S(1)}, u32[]{:S(2)}, u32[]{:S(2)}) collective-permute-start(f32[2,1,1,4096]{3,2,1,0:T(1,128)S(1)} %get-tuple-element.116), channel_id=1, source_target_pairs={{1,0},{2,1},{3,2},{5,4},{6,5},{7,6},{9,8},{10,9},{11,10},{13,12},{... | collective-permute-start | bytes 98312 | tf_op jit(solution)/shard_map/ppermute | solution.py:22
  68.9 8.2 %collective-permute-start.15 = (f32[1,8,4096]{2,1,0:T(8,128)S(1)}, f32[1,8,4096]{2,1,0:T(8,128)S(1)}, u32[]{:S(2)}, u32[]{:S(2)}) collective-permute-start(f32[1,8,4096]{2,1,0:T(8,128)S(1)} %get-tuple-element.3), channel_id=1, source_target_pairs={{4,0},{8,4},{12,8},{16,12},{20,16},{24,20},{28,24},{5,1},{9,5},{13... | collective-permute-start | bytes 393224 | tf_op jit(solution)/shard_map/ppermute | solution.py:30
  77.6 10.4 %collective-permute-start.16 = (f32[2,1,1,4096]{3,2,1,0:T(1,128)S(1)}, f32[2,1,1,4096]{3,2,1,0:T(1,128)S(1)}, u32[]{:S(2)}, u32[]{:S(2)}) collective-permute-start(f32[2,1,1,4096]{3,2,1,0:T(1,128)S(1)} %get-tuple-element.108), channel_id=1, source_target_pairs={{1,0},{2,1},{3,2},{5,4},{6,5},{7,6},{9,8},{10,9},{11,10},{13,12},{... | collective-permute-start | bytes 98312 | tf_op jit(solution)/shard_map/ppermute | solution.py:22
  78.9 9.1 %collective-permute-start.17 = (f32[2,1,1,4096]{3,2,1,0:T(1,128)S(1)}, f32[2,1,1,4096]{3,2,1,0:T(1,128)S(1)}, u32[]{:S(2)}, u32[]{:S(2)}) collective-permute-start(f32[2,1,1,4096]{3,2,1,0:T(1,128)S(1)} %get-tuple-element.109), channel_id=1, source_target_pairs={{0,1},{1,2},{2,3},{4,5},{5,6},{6,7},{8,9},{9,10},{10,11},{12,13},{... | collective-permute-start | bytes 98312 | tf_op jit(solution)/shard_map/ppermute | solution.py:21
  82.0 8.4 %collective-permute-start.18 = (f32[1,8,4096]{2,1,0:T(8,128)S(1)}, f32[1,8,4096]{2,1,0:T(8,128)S(1)}, u32[]{:S(2)}, u32[]{:S(2)}) collective-permute-start(f32[1,8,4096]{2,1,0:T(8,128)S(1)} %get-tuple-element.102), channel_id=1, source_target_pairs={{0,4},{4,8},{8,12},{12,16},{16,20},{20,24},{24,28},{1,5},{5,9},{9,... | collective-permute-start | bytes 393224 | tf_op jit(solution)/shard_map/ppermute | solution.py:30
  94.6 8.3 %collective-permute-start.20 = (f32[2,1,8,4096]{3,2,1,0:T(8,128)S(1)}, f32[2,1,8,4096]{3,2,1,0:T(8,128)S(1)}, u32[]{:S(2)}, u32[]{:S(2)}) collective-permute-start(f32[2,1,8,4096]{3,2,1,0:T(8,128)S(1)} %maximum_subtract_fusion.4), channel_id=1, source_target_pairs={{0,4},{4,0},{8,12},{12,8},{16,20},{20,16},{24,28},{28,24},{1,5},{5... | collective-permute-start | bytes 786440 | tf_op jit(solution)/shard_map/ppermute | solution.py:36
  103.3 9.8 %collective-permute-start.21 = (f32[2,1,1,4096]{3,2,1,0:T(1,128)S(1)}, f32[2,1,1,4096]{3,2,1,0:T(1,128)S(1)}, u32[]{:S(2)}, u32[]{:S(2)}) collective-permute-start(f32[2,1,1,4096]{3,2,1,0:T(1,128)S(1)} %get-tuple-element.98), channel_id=1, source_target_pairs={{1,0},{2,1},{3,2},{5,4},{6,5},{7,6},{9,8},{10,9},{11,10},{13,12},{... | collective-permute-start | bytes 98312 | tf_op jit(solution)/shard_map/ppermute | solution.py:22
  104.6 8.5 %collective-permute-start.22 = (f32[2,1,1,4096]{3,2,1,0:T(1,128)S(1)}, f32[2,1,1,4096]{3,2,1,0:T(1,128)S(1)}, u32[]{:S(2)}, u32[]{:S(2)}) collective-permute-start(f32[2,1,1,4096]{3,2,1,0:T(1,128)S(1)} %get-tuple-element.99), channel_id=1, source_target_pairs={{0,1},{1,2},{2,3},{4,5},{5,6},{6,7},{8,9},{9,10},{10,11},{12,13},{... | collective-permute-start | bytes 98312 | tf_op jit(solution)/shard_map/ppermute | solution.py:21
  119.8 9.2 %collective-permute-start.25 = (f32[2,1,1,4096]{3,2,1,0:T(1,128)S(1)}, f32[2,1,1,4096]{3,2,1,0:T(1,128)S(1)}, u32[]{:S(2)}, u32[]{:S(2)}) collective-permute-start(f32[2,1,1,4096]{3,2,1,0:T(1,128)S(1)} %get-tuple-element.90), channel_id=1, source_target_pairs={{1,0},{2,1},{3,2},{5,4},{6,5},{7,6},{9,8},{10,9},{11,10},{13,12},{... | collective-permute-start | bytes 98312 | tf_op jit(solution)/shard_map/ppermute | solution.py:22
  143.4 9.3 %collective-permute-start.30 = (f32[2,1,1,4096]{3,2,1,0:T(1,128)S(1)}, f32[2,1,1,4096]{3,2,1,0:T(1,128)S(1)}, u32[]{:S(2)}, u32[]{:S(2)}) collective-permute-start(f32[2,1,1,4096]{3,2,1,0:T(1,128)S(1)} %get-tuple-element.80), channel_id=1, source_target_pairs={{1,0},{2,1},{3,2},{5,4},{6,5},{7,6},{9,8},{10,9},{11,10},{13,12},{... | collective-permute-start | bytes 98312 | tf_op jit(solution)/shard_map/ppermute | solution.py:22
  144.7 8.0 %collective-permute-start.31 = (f32[2,1,1,4096]{3,2,1,0:T(1,128)S(1)}, f32[2,1,1,4096]{3,2,1,0:T(1,128)S(1)}, u32[]{:S(2)}, u32[]{:S(2)}) collective-permute-start(f32[2,1,1,4096]{3,2,1,0:T(1,128)S(1)} %get-tuple-element.81), channel_id=1, source_target_pairs={{0,1},{1,2},{2,3},{4,5},{5,6},{6,7},{8,9},{9,10},{10,11},{12,13},{... | collective-permute-start | bytes 98312 | tf_op jit(solution)/shard_map/ppermute | solution.py:21
  151.4 10.9 %collective-permute-start.33 = (f32[1,8,4096]{2,1,0:T(8,128)S(1)}, f32[1,8,4096]{2,1,0:T(8,128)S(1)}, u32[]{:S(2)}, u32[]{:S(2)}) collective-permute-start(f32[1,8,4096]{2,1,0:T(8,128)S(1)} %bitcast.253), channel_id=1, source_target_pairs={{16,0},{20,4},{24,8},{28,12},{17,1},{21,5},{25,9},{29,13},{18,2},{... | collective-permute-start | bytes 393224 | tf_op jit(solution)/shard_map/ppermute | solution.py:30
  168.7 10.6 %collective-permute-start.37 = (f32[1,8,4096]{2,1,0:T(8,128)S(1)}, f32[1,8,4096]{2,1,0:T(8,128)S(1)}, u32[]{:S(2)}, u32[]{:S(2)}) collective-permute-start(f32[1,8,4096]{2,1,0:T(8,128)S(1)} %get-tuple-element.67), channel_id=1, source_target_pairs={{16,0},{20,4},{24,8},{28,12},{17,1},{21,5},{25,9},{29,13},{18,2},{... | collective-permute-start | bytes 393224 | tf_op jit(solution)/shard_map/ppermute | solution.py:30
  179.3 11.8 %collective-permute-start.38 = (f32[2,1,8,4096]{3,2,1,0:T(8,128)S(1)}, f32[2,1,8,4096]{3,2,1,0:T(8,128)S(1)}, u32[]{:S(2)}, u32[]{:S(2)}) collective-permute-start(f32[2,1,8,4096]{3,2,1,0:T(8,128)S(1)} %maximum_subtract_fusion.8), channel_id=1, source_target_pairs={{0,16},{4,20},{8,24},{12,28},{16,0},{20,4},{24,8},{28,12},{1,17},{... | collective-permute-start | bytes 786440 | tf_op jit(solution)/shard_map/ppermute | solution.py:36
  (20 other events, 145.1 us)
where the time goes:
time: 200 us; the launch traced here: 198 us
  starting transfers between devices  94.6 us (47%)
  waiting for transfers between devices  88.9 us (44%)
  local copies, waits for them, and re-layouts  6.7 us (3%)
  other arithmetic  6.11 us (3%)
    ppermute x18, waiting for transfers between devices, from_behind(): return lax.ppermute(array, axis, pairs)  64.3 us
    ppermute x18, starting transfers between devices, from_behind(): return lax.ppermute(array, axis, pairs)  47 us
    ppermute x10, starting transfers between devices, extended_2(): before = lax.ppermute(last, axis, up)  30.5 us
    ppermute x3, waiting for transfers between devices, swapped(): return lax.ppermute(value, axis, pairs)  23.8 us
    ppermute x10, starting transfers between devices, extended_2(): after = lax.ppermute(first, axis, down)  12.9 us
    ppermute x3, starting transfers between devices, swapped(): return lax.ppermute(value, axis, pairs)  4.15 us
  transfers between devices with their start and end apart: 41, of which 22 were waited for; matrix products, arithmetic and copies ran while one was open for 2% of the time, Pallas kernels for 0%

commit v1 on v0

v1 whole, which is shorter than its diff:
```python
import numpy as np

import jax
import jax.numpy as jnp
from jax import lax
from jax.sharding import PartitionSpec as P

NY = 64

KAPPA_BASE = 0.25
COUPLING_BASE = 0.5
DAMPING = 0.6


def level_terms(level):
    diffusion = KAPPA_BASE * 2.0**level
    coupling = COUPLING_BASE * 2.0**level
    centre = 1.0 + 6.0 * diffusion
    determinant = centre * centre + coupling * coupling
    along = DAMPING * centre / determinant
    across = DAMPING * coupling / determinant
    return diffusion, coupling, centre, along, across


def coarse_polynomials(total_steps):
    levels = total_steps.bit_length()
    powers = 2 * levels + 1
    unit = np.eye(4 * total_steps).reshape(-1, 2, 2, total_steps)
    fields = np.zeros((4 * total_steps, 2, total_steps, powers))
    source = np.zeros_like(fields)
    fields[..., 0] = unit[:, 0]
    source[..., 0] = unit[:, 1]

    def image(values, diffusion, coupling, centre):
        out = centre * values
        out[..., 1:] -= diffusion * values[..., :-1]
        out[:, 0, 1:] -= values[:, 0, :-1]
        out[:, 1, :-1] -= values[:, 1, 1:]
        out[:, 0] += coupling * values[:, 1]
        out[:, 1] -= coupling * values[:, 0]
        return out

    for level in range(levels):
        diffusion, coupling, centre, along, across = level_terms(level)
        for _ in range(2):
            defect = source - image(fields, diffusion, coupling, centre)
            state, adjoint = defect[:, 0], defect[:, 1]
            fields = fields + np.stack([along * state - across * adjoint, across * state + along * adjoint], 1)
        if level < levels - 1:
            defect = source - image(fields, diffusion, coupling, centre)
            source = defect[:, :, 0::2] + defect[:, :, 1::2]
            fields = np.zeros_like(source)
    return fields[:, :, 0].reshape(2, 2, total_steps, 2, powers)


def plane_neighbours(values):
    length = values.shape[-1]
    columns = jnp.arange(length, dtype=jnp.int32) % NY
    single = jnp.zeros(values.shape[:-1] + (1,), jnp.float32)
    row = jnp.zeros(values.shape[:-1] + (NY,), jnp.float32)
    left = jnp.where(columns != 0, jnp.concatenate([single, values[..., :-1]], -1), 0.0)
    right = jnp.where(columns != NY - 1, jnp.concatenate([values[..., 1:], single], -1), 0.0)
    upper = jnp.concatenate([row, values[..., :-NY]], -1)
    lower = jnp.concatenate([values[..., NY:], row], -1)
    return left + right + upper + lower


def whole_neighbours(values):
    zero = jnp.zeros(values.shape[:-2] + (1, values.shape[-1]), jnp.float32)
    above = jnp.concatenate([zero, values[..., :-1, :]], -2)
    below = jnp.concatenate([values[..., 1:, :], zero], -2)
    return above + below + plane_neighbours(values)


def inner_neighbours(values):
    return values[..., :-2, :] + values[..., 2:, :] + plane_neighbours(values[..., 1:-1, :])


def shifted(value, axis, by):
    size = lax.axis_size(axis)
    return lax.ppermute(value, axis, [(i, i + by) for i in range(size) if 0 <= i + by < size])


def coarse_part(iterate, forcing):
    steps = iterate.shape[1]
    depth, cells = iterate.shape[2:]
    ranks, slabs = lax.axis_size("tm"), lax.axis_size("space")
    table = coarse_polynomials(steps * ranks)
    powers = table.shape[-1]
    table = table.reshape(2, 2, ranks, steps, 2, powers).transpose(2, 5, 4, 0, 1, 3).astype(np.float32)
    weights = jnp.asarray(table)[lax.axis_index("tm")]
    both = jnp.stack([iterate, forcing])
    offset = lax.axis_index("space") * depth
    total = jnp.zeros((2, depth * slabs, cells), jnp.float32)
    for power in reversed(range(powers)):
        share = jnp.sum(weights[power][..., None, None] * both[None], axis=(1, 2, 3))
        blank = jnp.zeros((2, depth * slabs, cells), jnp.float32)
        placed = lax.dynamic_update_slice(blank, share, (0, offset, 0))
        total = placed if power == powers - 1 else placed + whole_neighbours(total)
    return total


def smooth(iterate, forcing):
    depth = iterate.shape[2]
    rank, ranks = lax.axis_index("tm"), lax.axis_size("tm")
    slab, slabs = lax.axis_index("space"), lax.axis_size("space")
    diffusion, coupling, centre, along, across = level_terms(0)
    send_up = jnp.concatenate([iterate[:, :, -2:], forcing[:, :, -1:]], 2)
    send_down = jnp.concatenate([forcing[:, :, :1], iterate[:, :, :2]], 2)
    from_above = shifted(send_up, "space", 1)
    from_below = shifted(send_down, "space", -1)
    wide = jnp.concatenate([from_above[:, :, :2], iterate, from_below[:, :, 1:]], 2)
    source = jnp.concatenate([from_above[:, :, 2:], forcing, from_below[:, :, :1]], 2)

    def relaxed(fields, image_state, image_adjoint, source):
        defect_state = source[0] - image_state
        defect_adjoint = source[1] - image_adjoint
        return jnp.stack([
            fields[0] + along * defect_state - across * defect_adjoint,
            fields[1] + across * defect_state + along * defect_adjoint,
        ])

    def images(fields, around, before, after):
        state, adjoint = fields
        return (
            centre * state - diffusion * around[0] - before + coupling * adjoint,
            centre * adjoint - diffusion * around[1] - after - coupling * state,
        )

    middle = wide[:, :, 1:-1]
    none = jnp.zeros_like(middle[0, :1])
    before = jnp.concatenate([none, middle[0, :-1]], 0)
    after = jnp.concatenate([middle[1, 1:], none], 0)
    first = relaxed(middle, *images(middle, inner_neighbours(wide), before, after), source)
    plane = jnp.arange(depth + 2)
    inside = ((plane > 0) | (slab > 0)) & ((plane < depth + 1) | (slab < slabs - 1))
    first = jnp.where(inside[:, None], first, 0.0)
    forth = jnp.concatenate([middle[0, -1], first[0, -1, 1:-1]], 0)
    back = jnp.concatenate([middle[1, 0], first[1, 0, 1:-1]], 0)
    forth = shifted(forth, "tm", 1)
    back = shifted(back, "tm", -1)
    state_before, adjoint_after = forth[: depth + 2], back[: depth + 2]
    start = first[:, :1] + jnp.stack([along * state_before, across * state_before])[:, None]
    first = jnp.concatenate([start, first[:, 1:]], 1)
    end = first[:, -1:] + jnp.stack([-across * adjoint_after, along * adjoint_after])[:, None]
    first = jnp.concatenate([first[:, :-1], end], 1)
    before = jnp.where(rank > 0, forth[depth + 2 :] - across * iterate[1, 0], 0.0)
    after = jnp.where(rank < ranks - 1, back[depth + 2 :] + across * iterate[0, -1], 0.0)
    middle = first[:, :, 1:-1]
    before = jnp.concatenate([before[None], middle[0, :-1]], 0)
    after = jnp.concatenate([middle[1, 1:], after[None]], 0)
    return relaxed(middle, *images(middle, inner_neighbours(first), before, after), forcing)


def local(iterate, forcing):
    share = coarse_part(iterate, forcing)
    slab = lax.psum_scatter(share, "space", scatter_dimension=1, tiled=True)
    coarse = lax.psum(slab, "tm")
    smoothed = smooth(iterate, forcing)
    return smoothed, jnp.broadcast_to(coarse[:, None], iterate.shape)


def solution(mesh):
    specs = P(None, "tm", "space", None)
    return jax.shard_map(local, mesh=mesh, in_specs=(specs, specs), out_specs=(specs, specs), check_vma=False)
```

time: 200 us -> 217 us (1.085)
  starting transfers between devices: 94.6 us -> 9.31 us
  local copies, waits for them, and re-layouts: 6.7 us -> 58.3 us
  other arithmetic: 6.11 us -> 40.6 us
  between operations: 1.6 us -> 14.5 us
  waiting for transfers between devices: 88.9 us -> 92.7 us
    ppermute x41 -> x4, starting transfers between devices: 94.6 us -> 9.23 us  [shifted(): lax.ppermute(value, axis, [(i, i + by) for i in range(size) if 0 <= i + b...]
    ppermute x41 -> x4, waiting for transfers between devices: 88.9 us -> 15 us  [shifted(): lax.ppermute(value, axis, [(i, i + by) for i in range(size) if 0 <= i + b...]
    psum x0 -> x1, waiting for transfers between devices: none -> 73.4 us  [local(): coarse = lax.psum(slab, 'tm')]
    slice x18 -> x40, local copies, waits for them, and re-layouts: 3.66 us -> 55.4 us  [the longest x11 18.2 us: plane_neighbours(): upper = jnp.concatenate([row, values[..., :-NY]], -1)]
    add x26 -> x24, other arithmetic: 3.82 us -> 34.7 us  [the longest x10 16.9 us: coarse_part(): total = placed if power == powers - 1 else placed + whole_neighbours(total)]
    reduce_scatter x0 -> x1, waiting for transfers between devices: none -> 4.21 us  [local(): slab = lax.psum_scatter(share, 'space', scatter_dimension=1, tiled=True)]
    reduce_sum x0 -> x1, other arithmetic: none -> 2.76 us  [coarse_part(): jnp.sum(weights[power][..., None, None] * both[None], axis=(1, 2, 3))]
  transfers between devices with their start and end apart: 41 -> 6, of which waited for: 22 -> 3; matrix products, arithmetic and copies ran while one was open for 2% -> 44% of each run, Pallas kernels for 0% -> 0%
where the time goes in v1:
time: 217 us; the launch traced here: 215 us
  waiting for transfers between devices  92.7 us (43%)
  local copies, waits for them, and re-layouts  58.3 us (27%)
  other arithmetic  40.6 us (19%)
  between operations  14.5 us (7%)
  starting transfers between devices  9.31 us (4%)
    psum x1, waiting for transfers between devices, local(): coarse = lax.psum(slab, 'tm')  73.4 us
    slice x11, local copies, waits for them, and re-layouts, plane_neighbours(): upper = jnp.concatenate([row, values[..., :-NY]], -1)  18.2 us
    slice x11, local copies, waits for them, and re-layouts, plane_neighbours(): values[..., :-1]  18 us
    add x10, other arithmetic, coarse_part(): total = placed if power == powers - 1 else placed + whole_neighbours(total)  16.9 us
    slice x10, local copies, waits for them, and re-layouts, whole_neighbours(): above = jnp.concatenate([zero, values[..., :-1, :]], -2)  16.3 us
    add x10, other arithmetic, whole_neighbours(): return above + below + plane_neighbours(values)  16.3 us
    ppermute x4, waiting for transfers between devices, shifted(): lax.ppermute(value, axis, [(i, i + by) for i in range(size) if 0 <= i + b...  15 us
    ppermute x4, starting transfers between devices, shifted(): lax.ppermute(value, axis, [(i, i + by) for i in range(size) if 0 <= i + b...  9.23 us
  transfers between devices with their start and end apart: 6, of which 3 were waited for; matrix products, arithmetic and copies ran while one was open for 44% of the time, Pallas kernels for 0%

profile of v1, /device:TPU:0, one launch (start us, length us, event | category | flops | bytes accessed | tf_op | source)
XLA Modules:
  0.0 215.5 jit_solution(12632526643983187813)
XLA Ops:
  10.1 2.4 %collective-permute-start = (f32[2,2,3,4096]{3,2,1,0:T(4,128)S(1)}, f32[2,2,3,4096]{3,2,1,0:T(4,128)S(1)}, u32[]{:S(2)}, u32[]{:S(2)}) collective-permute-start(f32[2,2,3,4096]{3,2,1,0:T(4,128)S(1)} %pad_maximum_fusion.7), channel_id=1, source_target_pairs={{0,1},{1,2},{2,3},{4,5},{5,6},{6,7},{8,9},{9,10},{10,11},{12,13},{... | collective-permute-start | bytes 589832 | tf_op jit(solution)/shard_map/ppermute | solution.py:81
  14.8 2.8 %multiply_reduce_fusion = (f32[2,8,4096]{2,1,0:T(8,128)S(1)}, f32[2,8,4096]{2,1,0:T(8,128)S(1)}, f32[2,8,4096]{2,1,0:T(8,128)S(1)}, f32[2,8,4096]{2,1,0:T(8,128)...) fusion(f32[2,2,2,2]{3,2,1,0:T(2,128)S(1)} %get-tuple-element.11, ...), kind=kLoop, calls=%fused_computation.14 | loop fusion | flops 10813440 | bytes 3932864 | tf_op jit(solution)/shard_map/reduce_sum | solution.py:96
  23.8 1.9 fusion.75
  25.7 1.9 fusion.76
  32.7 1.9 fusion.72
  34.6 1.9 fusion.73
  41.7 1.9 fusion.69
  43.6 1.9 fusion.70
  50.7 1.9 fusion.66
  52.6 1.9 fusion.67
  59.6 1.9 fusion.63
  61.6 1.9 fusion.64
  68.6 1.9 fusion.60
  70.5 1.9 fusion.61
  77.6 1.9 fusion.57
  79.5 1.9 fusion.58
  86.5 1.9 fusion.54
  88.5 2.1 fusion.55
  95.7 1.9 fusion.51
  97.7 1.9 fusion.52
  106.0 4.3 %collective-permute-start.2 = (f32[18,4096]{1,0:T(8,128)S(1)}, f32[18,4096]{1,0:T(8,128)S(1)}, u32[]{:S(2)}, u32[]{:S(2)}) collective-permute-start(f32[18,4096]{1,0:T(8,128)S(1)} %pad_maximum_fusion.4), channel_id=1, source_target_pairs={{0,4},{4,8},{8,12},{12,16},{16,20},{20,24},{24,28},{1,5},{5,9},{9,... | collective-permute-start | bytes 884744 | tf_op jit(solution)/shard_map/ppermute | solution.py:81
  111.7 15.0 %collective-permute-done.2 = f32[18,4096]{1,0:T(8,128)S(1)} collective-permute-done((f32[18,4096]{1,0:T(8,128)S(1)}, f32[18,4096]{1,0:T(8,128)S(1)}, u32[]{:S(2)}, u32[]{:S(2)}) %collective-permute-start.2) | collective-permute-done | bytes 294944 | tf_op jit(solution)/shard_map/ppermute | solution.py:81
  128.4 4.2 %reduce-scatter.2.cloned.1.call-done = f32[2,8,4096]{2,1,0:T(8,128)} async-done(((f32[2,32,4096]{2,1,0:T(8,128)}), f32[2,8,4096]{2,1,0:T(8,128)}) %reduce-scatter.2.cloned.1.call-update) | async-done | bytes 262160 | tf_op jit(solution)/shard_map/reduce_scatter | solution.py:157
  133.4 73.4 %all-reduce.72.cloned.1.call-done = f32[2,8,4096]{2,1,0:T(8,128)} async-done(((f32[2,8,4096]{2,1,0:T(8,128)}), f32[2,8,4096]{2,1,0:T(8,128)}) %all-reduce.72.cloned.1.call-update) | async-done | bytes 262160 | tf_op jit(solution)/shard_map/psum | solution.py:158
  (84 shorter events, 64.2 us)
Async XLA Ops:
  7.2 6.7 %copy-start.1 = (f32[2,2,8,4096]{3,2,1,0:T(8,128)S(1)}, f32[2,2,8,4096]{3,2,1,0:T(8,128)}, u32[]{:S(2)}) copy-start(f32[2,2,8,4096]{3,2,1,0:T(8,128)} %param.3) | copy-start | bytes 1572868
  7.2 6.7 %copy-start = (f32[2,2,8,4096]{3,2,1,0:T(8,128)S(1)}, f32[2,2,8,4096]{3,2,1,0:T(8,128)}, u32[]{:S(2)}) copy-start(f32[2,2,8,4096]{3,2,1,0:T(8,128)} %param.4) | copy-start | bytes 1572868
  7.2 125.4 %reduce-scatter.2.cloned.1.call-start = ((), (), s32[]{:S(2)}) async-start(), calls=%async_computation.1 | async-start | bytes 1310720 | tf_op jit(solution)/shard_map/reduce_scatter | solution.py:157
  10.1 92.9 %collective-permute-start = (f32[2,2,3,4096]{3,2,1,0:T(4,128)S(1)}, f32[2,2,3,4096]{3,2,1,0:T(4,128)S(1)}, u32[]{:S(2)}, u32[]{:S(2)}) collective-permute-start(f32[2,2,3,4096]{3,2,1,0:T(4,128)S(1)} %pad_maximum_fusion.7), channel_id=1, source_target_pairs={{0,1},{1,2},{2,3},{4,5},{5,6},{6,7},{8,9},{9,10},{10,11},{12,13},{... | collective-permute-start | bytes 589832 | tf_op jit(solution)/shard_map/ppermute | solution.py:81
  12.6 90.5 %collective-permute-start.1 = (f32[2,2,3,4096]{3,2,1,0:T(4,128)S(1)}, f32[2,2,3,4096]{3,2,1,0:T(4,128)S(1)}, u32[]{:S(2)}, u32[]{:S(2)}) collective-permute-start(f32[2,2,3,4096]{3,2,1,0:T(4,128)S(1)} %pad_maximum_fusion.8), channel_id=1, source_target_pairs={{1,0},{2,1},{3,2},{5,4},{6,5},{7,6},{9,8},{10,9},{11,10},{13,12},{... | collective-permute-start | bytes 589832 | tf_op jit(solution)/shard_map/ppermute | solution.py:81
  102.9 103.9 %all-reduce.72.cloned.1.call-start = ((), (), s32[]{:S(2)}) async-start(), calls=%async_computation.2 | async-start | bytes 524288 | tf_op jit(solution)/shard_map/psum | solution.py:158
  106.0 20.6 %collective-permute-start.2 = (f32[18,4096]{1,0:T(8,128)S(1)}, f32[18,4096]{1,0:T(8,128)S(1)}, u32[]{:S(2)}, u32[]{:S(2)}) collective-permute-start(f32[18,4096]{1,0:T(8,128)S(1)} %pad_maximum_fusion.4), channel_id=1, source_target_pairs={{0,4},{4,8},{8,12},{12,16},{16,20},{20,24},{24,28},{1,5},{5,9},{9,... | collective-permute-start | bytes 884744 | tf_op jit(solution)/shard_map/ppermute | solution.py:81
  110.4 16.4 %collective-permute-start.3 = (f32[18,4096]{1,0:T(8,128)S(1)}, f32[18,4096]{1,0:T(8,128)S(1)}, u32[]{:S(2)}, u32[]{:S(2)}) collective-permute-start(f32[18,4096]{1,0:T(8,128)S(1)} %pad_maximum_fusion.5), channel_id=1, source_target_pairs={{4,0},{8,4},{12,8},{16,12},{20,16},{24,20},{28,24},{5,1},{9,5},{13... | collective-permute-start | bytes 884744 | tf_op jit(solution)/shard_map/ppermute | solution.py:81
Sparse Core Ops, SparseCore 0:
  103.0 29.4 reduce-scatter.1
  136.3 70.5 all-reduce.71

commit v2 on v1

--- a/solution.py
+++ b/solution.py
@@ -1,11 +1,16 @@
+import functools
+
 import numpy as np
 
 import jax
 import jax.numpy as jnp
 from jax import lax
+from jax.experimental import pallas as pl
+from jax.experimental.pallas import tpu as pltpu
 from jax.sharding import PartitionSpec as P
 
 NY = 64
+LANES = 128
 
 KAPPA_BASE = 0.25
 COUPLING_BASE = 0.5
@@ -65,20 +70,92 @@
     return left + right + upper + lower
 
 
-def whole_neighbours(values):
-    zero = jnp.zeros(values.shape[:-2] + (1, values.shape[-1]), jnp.float32)
-    above = jnp.concatenate([zero, values[..., :-1, :]], -2)
-    below = jnp.concatenate([values[..., 1:, :], zero], -2)
-    return above + below + plane_neighbours(values)
-
-
 def inner_neighbours(values):
     return values[..., :-2, :] + values[..., 2:, :] + plane_neighbours(values[..., 1:-1, :])
+
+
+def swapped(value, axis, mask):
+    return lax.ppermute(value, axis, [(i, i ^ mask) for i in range(lax.axis_size(axis))])
 
 
 def shifted(value, axis, by):
     size = lax.axis_size(axis)
     return lax.ppermute(value, axis, [(i, i + by) for i in range(size) if 0 <= i + by < size])
+
+
+def coarse_kernel(powers, inputs, rank_ref, weights_ref, iterate_ref, forcing_ref, keep_ref, send_ref, total):
+    depth, cells = iterate_ref.shape[2:]
+    slabs = total.shape[1] // depth
+    columns = cells // LANES
+    slab = rank_ref[1]
+    base = rank_ref[0] * (powers * 2 * inputs)
+    lane = lax.broadcasted_iota(jnp.int32, (depth, LANES), 1)
+    sublane = lax.broadcasted_iota(jnp.int32, (depth, LANES), 0)
+    low = lane < NY
+    not_last = (lane % NY) != NY - 1
+    not_first = (lane % NY) != 0
+    top, bottom = sublane == 0, sublane == depth - 1
+    zero = jnp.zeros((depth, LANES), jnp.float32)
+    here = pl.ds(pl.multiple_of(slab * depth, depth), depth)
+
+    def column(j):
+        return pl.ds(j * LANES, LANES)
+
+    def injected(power, out, values):
+        first = base + (power * 2 + out) * inputs
+        part = weights_ref[first] * values[0]
+        for k in range(1, inputs):
+            part = part + weights_ref[first + k] * values[k]
+        return part
+
+    def own(j):
+        refs = (iterate_ref, forcing_ref)
+        return [ref[f, n, :, column(j)] for ref in refs for f in range(2) for n in range(ref.shape[1])]
+
+    def loaded(f, j):
+        if j >= columns:
+            return [zero] * slabs
+        return [total[f, z * depth : (z + 1) * depth, column(j)] for z in range(slabs)]
+
+    total[...] = jnp.zeros_like(total)
+    for j in range(columns):
+        values = own(j)
+        for f in range(2):
+            total[f, here, column(j)] = injected(powers - 1, f, values)
+
+    def step(index, _):
+        power = powers - 2 - index
+        pairs = [[zero] * slabs for _ in range(2)]
+        now = [loaded(f, 0) for f in range(2)]
+        pairs = [now[f] for f in range(2)]
+        for j in range(columns):
+            values = own(j)
+            for f in range(2):
+                later = loaded(f, j + 1)
+                current = now[f]
+                pair = [a + b for a, b in zip(current, later)]
+                forth = [pltpu.roll(v, 1, 0) for v in current]
+                back = [pltpu.roll(v, depth - 1, 0) for v in current]
+                for z in range(slabs):
+                    rows = pltpu.roll(jnp.where(low, pair[z], pairs[f][z]), NY, 1)
+                    left = pltpu.roll(jnp.where(not_last, current[z], 0.0), 1, 1)
+                    right = pltpu.roll(jnp.where(not_first, current[z], 0.0), LANES - 1, 1)
+                    above = jnp.where(top, forth[z - 1] if z else 0.0, forth[z])
+                    below = jnp.where(bottom, back[z + 1] if z < slabs - 1 else 0.0, back[z])
+                    total[f, z * depth : (z + 1) * depth, column(j)] = (rows + (left + right)) + (above + below)
+                total[f, here, column(j)] += injected(power, f, values)
+                pairs[f] = pair
+                now[f] = later
+        return 0
+
+    lax.fori_loop(0, powers - 1, step, 0)
+    bit = lax.rem(slab, 2)
+    for half in range(slabs // 2):
+        for ref, flag in ((keep_ref, bit), (send_ref, 1 - bit)):
+            rows = pl.ds(pl.multiple_of((2 * half + flag) * depth, depth), depth)
+            for f in range(2):
+                for j in range(columns):
+                    ref[half, f, j] = total[f, rows, column(j)]
 
 
 def coarse_part(iterate, forcing):
@@ -88,16 +165,38 @@
     table = coarse_polynomials(steps * ranks)
     powers = table.shape[-1]
     table = table.reshape(2, 2, ranks, steps, 2, powers).transpose(2, 5, 4, 0, 1, 3).astype(np.float32)
-    weights = jnp.asarray(table)[lax.axis_index("tm")]
-    both = jnp.stack([iterate, forcing])
-    offset = lax.axis_index("space") * depth
-    total = jnp.zeros((2, depth * slabs, cells), jnp.float32)
-    for power in reversed(range(powers)):
-        share = jnp.sum(weights[power][..., None, None] * both[None], axis=(1, 2, 3))
-        blank = jnp.zeros((2, depth * slabs, cells), jnp.float32)
-        placed = lax.dynamic_update_slice(blank, share, (0, offset, 0))
-        total = placed if power == powers - 1 else placed + whole_neighbours(total)
-    return total
+    place = jnp.stack([lax.axis_index("tm"), lax.axis_index("space")]).astype(jnp.int32)
+    half = jax.ShapeDtypeStruct((slabs // 2, 2, cells // LANES, depth, LANES), jnp.float32)
+    smem = pl.BlockSpec(memory_space=pltpu.SMEM)
+    vmem = pl.BlockSpec(memory_space=pltpu.VMEM)
+    return pl.pallas_call(
+        functools.partial(coarse_kernel, powers, 4 * steps),
+        out_shape=(half, half),
+        in_specs=[smem, smem, vmem, vmem],
+        out_specs=(vmem, vmem),
+        scratch_shapes=[pltpu.VMEM((2, depth * slabs, cells), jnp.float32)],
+        compiler_params=pltpu.CompilerParams(vmem_limit_bytes=32 * 2**20),
+        cost_estimate=pl.CostEstimate(flops=10**8, bytes_accessed=3 * 2**20, transcendentals=0),
+    )(place, jnp.asarray(table.reshape(-1)), iterate, forcing)
+
+
+def spread_sum(keep, send):
+    slabs, ranks = lax.axis_size("space"), lax.axis_size("tm")
+    slab = lax.axis_index("space")
+    held = keep + swapped(send, "space", 1)
+    mask = 2
+    while mask < slabs:
+        bit = (slab // mask) % 2
+        held = held.reshape((-1, 2) + held.shape[1:])
+        other = lax.dynamic_index_in_dim(held, 1 - bit, 1, keepdims=False)
+        mine = lax.dynamic_index_in_dim(held, bit, 1, keepdims=False)
+        held = mine + swapped(other, "space", mask)
+        mask *= 2
+    tiles = held.reshape((ranks, -1) + held.shape[-2:])
+    parts = lax.all_to_all(tiles, "tm", 0, 0, tiled=True)
+    part = jnp.sum(parts, axis=0)
+    copies = jnp.broadcast_to(part[None], tiles.shape)
+    return lax.all_to_all(copies, "tm", 0, 0, tiled=True).reshape((2, -1) + held.shape[-2:])
 
 
 def smooth(iterate, forcing):
@@ -153,10 +252,10 @@
 
 
 def local(iterate, forcing):
-    share = coarse_part(iterate, forcing)
-    slab = lax.psum_scatter(share, "space", scatter_dimension=1, tiled=True)
-    coarse = lax.psum(slab, "tm")
+    keep, send = coarse_part(iterate, forcing)
     smoothed = smooth(iterate, forcing)
+    coarse = spread_sum(keep, send)
+    coarse = coarse.transpose(0, 2, 1, 3).reshape(iterate.shape[:1] + iterate.shape[2:])
     return smoothed, jnp.broadcast_to(coarse[:, None], iterate.shape)
 
 

time: 217 us -> 127 us (0.59)
  waiting for transfers between devices: 92.7 us -> 36.9 us
  local copies, waits for them, and re-layouts: 58.3 us -> 4.81 us
  Pallas kernels: 0 us -> 51 us
  other arithmetic: 40.6 us -> 7.02 us
  starting transfers between devices: 9.31 us -> 26 us
  between operations: 14.5 us -> 0.96 us
    psum x1 -> x0, waiting for transfers between devices: 73.4 us -> none  [local(): coarse = lax.psum(slab, 'tm')]
    pallas_call x0 -> x1, Pallas kernels: none -> 51 us  [coarse_part(): pl.pallas_call(functools.partial(coarse_kernel, powers, 4 * steps), out_s...]
    add x20 -> x2, other arithmetic: 33.3 us -> 1.83 us  [the longest x1 1.1 us: spread_sum(): held = keep + swapped(send, 'space', 1)]
    slice x11 -> x1, local copies, waits for them, and re-layouts: 18.2 us -> 0.36 us  [plane_neighbours(): upper = jnp.concatenate([row, values[..., :-NY]], -1)]
    slice x11 -> x1, local copies, waits for them, and re-layouts: 18 us -> 0.36 us  [plane_neighbours(): values[..., :-1]]
    slice x10 -> x0, local copies, waits for them, and re-layouts: 16.3 us -> none  [whole_neighbours(): above = jnp.concatenate([zero, values[..., :-1, :]], -2)]
    all_to_all x0 -> x2, waiting for transfers between devices: none -> 16.1 us  [the longest x1 8.39 us: spread_sum(): parts = lax.all_to_all(tiles, 'tm', 0, 0, tiled=True)]
    all_to_all x0 -> x2, starting transfers between devices: none -> 10.9 us  [the longest x1 7.2 us: spread_sum(): parts = lax.all_to_all(tiles, 'tm', 0, 0, tiled=True)]
  transfers between devices with their start and end apart: 6 -> 8, of which waited for: 3 -> 4; matrix products, arithmetic and copies ran while one was open for 44% -> 5% of each run, Pallas kernels for 0% -> 40%
where the time goes in v2:
time: 127 us
  Pallas kernels  51 us (40%)
  waiting for transfers between devices  36.9 us (29%)
  starting transfers between devices  26 us (20%)
  other arithmetic  7.02 us (6%)
  local copies, waits for them, and re-layouts  4.81 us (4%)
    pallas_call x1, Pallas kernels, coarse_part(): pl.pallas_call(functools.partial(coarse_kernel, powers, 4 * steps), out_s...  51 us
    ppermute x4, waiting for transfers between devices, shifted(): lax.ppermute(value, axis, [(i, i + by) for i in range(size) if 0 <= i + b...  15.7 us
    ppermute x4, starting transfers between devices, shifted(): lax.ppermute(value, axis, [(i, i + by) for i in range(size) if 0 <= i + b...  8.54 us
    all_to_all x1, waiting for transfers between devices, spread_sum(): parts = lax.all_to_all(tiles, 'tm', 0, 0, tiled=True)  8.39 us
    all_to_all x1, waiting for transfers between devices, spread_sum(): lax.all_to_all(copies, 'tm', 0, 0, tiled=True)  7.69 us
    all_to_all x1, starting transfers between devices, spread_sum(): parts = lax.all_to_all(tiles, 'tm', 0, 0, tiled=True)  7.2 us
    ppermute x2, starting transfers between devices, swapped(): lax.ppermute(value, axis, [(i, i ^ mask) for i in range(lax.axis_size(axi...  6.56 us
    ppermute x2, waiting for transfers between devices, swapped(): lax.ppermute(value, axis, [(i, i ^ mask) for i in range(lax.axis_size(axi...  5.2 us
  transfers between devices with their start and end apart: 8, of which 4 were waited for; matrix products, arithmetic and copies ran while one was open for 5% of the time, Pallas kernels for 40%

profile of v2, /device:TPU:0, one launch (start us, length us, event | category | flops | bytes accessed | tf_op | source)
XLA Modules:
  0.0 126.7 jit_solution(8577334651390437159)
XLA Ops:
  0.6 1.4 %fusion.41 = (f32[2,2,2,4096]{3,2,1,0:T(2,128)S(1)}, f32[2,2,2,4096]{3,2,1,0:T(2,128)S(1)}) fusion(f32[2,2,8,4096]{3,2,1,0:T(8,128)} %iterate_ref.1), kind=kLoop, calls=%fused_computation.97 | loop fusion | bytes 524288 | tf_op jit(solution)/shard_map/slice | solution.py:207
  2.3 2.5 %collective-permute-start = (f32[2,2,3,4096]{3,2,1,0:T(4,128)S(1)}, f32[2,2,3,4096]{3,2,1,0:T(4,128)S(1)}, u32[]{:S(2)}, u32[]{:S(2)}) collective-permute-start(f32[2,2,3,4096]{3,2,1,0:T(4,128)S(1)} %pad_maximum_fusion.6), channel_id=1, source_target_pairs={{0,1},{1,2},{2,3},{4,5},{5,6},{6,7},{8,9},{9,10},{10,11},{12,13},{... | collective-permute-start | bytes 589832 | tf_op jit(solution)/shard_map/ppermute | solution.py:83
  4.9 1.3 %collective-permute-start.1 = (f32[2,2,3,4096]{3,2,1,0:T(4,128)S(1)}, f32[2,2,3,4096]{3,2,1,0:T(4,128)S(1)}, u32[]{:S(2)}, u32[]{:S(2)}) collective-permute-start(f32[2,2,3,4096]{3,2,1,0:T(4,128)S(1)} %pad_maximum_fusion.7), channel_id=1, source_target_pairs={{1,0},{2,1},{3,2},{5,4},{6,5},{7,6},{9,8},{10,9},{11,10},{13,12},{... | collective-permute-start | bytes 589832 | tf_op jit(solution)/shard_map/ppermute | solution.py:83
  6.3 0.6 copy-done.2
  6.9 51.0 %shard_map.50 = (f32[2,2,32,8,128]{4,3,2,1,0:T(8,128)S(1)}, f32[2,2,32,8,128]{4,3,2,1,0:T(8,128)S(1)}) custom-call(s32[2]{0:T(128)S(1)} %pad_add_fusion.rank_ref, f32[1408]{0:T(1024)S(1)} %copy-done.2, f32[2,2,8,4096]{3,2,1,0:T(8,128)S(1)} %copy-done.1, f32[2,2,8,4096]{3,2,1,0:T(8,128)S(1)} %copy-done), custom_call_target="tpu_custom_call" | custom-call | flops 100000000 | bytes 3145728 | tf_op jit(solution)/shard_map/pallas_call | solution.py:172
  57.9 3.1 %collective-permute-start.4 = (f32[2,2,32,8,128]{4,3,2,1,0:T(8,128)S(1)}, f32[2,2,32,8,128]{4,3,2,1,0:T(8,128)}, u32[]{:S(2)}, u32[]{:S(2)}) collective-permute-start(f32[2,2,32,8,128]{4,3,2,1,0:T(8,128)S(1)} %get-tuple-element.5), channel_id=1, source_target_pairs={{0,1},{1,0},{2,3},{3,2},{4,5},{5,4},{6,7},{7,6},{8,9},{9,8},{10,11... | collective-permute-start | bytes 1572872 | tf_op jit(solution)/shard_map/ppermute | solution.py:78
  62.5 0.7 fusion
  63.3 0.4 subtract_bitcast_fusion
  64.1 3.4 %collective-permute-start.2 = (f32[18,4096]{1,0:T(8,128)S(1)}, f32[18,4096]{1,0:T(8,128)S(1)}, u32[]{:S(2)}, u32[]{:S(2)}) collective-permute-start(f32[18,4096]{1,0:T(8,128)S(1)} %pad_maximum_fusion.3), channel_id=1, source_target_pairs={{0,4},{4,8},{8,12},{12,16},{16,20},{20,24},{24,28},{1,5},{5,9},{9,... | collective-permute-start | bytes 884744 | tf_op jit(solution)/shard_map/ppermute | solution.py:83
  67.6 1.3 %collective-permute-start.3 = (f32[18,4096]{1,0:T(8,128)S(1)}, f32[18,4096]{1,0:T(8,128)S(1)}, u32[]{:S(2)}, u32[]{:S(2)}) collective-permute-start(f32[18,4096]{1,0:T(8,128)S(1)} %pad_maximum_fusion.4), channel_id=1, source_target_pairs={{4,0},{8,4},{12,8},{16,12},{20,16},{24,20},{28,24},{5,1},{9,5},{13... | collective-permute-start | bytes 884744 | tf_op jit(solution)/shard_map/ppermute | solution.py:83
  68.9 15.7 %collective-permute-done.2 = f32[18,4096]{1,0:T(8,128)S(1)} collective-permute-done((f32[18,4096]{1,0:T(8,128)S(1)}, f32[18,4096]{1,0:T(8,128)S(1)}, u32[]{:S(2)}, u32[]{:S(2)}) %collective-permute-start.2) | collective-permute-done | bytes 294944 | tf_op jit(solution)/shard_map/ppermute | solution.py:83
  85.3 0.4 fusion.4
  85.7 1.1 add.143
  86.8 3.4 %collective-permute-start.5 = (f32[1,2,32,8,128]{4,3,2,1,0:T(8,128)S(1)}, f32[1,2,32,8,128]{4,3,2,1,0:T(8,128)S(1)}, u32[]{:S(2)}, u32[]{:S(2)}) collective-permute-start(f32[1,2,32,8,128]{4,3,2,1,0:T(8,128)S(1)} %constant_dynamic-slice_fusion), channel_id=1, source_target_pairs={{0,2},{1,3},{2,0},{3,1},{4,6},{5,7},{6,4},{7,5},{8,10},{9,11},{10,... | collective-permute-start | bytes 786440 | tf_op jit(solution)/shard_map/ppermute | solution.py:78
  90.2 0.9 multiply_subtract_fusion
  91.2 5.2 %collective-permute-done.5 = f32[1,2,32,8,128]{4,3,2,1,0:T(8,128)S(1)} collective-permute-done((f32[1,2,32,8,128]{4,3,2,1,0:T(8,128)S(1)}, f32[1,2,32,8,128]{4,3,2,1,0:T(8,128)S(1)}, u32[]{:S(2)}, u32[]{:S(2)}) %collective-permute-start.5) | collective-permute-done | bytes 262176 | tf_op jit(solution)/shard_map/ppermute | solution.py:78
  96.4 0.7 dynamic-slice_add_fusion
  97.1 7.2 %all-to-all-start = ((f32[8,8,8,128]{3,2,1,0:T(8,128)}), f32[8,8,8,128]{3,2,1,0:T(8,128)S(1)}, u32[]{:S(2)}, u32[]{:S(2)}) async-start(f32[8,8,8,128]{3,2,1,0:T(8,128)} %bitcast.28), calls=%async_computation | async-start | bytes 524288 | tf_op jit(solution)/shard_map/all_to_all | solution.py:196
  104.5 8.4 %all-to-all-done = f32[8,8,8,128]{3,2,1,0:T(8,128)S(1)} async-done(((f32[8,8,8,128]{3,2,1,0:T(8,128)}), f32[8,8,8,128]{3,2,1,0:T(8,128)S(1)}, u32[]{:S(2)}, u32[]{:S(2)}) %all-to-all-start) | async-done | bytes 262176 | tf_op jit(solution)/shard_map/all_to_all | solution.py:196
  112.9 0.7 broadcast_in_dim.76
  113.6 3.7 %all-to-all-start.1 = ((f32[8,8,8,128]{3,2,1,0:T(8,128)}), f32[8,8,8,128]{3,2,1,0:T(8,128)S(1)}, u32[]{:S(2)}, u32[]{:S(2)}) async-start(f32[8,8,8,128]{3,2,1,0:T(8,128)} %broadcast_in_dim.76), calls=%async_computation.1 | async-start | bytes 524288 | tf_op jit(solution)/shard_map/all_to_all | solution.py:199
  117.4 0.8 pad_maximum_fusion.2
  118.2 7.7 %all-to-all-done.1 = f32[8,8,8,128]{3,2,1,0:T(8,128)S(1)} async-done(((f32[8,8,8,128]{3,2,1,0:T(8,128)}), f32[8,8,8,128]{3,2,1,0:T(8,128)S(1)}, u32[]{:S(2)}, u32[]{:S(2)}) %all-to-all-start.1) | async-done | bytes 262176 | tf_op jit(solution)/shard_map/all_to_all | solution.py:199
  125.9 0.8 broadcast_in_dim.78
  (46 shorter events, 3.2 us)
Async XLA Ops:
  0.6 1.4 %copy-start = (f32[2,2,8,4096]{3,2,1,0:T(8,128)S(1)}, f32[2,2,8,4096]{3,2,1,0:T(8,128)}, u32[]{:S(2)}) copy-start(f32[2,2,8,4096]{3,2,1,0:T(8,128)} %forcing_ref.1) | copy-start | bytes 1572868
  2.2 4.2 %copy-start.1 = (f32[2,2,8,4096]{3,2,1,0:T(8,128)S(1)}, f32[2,2,8,4096]{3,2,1,0:T(8,128)}, u32[]{:S(2)}) copy-start(f32[2,2,8,4096]{3,2,1,0:T(8,128)} %iterate_ref.1) | copy-start | bytes 1572868
  2.3 58.8 %collective-permute-start = (f32[2,2,3,4096]{3,2,1,0:T(4,128)S(1)}, f32[2,2,3,4096]{3,2,1,0:T(4,128)S(1)}, u32[]{:S(2)}, u32[]{:S(2)}) collective-permute-start(f32[2,2,3,4096]{3,2,1,0:T(4,128)S(1)} %pad_maximum_fusion.6), channel_id=1, source_target_pairs={{0,1},{1,2},{2,3},{4,5},{5,6},{6,7},{8,9},{9,10},{10,11},{12,13},{... | collective-permute-start | bytes 589832 | tf_op jit(solution)/shard_map/ppermute | solution.py:83
  4.9 56.2 %collective-permute-start.1 = (f32[2,2,3,4096]{3,2,1,0:T(4,128)S(1)}, f32[2,2,3,4096]{3,2,1,0:T(4,128)S(1)}, u32[]{:S(2)}, u32[]{:S(2)}) collective-permute-start(f32[2,2,3,4096]{3,2,1,0:T(4,128)S(1)} %pad_maximum_fusion.7), channel_id=1, source_target_pairs={{1,0},{2,1},{3,2},{5,4},{6,5},{7,6},{9,8},{10,9},{11,10},{13,12},{... | collective-permute-start | bytes 589832 | tf_op jit(solution)/shard_map/ppermute | solution.py:83
  6.2 0.7 copy-start.2
  57.9 27.8 %collective-permute-start.4 = (f32[2,2,32,8,128]{4,3,2,1,0:T(8,128)S(1)}, f32[2,2,32,8,128]{4,3,2,1,0:T(8,128)}, u32[]{:S(2)}, u32[]{:S(2)}) collective-permute-start(f32[2,2,32,8,128]{4,3,2,1,0:T(8,128)S(1)} %get-tuple-element.5), channel_id=1, source_target_pairs={{0,1},{1,0},{2,3},{3,2},{4,5},{5,4},{6,7},{7,6},{8,9},{9,8},{10,11... | collective-permute-start | bytes 1572872 | tf_op jit(solution)/shard_map/ppermute | solution.py:78
  64.1 20.5 %collective-permute-start.2 = (f32[18,4096]{1,0:T(8,128)S(1)}, f32[18,4096]{1,0:T(8,128)S(1)}, u32[]{:S(2)}, u32[]{:S(2)}) collective-permute-start(f32[18,4096]{1,0:T(8,128)S(1)} %pad_maximum_fusion.3), channel_id=1, source_target_pairs={{0,4},{4,8},{8,12},{12,16},{16,20},{20,24},{24,28},{1,5},{5,9},{9,... | collective-permute-start | bytes 884744 | tf_op jit(solution)/shard_map/ppermute | solution.py:83
  67.6 17.0 %collective-permute-start.3 = (f32[18,4096]{1,0:T(8,128)S(1)}, f32[18,4096]{1,0:T(8,128)S(1)}, u32[]{:S(2)}, u32[]{:S(2)}) collective-permute-start(f32[18,4096]{1,0:T(8,128)S(1)} %pad_maximum_fusion.4), channel_id=1, source_target_pairs={{4,0},{8,4},{12,8},{16,12},{20,16},{24,20},{28,24},{5,1},{9,5},{13... | collective-permute-start | bytes 884744 | tf_op jit(solution)/shard_map/ppermute | solution.py:83
  85.3 5.0 %copy-start.3 = (f32[1,1,8,4096]{3,2,1,0:T(8,128)}, f32[1,1,8,4096]{3,2,1,0:T(8,128)S(1)}, u32[]{:S(2)}) copy-start(f32[1,1,8,4096]{3,2,1,0:T(8,128)S(1)} %get-tuple-element.28) | copy-start | bytes 393220
  86.8 9.6 %collective-permute-start.5 = (f32[1,2,32,8,128]{4,3,2,1,0:T(8,128)S(1)}, f32[1,2,32,8,128]{4,3,2,1,0:T(8,128)S(1)}, u32[]{:S(2)}, u32[]{:S(2)}) collective-permute-start(f32[1,2,32,8,128]{4,3,2,1,0:T(8,128)S(1)} %constant_dynamic-slice_fusion), channel_id=1, source_target_pairs={{0,2},{1,3},{2,0},{3,1},{4,6},{5,7},{6,4},{7,5},{8,10},{9,11},{10,... | collective-permute-start | bytes 786440 | tf_op jit(solution)/shard_map/ppermute | solution.py:78
  97.1 7.2 %copy-start.4 = (f32[1,1,8,4096]{3,2,1,0:T(8,128)S(1)}, f32[1,1,8,4096]{3,2,1,0:T(8,128)}, u32[]{:S(2)}) copy-start(f32[1,1,8,4096]{3,2,1,0:T(8,128)} %copy-done.3) | copy-start | bytes 393220
  97.1 15.8 %all-to-all-start = ((f32[8,8,8,128]{3,2,1,0:T(8,128)}), f32[8,8,8,128]{3,2,1,0:T(8,128)S(1)}, u32[]{:S(2)}, u32[]{:S(2)}) async-start(f32[8,8,8,128]{3,2,1,0:T(8,128)} %bitcast.28), calls=%async_computation | async-start | bytes 524288 | tf_op jit(solution)/shard_map/all_to_all | solution.py:196
  113.6 3.7 %copy-start.5 = (f32[1,2,8,4096]{3,2,1,0:T(8,128)S(1)}, f32[1,2,8,4096]{3,2,1,0:T(8,128)}, u32[]{:S(2)}) copy-start(f32[1,2,8,4096]{3,2,1,0:T(8,128)} %get-tuple-element.6) | copy-start | bytes 786436
  113.6 12.2 %all-to-all-start.1 = ((f32[8,8,8,128]{3,2,1,0:T(8,128)}), f32[8,8,8,128]{3,2,1,0:T(8,128)S(1)}, u32[]{:S(2)}, u32[]{:S(2)}) async-start(f32[8,8,8,128]{3,2,1,0:T(8,128)} %broadcast_in_dim.76), calls=%async_computation.1 | async-start | bytes 524288 | tf_op jit(solution)/shard_map/all_to_all | solution.py:199

commit v3 on v2

--- a/solution.py
+++ b/solution.py
@@ -83,12 +83,12 @@
     return lax.ppermute(value, axis, [(i, i + by) for i in range(size) if 0 <= i + by < size])
 
 
-def coarse_kernel(powers, inputs, rank_ref, weights_ref, iterate_ref, forcing_ref, keep_ref, send_ref, total):
+def coarse_kernel(powers, inputs, slabs, place_ref, weights_ref, iterate_ref, forcing_ref, keep_ref, send_ref, even, odd):
     depth, cells = iterate_ref.shape[2:]
-    slabs = total.shape[1] // depth
     columns = cells // LANES
-    slab = rank_ref[1]
-    base = rank_ref[0] * (powers * 2 * inputs)
+    middle = slabs - 1
+    slab = place_ref[1]
+    base = place_ref[0] * (powers * 2 * inputs)
     lane = lax.broadcasted_iota(jnp.int32, (depth, LANES), 1)
     sublane = lax.broadcasted_iota(jnp.int32, (depth, LANES), 0)
     low = lane < NY
@@ -96,66 +96,86 @@
     not_first = (lane % NY) != 0
     top, bottom = sublane == 0, sublane == depth - 1
     zero = jnp.zeros((depth, LANES), jnp.float32)
-    here = pl.ds(pl.multiple_of(slab * depth, depth), depth)
-
-    def column(j):
-        return pl.ds(j * LANES, LANES)
-
-    def injected(power, out, values):
+
+    def inside(away):
+        at = slab + away
+        return jnp.where((at >= 0) & (at < slabs), 1.0, 0.0).astype(jnp.float32)
+
+    def weights(power, out):
         first = base + (power * 2 + out) * inputs
-        part = weights_ref[first] * values[0]
-        for k in range(1, inputs):
-            part = part + weights_ref[first + k] * values[k]
-        return part
-
-    def own(j):
+        return [weights_ref[first + k] for k in range(inputs)]
+
+    def injected(factors, j):
         refs = (iterate_ref, forcing_ref)
-        return [ref[f, n, :, column(j)] for ref in refs for f in range(2) for n in range(ref.shape[1])]
-
-    def loaded(f, j):
-        if j >= columns:
-            return [zero] * slabs
-        return [total[f, z * depth : (z + 1) * depth, column(j)] for z in range(slabs)]
-
-    total[...] = jnp.zeros_like(total)
-    for j in range(columns):
-        values = own(j)
+        columns = pl.ds(j * LANES, LANES)
+        values = [ref[f, n, :, columns] for ref in refs for f in range(2) for n in range(ref.shape[1])]
+        terms = [factor * value for factor, value in zip(factors, values)]
+        while len(terms) > 1:
+            terms = [sum(terms[k : k + 2]) for k in range(0, len(terms), 2)]
+        return terms[0]
+
+    def advance(source, target, power, reach):
+        aways = list(range(-reach, reach + 1))
+        masks = [inside(away) for away in aways]
         for f in range(2):
-            total[f, here, column(j)] = injected(powers - 1, f, values)
-
-    def step(index, _):
-        power = powers - 2 - index
-        pairs = [[zero] * slabs for _ in range(2)]
-        now = [loaded(f, 0) for f in range(2)]
-        pairs = [now[f] for f in range(2)]
+            factors = weights(power, f)
+
+            def loaded(j):
+                if j >= columns:
+                    return [zero for _ in aways]
+                return [source[f, middle + away, j] for away in aways]
+
+            now = loaded(0)
+            before = now
+            for j in range(columns):
+                later = loaded(j + 1)
+                pair = [a + b for a, b in zip(now, later)]
+                forth = [zero] + [pltpu.roll(v, 1, 0) for v in now]
+                back = [pltpu.roll(v, depth - 1, 0) for v in now] + [zero]
+                for k, away in enumerate(aways):
+                    rows = pltpu.roll(jnp.where(low, pair[k], before[k]), NY, 1)
+                    left = pltpu.roll(jnp.where(not_last, now[k], 0.0), 1, 1)
+                    right = pltpu.roll(jnp.where(not_first, now[k], 0.0), LANES - 1, 1)
+                    above = jnp.where(top, forth[k], forth[k + 1])
+                    below = jnp.where(bottom, back[k + 1], back[k])
+                    value = (rows + (left + right)) + (above + below)
+                    if away:
+                        value = value * masks[k]
+                    else:
+                        value = value + injected(factors, j)
+                    target[f, middle + away, j] = value
+                before, now = pair, later
+
+    even[...] = jnp.zeros_like(even)
+    odd[...] = jnp.zeros_like(odd)
+    for f in range(2):
+        factors = weights(powers - 1, f)
         for j in range(columns):
-            values = own(j)
-            for f in range(2):
-                later = loaded(f, j + 1)
-                current = now[f]
-                pair = [a + b for a, b in zip(current, later)]
-                forth = [pltpu.roll(v, 1, 0) for v in current]
-                back = [pltpu.roll(v, depth - 1, 0) for v in current]
-                for z in range(slabs):
-                    rows = pltpu.roll(jnp.where(low, pair[z], pairs[f][z]), NY, 1)
-                    left = pltpu.roll(jnp.where(not_last, current[z], 0.0), 1, 1)
-                    right = pltpu.roll(jnp.where(not_first, current[z], 0.0), LANES - 1, 1)
-                    above = jnp.where(top, forth[z - 1] if z else 0.0, forth[z])
-                    below = jnp.where(bottom, back[z + 1] if z < slabs - 1 else 0.0, back[z])
-                    total[f, z * depth : (z + 1) * depth, column(j)] = (rows + (left + right)) + (above + below)
-                total[f, here, column(j)] += injected(power, f, values)
-                pairs[f] = pair
-                now[f] = later
-        return 0
-
-    lax.fori_loop(0, powers - 1, step, 0)
+            even[f, middle, j] = injected(factors, j)
+    buffers = (even, odd)
+    done = 0
+    while done < powers - 1:
+        reach = min(done // depth + 1, middle)
+        count = powers - 1 - done if reach == middle else min(depth, powers - 1 - done)
+
+        def twice(index, _):
+            power = powers - 2 - done - 2 * index
+            advance(buffers[0], buffers[1], power, reach)
+            advance(buffers[1], buffers[0], power - 1, reach)
+            return 0
+
+        lax.fori_loop(0, count // 2, twice, 0)
+        done += count
+        if count % 2:
+            advance(buffers[0], buffers[1], powers - 1 - done, reach)
+            buffers = buffers[::-1]
+
     bit = lax.rem(slab, 2)
     for half in range(slabs // 2):
         for ref, flag in ((keep_ref, bit), (send_ref, 1 - bit)):
-            rows = pl.ds(pl.multiple_of((2 * half + flag) * depth, depth), depth)
+            away = 2 * half + flag - slab
             for f in range(2):
-                for j in range(columns):
-                    ref[half, f, j] = total[f, rows, column(j)]
+                ref[half, f] = buffers[0][f, middle + away]
 
 
 def coarse_part(iterate, forcing):
@@ -170,11 +190,11 @@
     smem = pl.BlockSpec(memory_space=pltpu.SMEM)
     vmem = pl.BlockSpec(memory_space=pltpu.VMEM)
     return pl.pallas_call(
-        functools.partial(coarse_kernel, powers, 4 * steps),
+        functools.partial(coarse_kernel, powers, 4 * steps, slabs),
         out_shape=(half, half),
         in_specs=[smem, smem, vmem, vmem],
         out_specs=(vmem, vmem),
-        scratch_shapes=[pltpu.VMEM((2, depth * slabs, cells), jnp.float32)],
+        scratch_shapes=[pltpu.VMEM((2, 2 * slabs - 1, cells // LANES, depth, LANES), jnp.float32)] * 2,
         compiler_params=pltpu.CompilerParams(vmem_limit_bytes=32 * 2**20),
         cost_estimate=pl.CostEstimate(flops=10**8, bytes_accessed=3 * 2**20, transcendentals=0),
     )(place, jnp.asarray(table.reshape(-1)), iterate, forcing)

time: 127 us -> 83.4 us (0.66)
  Pallas kernels: 51 us -> 8.26 us
    pallas_call x1, Pallas kernels: 51 us -> 8.26 us  [coarse_part(): pl.pallas_call(functools.partial(coarse_kernel, powers, 4 * steps, slabs)...]
  transfers between devices with their start and end apart: 8 -> 8, of which waited for: 4 -> 4; matrix products, arithmetic and copies ran while one was open for 5% -> 7% of each run, Pallas kernels for 40% -> 10%
where the time goes in v3:
time: 83.4 us; the launch traced here: 82.9 us
  waiting for transfers between devices  36.9 us (44%)
  starting transfers between devices  24.9 us (30%)
  Pallas kernels  8.26 us (10%)
  other arithmetic  7.02 us (8%)
  local copies, waits for them, and re-layouts  4.81 us (6%)
  between operations  0.96 us (1%)
    ppermute x4, waiting for transfers between devices, shifted(): lax.ppermute(value, axis, [(i, i + by) for i in range(size) if 0 <= i + b...  15.7 us
    ppermute x4, starting transfers between devices, shifted(): lax.ppermute(value, axis, [(i, i + by) for i in range(size) if 0 <= i + b...  8.54 us
    all_to_all x1, waiting for transfers between devices, spread_sum(): parts = lax.all_to_all(tiles, 'tm', 0, 0, tiled=True)  8.39 us
    pallas_call x1, Pallas kernels, coarse_part(): pl.pallas_call(functools.partial(coarse_kernel, powers, 4 * steps, slabs)...  8.26 us
    all_to_all x1, waiting for transfers between devices, spread_sum(): lax.all_to_all(copies, 'tm', 0, 0, tiled=True)  7.69 us
    all_to_all x1, starting transfers between devices, spread_sum(): parts = lax.all_to_all(tiles, 'tm', 0, 0, tiled=True)  7.2 us
    ppermute x2, starting transfers between devices, swapped(): lax.ppermute(value, axis, [(i, i ^ mask) for i in range(lax.axis_size(axi...  5.4 us
    ppermute x2, waiting for transfers between devices, swapped(): lax.ppermute(value, axis, [(i, i ^ mask) for i in range(lax.axis_size(axi...  5.2 us
  transfers between devices with their start and end apart: 8, of which 4 were waited for; matrix products, arithmetic and copies ran while one was open for 7% of the time, Pallas kernels for 10%

profile of v3, /device:TPU:0, one launch (start us, length us, event | category | flops | bytes accessed | tf_op | source)
XLA Modules:
  0.0 82.9 jit_solution(7183716329316762992)
XLA Ops:
  0.6 1.4 %fusion.41 = (f32[2,2,2,4096]{3,2,1,0:T(2,128)S(1)}, f32[2,2,2,4096]{3,2,1,0:T(2,128)S(1)}) fusion(f32[2,2,8,4096]{3,2,1,0:T(8,128)} %iterate_ref.1), kind=kLoop, calls=%fused_computation.97 | loop fusion | bytes 524288 | tf_op jit(solution)/shard_map/slice | solution.py:227
  2.3 2.5 %collective-permute-start = (f32[2,2,3,4096]{3,2,1,0:T(4,128)S(1)}, f32[2,2,3,4096]{3,2,1,0:T(4,128)S(1)}, u32[]{:S(2)}, u32[]{:S(2)}) collective-permute-start(f32[2,2,3,4096]{3,2,1,0:T(4,128)S(1)} %pad_maximum_fusion.6), channel_id=1, source_target_pairs={{0,1},{1,2},{2,3},{4,5},{5,6},{6,7},{8,9},{9,10},{10,11},{12,13},{... | collective-permute-start | bytes 589832 | tf_op jit(solution)/shard_map/ppermute | solution.py:83
  4.9 1.3 %collective-permute-start.1 = (f32[2,2,3,4096]{3,2,1,0:T(4,128)S(1)}, f32[2,2,3,4096]{3,2,1,0:T(4,128)S(1)}, u32[]{:S(2)}, u32[]{:S(2)}) collective-permute-start(f32[2,2,3,4096]{3,2,1,0:T(4,128)S(1)} %pad_maximum_fusion.7), channel_id=1, source_target_pairs={{1,0},{2,1},{3,2},{5,4},{6,5},{7,6},{9,8},{10,9},{11,10},{13,12},{... | collective-permute-start | bytes 589832 | tf_op jit(solution)/shard_map/ppermute | solution.py:83
  6.3 0.6 copy-done.2
  6.9 8.3 %shard_map.50 = (f32[2,2,32,8,128]{4,3,2,1,0:T(8,128)S(1)}, f32[2,2,32,8,128]{4,3,2,1,0:T(8,128)S(1)}) custom-call(s32[2]{0:T(128)S(1)} %pad_add_fusion.place_ref, f32[1408]{0:T(1024)S(1)} %copy-done.2, f32[2,2,8,4096]{3,2,1,0:T(8,128)S(1)} %copy-done.1, f32[2,2,8,4096]{3,2,1,0:T(8,128)S(1)} %copy-done), custom_call_target="tpu_custom_call" | custom-call | flops 100000000 | bytes 3145728 | tf_op jit(solution)/shard_map/pallas_call | solution.py:192
  15.2 3.3 %collective-permute-start.4 = (f32[2,2,32,8,128]{4,3,2,1,0:T(8,128)S(1)}, f32[2,2,32,8,128]{4,3,2,1,0:T(8,128)}, u32[]{:S(2)}, u32[]{:S(2)}) collective-permute-start(f32[2,2,32,8,128]{4,3,2,1,0:T(8,128)S(1)} %get-tuple-element.5), channel_id=1, source_target_pairs={{0,1},{1,0},{2,3},{3,2},{4,5},{5,4},{6,7},{7,6},{8,9},{9,8},{10,11... | collective-permute-start | bytes 1572872 | tf_op jit(solution)/shard_map/ppermute | solution.py:78
  20.0 0.7 fusion
  20.8 0.4 subtract_bitcast_fusion
  21.5 3.4 %collective-permute-start.2 = (f32[18,4096]{1,0:T(8,128)S(1)}, f32[18,4096]{1,0:T(8,128)S(1)}, u32[]{:S(2)}, u32[]{:S(2)}) collective-permute-start(f32[18,4096]{1,0:T(8,128)S(1)} %pad_maximum_fusion.3), channel_id=1, source_target_pairs={{0,4},{4,8},{8,12},{12,16},{16,20},{20,24},{24,28},{1,5},{5,9},{9,... | collective-permute-start | bytes 884744 | tf_op jit(solution)/shard_map/ppermute | solution.py:83
  25.0 1.3 %collective-permute-start.3 = (f32[18,4096]{1,0:T(8,128)S(1)}, f32[18,4096]{1,0:T(8,128)S(1)}, u32[]{:S(2)}, u32[]{:S(2)}) collective-permute-start(f32[18,4096]{1,0:T(8,128)S(1)} %pad_maximum_fusion.4), channel_id=1, source_target_pairs={{4,0},{8,4},{12,8},{16,12},{20,16},{24,20},{28,24},{5,1},{9,5},{13... | collective-permute-start | bytes 884744 | tf_op jit(solution)/shard_map/ppermute | solution.py:83
  26.3 15.7 %collective-permute-done.2 = f32[18,4096]{1,0:T(8,128)S(1)} collective-permute-done((f32[18,4096]{1,0:T(8,128)S(1)}, f32[18,4096]{1,0:T(8,128)S(1)}, u32[]{:S(2)}, u32[]{:S(2)}) %collective-permute-start.2) | collective-permute-done | bytes 294944 | tf_op jit(solution)/shard_map/ppermute | solution.py:83
  42.8 0.4 fusion.4
  43.1 1.1 %add.143 = f32[2,2,32,8,128]{4,3,2,1,0:T(8,128)S(1)} add(f32[2,2,32,8,128]{4,3,2,1,0:T(8,128)S(1)} %get-tuple-element.4, f32[2,2,32,8,128]{4,3,2,1,0:T(8,128)} %collective-permute-done.4) | non-fusion elementwise | flops 131072 | bytes 1572864 | tf_op jit(solution)/shard_map/add | solution.py:206
  44.3 2.1 %collective-permute-start.5 = (f32[1,2,32,8,128]{4,3,2,1,0:T(8,128)S(1)}, f32[1,2,32,8,128]{4,3,2,1,0:T(8,128)S(1)}, u32[]{:S(2)}, u32[]{:S(2)}) collective-permute-start(f32[1,2,32,8,128]{4,3,2,1,0:T(8,128)S(1)} %constant_dynamic-slice_fusion), channel_id=1, source_target_pairs={{0,2},{1,3},{2,0},{3,1},{4,6},{5,7},{6,4},{7,5},{8,10},{9,11},{10,... | collective-permute-start | bytes 786440 | tf_op jit(solution)/shard_map/ppermute | solution.py:78
  46.4 0.9 %multiply_subtract_fusion = (f32[1,2,8,4096]{3,2,1,0:T(8,128)}, f32[1,2,8,4096]{3,2,1,0:T(8,128)S(1)}) fusion(f32[1,1,8,4096]{3,2,1,0:T(8,128)S(1)} %slice.245, f32[1,1,8,4096]{3,2,1,0:T(8,128)S(1)} %get-tuple-element.28, f32[2,2,8,4096]{3,2,1,0:T(8,128)S(1)} %fusion.4, f32[2,2,8,4096]{3,2,1,0:T(8,128)S(1)} %copy-done, ...), kind=kLoop, calls=%fused_computation.72 | loop fusion | flops 1441792 | bytes 2752512 | tf_op jit(solution)/shard_map/sub | solution.py:238
  47.3 5.2 %collective-permute-done.5 = f32[1,2,32,8,128]{4,3,2,1,0:T(8,128)S(1)} collective-permute-done((f32[1,2,32,8,128]{4,3,2,1,0:T(8,128)S(1)}, f32[1,2,32,8,128]{4,3,2,1,0:T(8,128)S(1)}, u32[]{:S(2)}, u32[]{:S(2)}) %collective-permute-start.5) | collective-permute-done | bytes 262176 | tf_op jit(solution)/shard_map/ppermute | solution.py:78
  52.5 0.7 dynamic-slice_add_fusion
  53.2 7.2 %all-to-all-start = ((f32[8,8,8,128]{3,2,1,0:T(8,128)}), f32[8,8,8,128]{3,2,1,0:T(8,128)S(1)}, u32[]{:S(2)}, u32[]{:S(2)}) async-start(f32[8,8,8,128]{3,2,1,0:T(8,128)} %bitcast.28), calls=%async_computation | async-start | bytes 524288 | tf_op jit(solution)/shard_map/all_to_all | solution.py:216
  60.6 8.4 %all-to-all-done = f32[8,8,8,128]{3,2,1,0:T(8,128)S(1)} async-done(((f32[8,8,8,128]{3,2,1,0:T(8,128)}), f32[8,8,8,128]{3,2,1,0:T(8,128)S(1)}, u32[]{:S(2)}, u32[]{:S(2)}) %all-to-all-start) | async-done | bytes 262176 | tf_op jit(solution)/shard_map/all_to_all | solution.py:216
  69.1 0.7 broadcast_in_dim.76
  69.8 3.7 %all-to-all-start.1 = ((f32[8,8,8,128]{3,2,1,0:T(8,128)}), f32[8,8,8,128]{3,2,1,0:T(8,128)S(1)}, u32[]{:S(2)}, u32[]{:S(2)}) async-start(f32[8,8,8,128]{3,2,1,0:T(8,128)} %broadcast_in_dim.76), calls=%async_computation.1 | async-start | bytes 524288 | tf_op jit(solution)/shard_map/all_to_all | solution.py:219
  73.5 0.8 pad_maximum_fusion.2
  74.3 7.7 %all-to-all-done.1 = f32[8,8,8,128]{3,2,1,0:T(8,128)S(1)} async-done(((f32[8,8,8,128]{3,2,1,0:T(8,128)}), f32[8,8,8,128]{3,2,1,0:T(8,128)S(1)}, u32[]{:S(2)}, u32[]{:S(2)}) %all-to-all-start.1) | async-done | bytes 262176 | tf_op jit(solution)/shard_map/all_to_all | solution.py:219
  82.0 0.8 broadcast_in_dim.78
  (46 shorter events, 3.2 us)
Async XLA Ops:
  0.6 1.4 %copy-start = (f32[2,2,8,4096]{3,2,1,0:T(8,128)S(1)}, f32[2,2,8,4096]{3,2,1,0:T(8,128)}, u32[]{:S(2)}) copy-start(f32[2,2,8,4096]{3,2,1,0:T(8,128)} %forcing_ref.1) | copy-start | bytes 1572868
  2.2 4.2 %copy-start.1 = (f32[2,2,8,4096]{3,2,1,0:T(8,128)S(1)}, f32[2,2,8,4096]{3,2,1,0:T(8,128)}, u32[]{:S(2)}) copy-start(f32[2,2,8,4096]{3,2,1,0:T(8,128)} %iterate_ref.1) | copy-start | bytes 1572868
  2.3 16.2 %collective-permute-start = (f32[2,2,3,4096]{3,2,1,0:T(4,128)S(1)}, f32[2,2,3,4096]{3,2,1,0:T(4,128)S(1)}, u32[]{:S(2)}, u32[]{:S(2)}) collective-permute-start(f32[2,2,3,4096]{3,2,1,0:T(4,128)S(1)} %pad_maximum_fusion.6), channel_id=1, source_target_pairs={{0,1},{1,2},{2,3},{4,5},{5,6},{6,7},{8,9},{9,10},{10,11},{12,13},{... | collective-permute-start | bytes 589832 | tf_op jit(solution)/shard_map/ppermute | solution.py:83
  4.9 13.6 %collective-permute-start.1 = (f32[2,2,3,4096]{3,2,1,0:T(4,128)S(1)}, f32[2,2,3,4096]{3,2,1,0:T(4,128)S(1)}, u32[]{:S(2)}, u32[]{:S(2)}) collective-permute-start(f32[2,2,3,4096]{3,2,1,0:T(4,128)S(1)} %pad_maximum_fusion.7), channel_id=1, source_target_pairs={{1,0},{2,1},{3,2},{5,4},{6,5},{7,6},{9,8},{10,9},{11,10},{13,12},{... | collective-permute-start | bytes 589832 | tf_op jit(solution)/shard_map/ppermute | solution.py:83
  6.2 0.7 copy-start.2
  15.2 27.9 %collective-permute-start.4 = (f32[2,2,32,8,128]{4,3,2,1,0:T(8,128)S(1)}, f32[2,2,32,8,128]{4,3,2,1,0:T(8,128)}, u32[]{:S(2)}, u32[]{:S(2)}) collective-permute-start(f32[2,2,32,8,128]{4,3,2,1,0:T(8,128)S(1)} %get-tuple-element.5), channel_id=1, source_target_pairs={{0,1},{1,0},{2,3},{3,2},{4,5},{5,4},{6,7},{7,6},{8,9},{9,8},{10,11... | collective-permute-start | bytes 1572872 | tf_op jit(solution)/shard_map/ppermute | solution.py:78
  21.5 20.5 %collective-permute-start.2 = (f32[18,4096]{1,0:T(8,128)S(1)}, f32[18,4096]{1,0:T(8,128)S(1)}, u32[]{:S(2)}, u32[]{:S(2)}) collective-permute-start(f32[18,4096]{1,0:T(8,128)S(1)} %pad_maximum_fusion.3), channel_id=1, source_target_pairs={{0,4},{4,8},{8,12},{12,16},{16,20},{20,24},{24,28},{1,5},{5,9},{9,... | collective-permute-start | bytes 884744 | tf_op jit(solution)/shard_map/ppermute | solution.py:83
  25.0 17.0 %collective-permute-start.3 = (f32[18,4096]{1,0:T(8,128)S(1)}, f32[18,4096]{1,0:T(8,128)S(1)}, u32[]{:S(2)}, u32[]{:S(2)}) collective-permute-start(f32[18,4096]{1,0:T(8,128)S(1)} %pad_maximum_fusion.4), channel_id=1, source_target_pairs={{4,0},{8,4},{12,8},{16,12},{20,16},{24,20},{28,24},{5,1},{9,5},{13... | collective-permute-start | bytes 884744 | tf_op jit(solution)/shard_map/ppermute | solution.py:83
  42.7 3.6 %copy-start.3 = (f32[1,1,8,4096]{3,2,1,0:T(8,128)}, f32[1,1,8,4096]{3,2,1,0:T(8,128)S(1)}, u32[]{:S(2)}) copy-start(f32[1,1,8,4096]{3,2,1,0:T(8,128)S(1)} %get-tuple-element.28) | copy-start | bytes 393220
  44.3 8.2 %collective-permute-start.5 = (f32[1,2,32,8,128]{4,3,2,1,0:T(8,128)S(1)}, f32[1,2,32,8,128]{4,3,2,1,0:T(8,128)S(1)}, u32[]{:S(2)}, u32[]{:S(2)}) collective-permute-start(f32[1,2,32,8,128]{4,3,2,1,0:T(8,128)S(1)} %constant_dynamic-slice_fusion), channel_id=1, source_target_pairs={{0,2},{1,3},{2,0},{3,1},{4,6},{5,7},{6,4},{7,5},{8,10},{9,11},{10,... | collective-permute-start | bytes 786440 | tf_op jit(solution)/shard_map/ppermute | solution.py:78
  53.2 7.2 %copy-start.4 = (f32[1,1,8,4096]{3,2,1,0:T(8,128)S(1)}, f32[1,1,8,4096]{3,2,1,0:T(8,128)}, u32[]{:S(2)}) copy-start(f32[1,1,8,4096]{3,2,1,0:T(8,128)} %copy-done.3) | copy-start | bytes 393220
  53.2 15.8 %all-to-all-start = ((f32[8,8,8,128]{3,2,1,0:T(8,128)}), f32[8,8,8,128]{3,2,1,0:T(8,128)S(1)}, u32[]{:S(2)}, u32[]{:S(2)}) async-start(f32[8,8,8,128]{3,2,1,0:T(8,128)} %bitcast.28), calls=%async_computation | async-start | bytes 524288 | tf_op jit(solution)/shard_map/all_to_all | solution.py:216
  69.8 3.7 %copy-start.5 = (f32[1,2,8,4096]{3,2,1,0:T(8,128)S(1)}, f32[1,2,8,4096]{3,2,1,0:T(8,128)}, u32[]{:S(2)}) copy-start(f32[1,2,8,4096]{3,2,1,0:T(8,128)} %get-tuple-element.6) | copy-start | bytes 786436
  69.8 12.2 %all-to-all-start.1 = ((f32[8,8,8,128]{3,2,1,0:T(8,128)}), f32[8,8,8,128]{3,2,1,0:T(8,128)S(1)}, u32[]{:S(2)}, u32[]{:S(2)}) async-start(f32[8,8,8,128]{3,2,1,0:T(8,128)} %broadcast_in_dim.76), calls=%async_computation.1 | async-start | bytes 524288 | tf_op jit(solution)/shard_map/all_to_all | solution.py:219

commit v4 on v1

v4 whole, which is shorter than its diff:
```python
import functools

import numpy as np

import jax
import jax.numpy as jnp
from jax import lax
from jax.experimental import pallas as pl
from jax.experimental.pallas import tpu as pltpu
from jax.sharding import PartitionSpec as P

NY = 64
LANES = 128

KAPPA_BASE = 0.25
COUPLING_BASE = 0.5
DAMPING = 0.6


def level_terms(level):
    diffusion = KAPPA_BASE * 2.0**level
    coupling = COUPLING_BASE * 2.0**level
    centre = 1.0 + 6.0 * diffusion
    determinant = centre * centre + coupling * coupling
    along = DAMPING * centre / determinant
    across = DAMPING * coupling / determinant
    return diffusion, coupling, centre, along, across


def coarse_polynomials(total_steps):
    levels = total_steps.bit_length()
    powers = 2 * levels + 1
    unit = np.eye(4 * total_steps).reshape(-1, 2, 2, total_steps)
    fields = np.zeros((4 * total_steps, 2, total_steps, powers))
    source = np.zeros_like(fields)
    fields[..., 0] = unit[:, 0]
    source[..., 0] = unit[:, 1]

    def image(values, diffusion, coupling, centre):
        out = centre * values
        out[..., 1:] -= diffusion * values[..., :-1]
        out[:, 0, 1:] -= values[:, 0, :-1]
        out[:, 1, :-1] -= values[:, 1, 1:]
        out[:, 0] += coupling * values[:, 1]
        out[:, 1] -= coupling * values[:, 0]
        return out

    for level in range(levels):
        diffusion, coupling, centre, along, across = level_terms(level)
        for _ in range(2):
            defect = source - image(fields, diffusion, coupling, centre)
            state, adjoint = defect[:, 0], defect[:, 1]
            fields = fields + np.stack([along * state - across * adjoint, across * state + along * adjoint], 1)
        if level < levels - 1:
            defect = source - image(fields, diffusion, coupling, centre)
            source = defect[:, :, 0::2] + defect[:, :, 1::2]
            fields = np.zeros_like(source)
    return fields[:, :, 0].reshape(2, 2, total_steps, 2, powers)


def lane_index(depth):
    return lax.broadcasted_iota(jnp.int32, (depth, LANES), 1)


def sublane_index(depth):
    return lax.broadcasted_iota(jnp.int32, (depth, LANES), 0)


def column(j):
    return pl.ds(j * LANES, LANES)


def swapped_halves(value):
    return pltpu.roll(value, NY, 1)


def beside(value, lane):
    left = pltpu.roll(jnp.where((lane % NY) != NY - 1, value, 0.0), 1, 1)
    right = pltpu.roll(jnp.where((lane % NY) != 0, value, 0.0), LANES - 1, 1)
    return left + right


def tree_sum(terms):
    while len(terms) > 1:
        terms = [sum(terms[k : k + 2]) for k in range(0, len(terms), 2)]
    return terms[0]


def coarse_kernel(powers, steps, slabs, middle, place_ref, weights_ref, iterate_ref, forcing_ref, keep_ref, send_ref, even, odd, packed):
    depth, cells = iterate_ref.shape[2:]
    columns = cells // LANES
    rows = cells // NY
    inputs = 2 * steps
    slab, shift = place_ref[1], place_ref[2]
    base = place_ref[0] * (powers * 4 * inputs)
    lane = lane_index(depth)
    low = lane < NY
    zero = jnp.zeros((depth, LANES), jnp.float32)

    def inside(away):
        at = slab + away
        return jnp.where((at >= 0) & (at < slabs), 1.0, 0.0).astype(jnp.float32)

    for j in range(columns):
        for kind, ref in enumerate((iterate_ref, forcing_ref)):
            for n in range(steps):
                state, adjoint = ref[0, n, :, column(j)], ref[1, n, :, column(j)]
                state_turned, adjoint_turned = swapped_halves(state), swapped_halves(adjoint)
                k = 2 * (kind * steps + n)
                packed[k, 2 * j] = jnp.where(low, state, adjoint_turned)
                packed[k, 2 * j + 1] = jnp.where(low, state_turned, adjoint)
                packed[k + 1, 2 * j] = jnp.where(low, adjoint, state_turned)
                packed[k + 1, 2 * j + 1] = jnp.where(low, adjoint_turned, state)

    def weights(power):
        first = base + power * 4 * inputs
        return [
            jnp.where(low, weights_ref[first + 2 * k], weights_ref[first + 2 * k + 1]) for k in range(2 * inputs)
        ]

    def injected(factors, i):
        return tree_sum([factor * packed[k, i] for k, factor in enumerate(factors)])

    def advance(source, target, power, reach):
        aways = list(range(-reach, reach + 1))
        masks = [inside(away) for away in aways]
        factors = weights(power)

        def loaded(i):
            if i >= rows:
                return [zero for _ in aways]
            return [source[i, pl.ds((middle + away) * depth, depth), :] for away in aways]

        before = [zero for _ in aways]
        now = loaded(0)
        for i in range(rows):
            later = loaded(i + 1)
            for k, away in enumerate(aways):
                start = (middle + away) * depth
                above = source[i, pl.ds(shift + (start - 1), depth), :]
                below = source[i, pl.ds(shift + (start + 1), depth), :]
                value = (before[k] + later[k]) + beside(now[k], lane) + (above + below)
                if away:
                    value = value * masks[k]
                else:
                    value = value + injected(factors, i)
                target[i, pl.ds(start, depth), :] = value
            before, now = now, later

    even[...] = jnp.zeros_like(even)
    odd[...] = jnp.zeros_like(odd)
    factors = weights(powers - 1)
    for i in range(rows):
        even[i, pl.ds(middle * depth, depth), :] = injected(factors, i)
    buffers = (even, odd)
    done = 0
    while done < powers - 1:
        reach = min(done // depth + 1, slabs - 1)
        count = powers - 1 - done if reach == slabs - 1 else min(depth, powers - 1 - done)

        def twice(index, _):
            power = powers - 2 - done - 2 * index
            advance(buffers[0], buffers[1], power, reach)
            advance(buffers[1], buffers[0], power - 1, reach)
            return 0

        lax.fori_loop(0, count // 2, twice, 0)
        done += count
        if count % 2:
            advance(buffers[0], buffers[1], powers - 1 - done, reach)
            buffers = buffers[::-1]

    final = buffers[0]
    tiles = keep_ref.shape[2]
    bit = lax.rem(slab, 2)
    for half in range(slabs // 2):
        for ref, flag in ((keep_ref, bit), (send_ref, 1 - bit)):
            away = 2 * half + flag - slab
            planes = pl.ds(pl.multiple_of((middle + away) * depth, depth), depth)
            for j in range(columns):
                first, second = final[2 * j, planes, :], final[2 * j + 1, planes, :]
                for f, value in (
                    (0, jnp.where(low, first, swapped_halves(second))),
                    (1, jnp.where(low, swapped_halves(first), second)),
                ):
                    tile = f * columns + j
                    ref[tile // tiles, half, tile % tiles] = value


def vmem_call(kernel, out_shapes, smem_inputs, inputs, scratch=(), flops=10**6):
    smem = pl.BlockSpec(memory_space=pltpu.SMEM)
    vmem = pl.BlockSpec(memory_space=pltpu.VMEM)
    out_shape = tuple(jax.ShapeDtypeStruct(shape, jnp.float32) for shape in out_shapes)
    return pl.pallas_call(
        kernel,
        out_shape=out_shape,
        in_specs=[smem] * len(smem_inputs) + [vmem] * len(inputs),
        out_specs=(vmem,) * len(out_shape),
        scratch_shapes=list(scratch),
        compiler_params=pltpu.CompilerParams(vmem_limit_bytes=32 * 2**20),
        cost_estimate=pl.CostEstimate(flops=flops, bytes_accessed=2**20, transcendentals=0),
    )(*smem_inputs, *inputs)


def coarse_part(place, iterate, forcing):
    steps = iterate.shape[1]
    depth, cells = iterate.shape[2:]
    ranks, slabs = lax.axis_size("tm"), 2 * lax.axis_size("pair")
    table = coarse_polynomials(steps * ranks)
    powers = table.shape[-1]
    table = table.reshape(2, 2, ranks, steps, 2, powers)
    same = np.stack([table[:, 0, :, :, 0], table[:, 1, :, :, 1]], -1)
    other = np.stack([table[:, 1, :, :, 0], table[:, 0, :, :, 1]], -1)
    weights = np.stack([same, other], -2).transpose(1, 3, 0, 2, 4, 5).astype(np.float32)
    reach = min(-(-(powers - 1) // depth), slabs - 1)
    middle = max(reach + 1, slabs - 1)
    tiles = 2 * cells // LANES
    half = (ranks, slabs // 2, tiles // ranks, depth, LANES)
    buffer = pltpu.VMEM((cells // NY, (2 * middle + 1) * depth, LANES), jnp.float32)
    packed = pltpu.VMEM((4 * steps, cells // NY, depth, LANES), jnp.float32)
    return vmem_call(
        functools.partial(coarse_kernel, powers, steps, slabs, middle),
        (half, half),
        (place, jnp.asarray(weights.reshape(-1))),
        (iterate, forcing),
        (buffer, buffer, packed),
        flops=10**8,
    )


def relaxed(fields, around, before, after, source):
    diffusion, coupling, centre, along, across = level_terms(0)
    state, adjoint = fields
    defect_state = source[0] - (centre * state - diffusion * around[0] - before + coupling * adjoint)
    defect_adjoint = source[1] - (centre * adjoint - diffusion * around[1] - after - coupling * state)
    return (
        state + along * defect_state - across * defect_adjoint,
        adjoint + across * defect_state + along * defect_adjoint,
    )


def first_kernel(iterate_ref, forcing_ref, first_ref, up_ref, down_ref):
    steps, depth, cells = iterate_ref.shape[1:]
    columns = cells // LANES
    lane, sublane = lane_index(depth), sublane_index(depth)
    low = lane < NY
    zero = jnp.zeros((depth, LANES), jnp.float32)
    slots = [(f, n) for f in range(2) for n in range(steps)]

    def loaded(j):
        return {s: iterate_ref[s[0], s[1], :, column(j)] if j < columns else zero for s in slots}

    now = loaded(0)
    pairs_before = now
    for j in range(columns):
        later = loaded(j + 1)
        pairs = {s: now[s] + later[s] for s in slots}
        around = {}
        for s in slots:
            across_rows = swapped_halves(jnp.where(low, pairs[s], pairs_before[s]))
            above = jnp.where(sublane == 0, 0.0, pltpu.roll(now[s], 1, 0))
            below = jnp.where(sublane == depth - 1, 0.0, pltpu.roll(now[s], depth - 1, 0))
            around[s] = across_rows + beside(now[s], lane) + (above + below)
        for n in range(steps):
            values = relaxed(
                (now[0, n], now[1, n]),
                (around[0, n], around[1, n]),
                now[0, n - 1] if n else zero,
                now[1, n + 1] if n < steps - 1 else zero,
                (forcing_ref[0, n, :, column(j)], forcing_ref[1, n, :, column(j)]),
            )
            for f in range(2):
                first_ref[f, n, :, column(j)] = values[f]
                slot = f * steps + n
                for ref, plane in ((up_ref, depth - 1), (down_ref, 0)):
                    ref[slot : slot + 1, column(j)] = now[f, n][plane : plane + 1]
                    slot_after = 2 * steps + slot
                    ref[slot_after : slot_after + 1, column(j)] = values[f][plane : plane + 1]
        now, pairs_before = later, pairs


def second_kernel(
    steps, slabs, place_ref, iterate_ref, first_ref, up_ref, down_ref, above_ref, below_ref, swept_ref, edge_ref, forth_ref, back_ref
):
    diffusion, _, _, along, across = level_terms(0)
    depth, cells = iterate_ref.shape[2:]
    columns = cells // LANES
    slab = place_ref[1]
    sublane = sublane_index(depth)
    count = 2 * steps
    has_above = jnp.where(slab > 0, 1.0, 0.0).astype(jnp.float32)
    has_below = jnp.where(slab < slabs - 1, 1.0, 0.0).astype(jnp.float32)

    def mixed(rows):
        state, adjoint = rows[:steps], rows[steps:]
        return jnp.concatenate(
            [
                (along * diffusion) * state - (across * diffusion) * adjoint,
                (across * diffusion) * state + (along * diffusion) * adjoint,
            ],
            0,
        )

    def one(j):
        return slice(j * LANES, (j + 1) * LANES)

    for j in range(columns):
        from_above, from_below = above_ref[:, one(j)], below_ref[:, one(j)]
        edge_ref[:count, one(j)] = (from_above[count:] + mixed(down_ref[:count, one(j)])) * has_above
        edge_ref[count:, one(j)] = (from_below[count:] + mixed(up_ref[:count, one(j)])) * has_below
        add_above, add_below = mixed(from_above[:count]), mixed(from_below[:count])
        for f in range(2):
            for n in range(steps):
                k = f * steps + n
                value = first_ref[f, n, :, one(j)]
                value = value + jnp.where(sublane == 0, add_above[k : k + 1], 0.0)
                value = value + jnp.where(sublane == depth - 1, add_below[k : k + 1], 0.0)
                swept_ref[f, n, :, one(j)] = value
                for ref, field, step in ((forth_ref, 0, steps - 1), (back_ref, 1, 0)):
                    if (f, n) == (field, step):
                        ref[j] = iterate_ref[f, n, :, one(j)]
                        ref[columns + j] = value
                        block, row = 2 * columns + j // depth, j % depth
                        ref[block, row : row + 1] = from_above[k : k + 1]
                        block += columns // depth
                        ref[block, row : row + 1] = from_below[k : k + 1]


def third_kernel(steps, ranks, place_ref, iterate_ref, forcing_ref, swept_ref, edge_ref, forth_ref, back_ref, out_ref):
    _, _, _, along, across = level_terms(0)
    depth, cells = iterate_ref.shape[2:]
    columns = cells // LANES
    rank = place_ref[0]
    lane, sublane = lane_index(depth), sublane_index(depth)
    low = lane < NY
    zero = jnp.zeros((depth, LANES), jnp.float32)
    slots = [(f, n) for f in range(2) for n in range(steps)]
    has_before = jnp.where(rank > 0, 1.0, 0.0).astype(jnp.float32)
    has_after = jnp.where(rank < ranks - 1, 1.0, 0.0).astype(jnp.float32)
    gain = {(0, 0): ("forth", along), (1, 0): ("forth", across), (0, steps - 1): ("back", -across), (1, steps - 1): ("back", along)}

    def loaded(j):
        if j >= columns:
            return {s: zero for s in slots}
        near = {"forth": forth_ref[j], "back": back_ref[j]}
        values = {}
        for s in slots:
            values[s] = swept_ref[s[0], s[1], :, column(j)]
            if s in gain:
                values[s] = values[s] + gain[s][1] * near[gain[s][0]]
        return values

    def edges(j, side):
        block, row = 2 * columns + side * (columns // depth) + j // depth, j % depth
        near = {"forth": forth_ref[block, row : row + 1], "back": back_ref[block, row : row + 1]}
        values = {}
        for s in slots:
            k = side * 2 * steps + s[0] * steps + s[1]
            values[s] = edge_ref[k : k + 1, column(j)]
            if s in gain:
                values[s] = values[s] + gain[s][1] * near[gain[s][0]]
        return values

    now = loaded(0)
    pairs_before = now
    for j in range(columns):
        later = loaded(j + 1)
        over, under = edges(j, 0), edges(j, 1)
        pairs = {s: now[s] + later[s] for s in slots}
        around = {}
        for s in slots:
            across_rows = swapped_halves(jnp.where(low, pairs[s], pairs_before[s]))
            above = jnp.where(sublane == 0, over[s], pltpu.roll(now[s], 1, 0))
            below = jnp.where(sublane == depth - 1, under[s], pltpu.roll(now[s], depth - 1, 0))
            around[s] = across_rows + beside(now[s], lane) + (above + below)
        before = (forth_ref[columns + j] - across * iterate_ref[1, 0, :, column(j)]) * has_before
        after = (back_ref[columns + j] + across * iterate_ref[0, steps - 1, :, column(j)]) * has_after
        for n in range(steps):
            values = relaxed(
                (now[0, n], now[1, n]),
                (around[0, n], around[1, n]),
                now[0, n - 1] if n else before,
                now[1, n + 1] if n < steps - 1 else after,
                (forcing_ref[0, n, :, column(j)], forcing_ref[1, n, :, column(j)]),
            )
            for f in range(2):
                out_ref[f, n, :, column(j)] = values[f]
        now, pairs_before = later, pairs


def shifted(value, axis, by):
    size = lax.axis_size(axis)
    return lax.ppermute(value, axis, [(i, i + by) for i in range(size) if 0 <= i + by < size])


def sum_kernel(parts_ref, copies_ref):
    tiles = copies_ref.shape[1]
    for tile in range(tiles):
        total = tree_sum([parts_ref[k, tile] for k in range(parts_ref.shape[0])])
        for k in range(copies_ref.shape[0]):
            copies_ref[k, tile] = total


def local(iterate, forcing):
    steps, depth, cells = iterate.shape[1:]
    columns = cells // LANES
    ranks, slabs = lax.axis_size("tm"), 2 * lax.axis_size("pair")
    place = jnp.stack([lax.axis_index("tm"), lax.axis_index(("pair", "core")), jnp.zeros((), jnp.int32)]).astype(jnp.int32)
    first, up, down = vmem_call(
        first_kernel, (iterate.shape, (4 * steps, cells), (4 * steps, cells)), (), (iterate, forcing)
    )
    above = shifted(up, ("pair", "core"), 1)
    below = shifted(down, ("pair", "core"), -1)
    payload = (2 * columns + 2 * columns // depth, depth, LANES)
    swept, edge, forth, back = vmem_call(
        functools.partial(second_kernel, steps, slabs),
        (iterate.shape, (4 * steps, cells), payload, payload),
        (place,),
        (iterate, first, up, down, above, below),
    )
    forth = shifted(forth, "tm", 1)
    back = shifted(back, "tm", -1)

    keep, send = coarse_part(place, iterate, forcing)
    held = keep + lax.ppermute(send, "core", [(0, 1), (1, 0)])
    shape = held.shape
    parts = lax.all_to_all(held.reshape((-1,) + shape[2:]), ("tm", "pair"), 0, 0, tiled=True)
    (copies,) = vmem_call(sum_kernel, ((ranks,) + shape[2:],), (), (parts,))
    coarse = lax.all_to_all(copies, "tm", 0, 0, tiled=True).reshape(2, columns, depth, LANES)
    coarse = coarse.transpose(0, 2, 1, 3).reshape(2, depth, cells)

    (smoothed,) = vmem_call(
        functools.partial(third_kernel, steps, ranks),
        (iterate.shape,),
        (place,),
        (iterate, forcing, swept, edge, forth, back),
    )
    return smoothed, jnp.broadcast_to(coarse[:, None], iterate.shape)


def solution(mesh):
    ranks, slabs = mesh.shape["tm"], mesh.shape["space"]
    fine = jax.sharding.Mesh(mesh.devices.reshape(ranks, slabs // 2, 2), ("tm", "pair", "core"))
    specs = P(None, "tm", ("pair", "core"), None)
    return jax.shard_map(local, mesh=fine, in_specs=(specs, specs), out_specs=(specs, specs), check_vma=False)
```

time: 217 us -> 68.2 us (0.31)
  the two profiles are of different devices: /device:TPU:0 before, /device:TPU:9 now
where the time goes in v4:
time: 68.2 us; the launch traced here: 67.8 us
  blocking collectives  20.1 us (29%)
  starting transfers between devices  17.5 us (26%)
  waiting for transfers between devices  15.2 us (22%)
  Pallas kernels  10.6 us (16%)
  local copies, waits for them, and re-layouts  3.53 us (5%)
  between operations  0.72 us (1%)
    all_to_all x1, blocking collectives, local(): lax.all_to_all(held.reshape((-1,) + shape[2:]), ('tm', 'pair'), 0, 0, til...  20.1 us
    ppermute x4, waiting for transfers between devices, shifted(): lax.ppermute(value, axis, [(i, i + by) for i in range(size) if 0 <= i + b...  13.6 us
    ppermute x4, starting transfers between devices, shifted(): lax.ppermute(value, axis, [(i, i + by) for i in range(size) if 0 <= i + b...  12.2 us
    pallas_call x5, Pallas kernels, vmem_call(): pl.pallas_call(kernel, out_shape=out_shape, in_specs=[smem] * len(smem_in...  10.6 us
    all_to_all x1, starting transfers between devices, local(): lax.all_to_all(copies, 'tm', 0, 0, tiled=True)  4.54 us
    unnamed x10, local copies, waits for them, and re-layouts  2.7 us
    ppermute x1, waiting for transfers between devices, local(): held = keep + lax.ppermute(send, 'core', [(0, 1), (1, 0)])  1.54 us
  transfers between devices with their start and end apart: 6, of which 4 were waited for; matrix products, arithmetic and copies ran while one was open for 0% of the time, Pallas kernels for 5%

profile of v4, /device:TPU:9, one launch (start us, length us, event | category | flops | bytes accessed | tf_op | source)
XLA Modules:
  0.0 67.8 jit_solution(8667573505487001232)
XLA Ops:
  0.6 0.0 copy-start.4
  0.6 0.1 pad_add_fusion.place_ref
  0.7 0.6 copy-done.4
  1.3 1.0 %copy-done = f32[2,2,8,4096]{3,2,1,0:T(8,128)S(1)} copy-done((f32[2,2,8,4096]{3,2,1,0:T(8,128)S(1)}, f32[2,2,8,4096]{3,2,1,0:T(8,128)}, u32[]{:S(2)}) %copy-start) | copy-done | bytes 524312
  2.4 1.0 %copy-done.2 = f32[2,2,8,4096]{3,2,1,0:T(8,128)S(1)} copy-done((f32[2,2,8,4096]{3,2,1,0:T(8,128)S(1)}, f32[2,2,8,4096]{3,2,1,0:T(8,128)}, u32[]{:S(2)}) %copy-start.2) | copy-done | bytes 524312
  3.4 6.6 %shard_map.53 = (f32[8,2,8,8,128]{4,3,2,1,0:T(8,128)S(1)}, f32[8,2,8,8,128]{4,3,2,1,0:T(8,128)S(1)}) custom-call(s32[3]{0:T(128)S(1)} %pad_add_fusion.place_ref, f32[1408]{0:T(1024)S(1)} %copy-done.4, f32[2,2,8,4096]{3,2,1,0:T(8,128)S(1)} %copy-done, f32[2,2,8,4096]{3,2,1,0:T(8,128)S(1)} %copy-done.2), custom_call_target="tpu_custom_call" | custom-call | flops 100000000 | bytes 1048576 | tf_op jit(solution)/shard_map/pallas_call | solution.py:194
  10.0 0.7 %collective-permute-start.4 = (f32[8,2,8,8,128]{4,3,2,1,0:T(8,128)S(1)}, f32[8,2,8,8,128]{4,3,2,1,0:T(8,128)S(1)}, u32[]{:S(2)}, u32[]{:S(2)}) collective-permute-start(f32[8,2,8,8,128]{4,3,2,1,0:T(8,128)S(1)} %get-tuple-element.19), channel_id=1, source_target_pairs={{0,1},{1,0},{2,3},{3,2},{4,5},{5,4},{6,7},{7,6},{8,9},{9,8},{10,11... | collective-permute-start | bytes 1572872 | tf_op jit(solution)/shard_map/ppermute | solution.py:425
  10.8 1.5 %collective-permute-done.4 = f32[8,2,8,8,128]{4,3,2,1,0:T(8,128)S(1)} collective-permute-done((f32[8,2,8,8,128]{4,3,2,1,0:T(8,128)S(1)}, f32[8,2,8,8,128]{4,3,2,1,0:T(8,128)S(1)}, u32[]{:S(2)}, u32[]{:S(2)}) %collective-permute-start.4) | collective-permute-done | bytes 524320 | tf_op jit(solution)/shard_map/ppermute | solution.py:425
  12.3 0.1 add.7
  12.4 20.1 %all_to_all.10.parts_ref = f32[16,8,8,128]{3,2,1,0:T(8,128)S(1)} all-to-all(f32[16,8,8,128]{3,2,1,0:T(8,128)S(1)} %bitcast.8), channel_id=1, replica_groups=mesh['tm'=8,'pair'=2,'core'=2] {'tm','pair'}, dimensions={0} | all-to-all | bytes 1048576 | tf_op jit(solution)/shard_map/all_to_all | solution.py:427
  32.5 0.7 %shard_map.54 = f32[8,8,8,128]{3,2,1,0:T(8,128)} custom-call(f32[16,8,8,128]{3,2,1,0:T(8,128)S(1)} %all_to_all.10.parts_ref), custom_call_target="tpu_custom_call" | custom-call | flops 1000000 | bytes 1048576 | tf_op jit(solution)/shard_map/pallas_call | solution.py:194
  33.2 4.5 %all-to-all-start.1 = ((f32[8,8,8,128]{3,2,1,0:T(8,128)}), f32[8,8,8,128]{3,2,1,0:T(8,128)S(1)}, u32[]{:S(2)}, u32[]{:S(2)}) async-start(f32[8,8,8,128]{3,2,1,0:T(8,128)} %shard_map.54), calls=%async_computation.1 | async-start | bytes 524288 | tf_op jit(solution)/shard_map/all_to_all | solution.py:429
  37.8 0.5 shard_map.50
  38.3 4.1 %collective-permute-start = (f32[8,4096]{1,0:T(8,128)S(1)}, f32[8,4096]{1,0:T(8,128)S(1)}, u32[]{:S(2)}, u32[]{:S(2)}) collective-permute-start(f32[8,4096]{1,0:T(8,128)S(1)} %get-tuple-element.12.up_ref), channel_id=1, source_target_pairs={{0,1},{1,2},{2,3},{4,5},{5,6},{6,7},{8,9},{9,10},{10,11},{12,13},{... | collective-permute-start | bytes 393224 | tf_op jit(solution)/shard_map/ppermute | solution.py:393
  42.4 1.9 %collective-permute-start.1 = (f32[8,4096]{1,0:T(8,128)S(1)}, f32[8,4096]{1,0:T(8,128)S(1)}, u32[]{:S(2)}, u32[]{:S(2)}) collective-permute-start(f32[8,4096]{1,0:T(8,128)S(1)} %get-tuple-element.13.down_ref), channel_id=1, source_target_pairs={{1,0},{2,1},{3,2},{5,4},{6,5},{7,6},{9,8},{10,9},{11,10},{13,12},{... | collective-permute-start | bytes 393224 | tf_op jit(solution)/shard_map/ppermute | solution.py:393
  44.4 4.3 %collective-permute-done.1.below_ref = f32[8,4096]{1,0:T(8,128)S(1)} collective-permute-done((f32[8,4096]{1,0:T(8,128)S(1)}, f32[8,4096]{1,0:T(8,128)S(1)}, u32[]{:S(2)}, u32[]{:S(2)}) %collective-permute-start.1) | collective-permute-done | bytes 131104 | tf_op jit(solution)/shard_map/ppermute | solution.py:393
  48.7 0.8 %shard_map.51 = (f32[2,2,8,4096]{3,2,1,0:T(8,128)S(1)}, f32[8,4096]{1,0:T(8,128)S(1)}, f32[72,8,128]{2,1,0:T(8,128)S(1)}, f32[72,8,128]{2,1,0:T(8,128)S(1)}) custom-call(s32[3]{0:T(128)S(1)} %pad_add_fusion.place_ref, f32[2,2,8,4096]{3,2,1,0:T(8,128)S(1)} %copy-done.1, f32[2,2,8,4096]{3,2,1,0:T(8,128)S(1)} %get-tuple-element.11.first_ref, ...), custom_call_target="tpu_custom_call" | custom-call | flops 1000000 | bytes 1048576 | tf_op jit(solution)/shard_map/pallas_call | solution.py:194
  49.5 3.1 %collective-permute-start.2 = (f32[72,8,128]{2,1,0:T(8,128)S(1)}, f32[72,8,128]{2,1,0:T(8,128)S(1)}, u32[]{:S(2)}, u32[]{:S(2)}) collective-permute-start(f32[72,8,128]{2,1,0:T(8,128)S(1)} %get-tuple-element.16), channel_id=1, source_target_pairs={{0,4},{4,8},{8,12},{12,16},{16,20},{20,24},{24,28},{1,5},{5,9},{9,... | collective-permute-start | bytes 884744 | tf_op jit(solution)/shard_map/ppermute | solution.py:393
  52.6 3.1 %collective-permute-start.3 = (f32[72,8,128]{2,1,0:T(8,128)S(1)}, f32[72,8,128]{2,1,0:T(8,128)S(1)}, u32[]{:S(2)}, u32[]{:S(2)}) collective-permute-start(f32[72,8,128]{2,1,0:T(8,128)S(1)} %get-tuple-element.17), channel_id=1, source_target_pairs={{4,0},{8,4},{12,8},{16,12},{20,16},{24,20},{28,24},{5,1},{9,5},{13... | collective-permute-start | bytes 884744 | tf_op jit(solution)/shard_map/ppermute | solution.py:393
  55.7 7.5 %collective-permute-done.2.forth_ref = f32[72,8,128]{2,1,0:T(8,128)S(1)} collective-permute-done((f32[72,8,128]{2,1,0:T(8,128)S(1)}, f32[72,8,128]{2,1,0:T(8,128)S(1)}, u32[]{:S(2)}, u32[]{:S(2)}) %collective-permute-start.2) | collective-permute-done | bytes 294944 | tf_op jit(solution)/shard_map/ppermute | solution.py:393
  63.2 1.8 %collective-permute-done.3.back_ref = f32[72,8,128]{2,1,0:T(8,128)S(1)} collective-permute-done((f32[72,8,128]{2,1,0:T(8,128)S(1)}, f32[72,8,128]{2,1,0:T(8,128)S(1)}, u32[]{:S(2)}, u32[]{:S(2)}) %collective-permute-start.3) | collective-permute-done | bytes 294944 | tf_op jit(solution)/shard_map/ppermute | solution.py:393
  65.0 1.9 %shard_map.52 = f32[2,2,8,4096]{3,2,1,0:T(8,128)} custom-call(s32[3]{0:T(128)S(1)} %pad_add_fusion.place_ref, f32[2,2,8,4096]{3,2,1,0:T(8,128)S(1)} %copy-done.1, f32[2,2,8,4096]{3,2,1,0:T(8,128)S(1)} %copy-done.3, f32[2,2,8,4096]{3,2,1,0:T(8,128)S(1)} %get-tuple-element.14.swept_ref, f32[8,4096]{1,0:T(8,128)S(1)} %get-tuple-element.15.edge_ref, ...), custom_call_target="tpu_custom_call" | custom-call | flops 1000000 | bytes 1048576 | tf_op jit(solution)/shard_map/pallas_call | solution.py:194
  66.9 0.0 all-to-all-done.1
  66.9 0.8 %broadcast_in_dim.8 = f32[2,2,8,4096]{3,2,1,0:T(8,128)} broadcast(f32[2,8,4096]{2,1,0:T(8,128)S(1)} %bitcast.9), dimensions={0,2,3} | broadcast | bytes 786432 | tf_op jit(solution)/shard_map/broadcast_in_dim | solution.py:438
  (7 shorter events, 0.0 us)
Async XLA Ops:
  0.6 0.7 %copy-start.4 = (f32[1408]{0:T(1024)S(1)}, f32[1408]{0:T(1024)}, u32[]{:S(2)}) copy-start(f32[1408]{0:T(1024)} %constant.18.clone.weights_ref) | copy-start | bytes 16900
  1.3 1.0 %copy-start = (f32[2,2,8,4096]{3,2,1,0:T(8,128)S(1)}, f32[2,2,8,4096]{3,2,1,0:T(8,128)}, u32[]{:S(2)}) copy-start(f32[2,2,8,4096]{3,2,1,0:T(8,128)} %iterate_ref.7) | copy-start | bytes 1572868
  2.4 1.0 %copy-start.2 = (f32[2,2,8,4096]{3,2,1,0:T(8,128)S(1)}, f32[2,2,8,4096]{3,2,1,0:T(8,128)}, u32[]{:S(2)}) copy-start(f32[2,2,8,4096]{3,2,1,0:T(8,128)} %forcing_ref.5) | copy-start | bytes 1572868
  10.0 2.3 %collective-permute-start.4 = (f32[8,2,8,8,128]{4,3,2,1,0:T(8,128)S(1)}, f32[8,2,8,8,128]{4,3,2,1,0:T(8,128)S(1)}, u32[]{:S(2)}, u32[]{:S(2)}) collective-permute-start(f32[8,2,8,8,128]{4,3,2,1,0:T(8,128)S(1)} %get-tuple-element.19), channel_id=1, source_target_pairs={{0,1},{1,0},{2,3},{3,2},{4,5},{5,4},{6,7},{7,6},{8,9},{9,8},{10,11... | collective-permute-start | bytes 1572872 | tf_op jit(solution)/shard_map/ppermute | solution.py:425
  32.5 5.3 %copy-start.1 = (f32[2,2,8,4096]{3,2,1,0:T(8,128)S(1)}, f32[2,2,8,4096]{3,2,1,0:T(8,128)}, u32[]{:S(2)}) copy-start(f32[2,2,8,4096]{3,2,1,0:T(8,128)} %iterate_ref.7) | copy-start | bytes 1572868
  32.5 5.3 %copy-start.3 = (f32[2,2,8,4096]{3,2,1,0:T(8,128)S(1)}, f32[2,2,8,4096]{3,2,1,0:T(8,128)}, u32[]{:S(2)}) copy-start(f32[2,2,8,4096]{3,2,1,0:T(8,128)} %forcing_ref.5) | copy-start | bytes 1572868
  33.2 33.7 %all-to-all-start.1 = ((f32[8,8,8,128]{3,2,1,0:T(8,128)}), f32[8,8,8,128]{3,2,1,0:T(8,128)S(1)}, u32[]{:S(2)}, u32[]{:S(2)}) async-start(f32[8,8,8,128]{3,2,1,0:T(8,128)} %shard_map.54), calls=%async_computation.1 | async-start | bytes 524288 | tf_op jit(solution)/shard_map/all_to_all | solution.py:429
  38.3 6.1 %collective-permute-start = (f32[8,4096]{1,0:T(8,128)S(1)}, f32[8,4096]{1,0:T(8,128)S(1)}, u32[]{:S(2)}, u32[]{:S(2)}) collective-permute-start(f32[8,4096]{1,0:T(8,128)S(1)} %get-tuple-element.12.up_ref), channel_id=1, source_target_pairs={{0,1},{1,2},{2,3},{4,5},{5,6},{6,7},{8,9},{9,10},{10,11},{12,13},{... | collective-permute-start | bytes 393224 | tf_op jit(solution)/shard_map/ppermute | solution.py:393
  42.4 6.3 %collective-permute-start.1 = (f32[8,4096]{1,0:T(8,128)S(1)}, f32[8,4096]{1,0:T(8,128)S(1)}, u32[]{:S(2)}, u32[]{:S(2)}) collective-permute-start(f32[8,4096]{1,0:T(8,128)S(1)} %get-tuple-element.13.down_ref), channel_id=1, source_target_pairs={{1,0},{2,1},{3,2},{5,4},{6,5},{7,6},{9,8},{10,9},{11,10},{13,12},{... | collective-permute-start | bytes 393224 | tf_op jit(solution)/shard_map/ppermute | solution.py:393
  49.5 13.7 %collective-permute-start.2 = (f32[72,8,128]{2,1,0:T(8,128)S(1)}, f32[72,8,128]{2,1,0:T(8,128)S(1)}, u32[]{:S(2)}, u32[]{:S(2)}) collective-permute-start(f32[72,8,128]{2,1,0:T(8,128)S(1)} %get-tuple-element.16), channel_id=1, source_target_pairs={{0,4},{4,8},{8,12},{12,16},{16,20},{20,24},{24,28},{1,5},{5,9},{9,... | collective-permute-start | bytes 884744 | tf_op jit(solution)/shard_map/ppermute | solution.py:393
  52.6 12.4 %collective-permute-start.3 = (f32[72,8,128]{2,1,0:T(8,128)S(1)}, f32[72,8,128]{2,1,0:T(8,128)S(1)}, u32[]{:S(2)}, u32[]{:S(2)}) collective-permute-start(f32[72,8,128]{2,1,0:T(8,128)S(1)} %get-tuple-element.17), channel_id=1, source_target_pairs={{4,0},{8,4},{12,8},{16,12},{20,16},{24,20},{28,24},{5,1},{9,5},{13... | collective-permute-start | bytes 884744 | tf_op jit(solution)/shard_map/ppermute | solution.py:393

commit v5 on v4

--- a/solution.py
+++ b/solution.py
@@ -184,17 +184,17 @@
                     (1, jnp.where(low, swapped_halves(first), second)),
                 ):
                     tile = f * columns + j
-                    ref[tile // tiles, half, tile % tiles] = value
-
-
-def vmem_call(kernel, out_shapes, smem_inputs, inputs, scratch=(), flops=10**6):
+                    ref[half, tile // tiles, tile % tiles] = value
+
+
+def vmem_call(kernel, out_shapes, smem_inputs, inputs, scratch=(), flops=10**6, space=pltpu.VMEM):
     smem = pl.BlockSpec(memory_space=pltpu.SMEM)
     vmem = pl.BlockSpec(memory_space=pltpu.VMEM)
     out_shape = tuple(jax.ShapeDtypeStruct(shape, jnp.float32) for shape in out_shapes)
     return pl.pallas_call(
         kernel,
         out_shape=out_shape,
-        in_specs=[smem] * len(smem_inputs) + [vmem] * len(inputs),
+        in_specs=[smem] * len(smem_inputs) + [pl.BlockSpec(memory_space=space)] * len(inputs),
         out_specs=(vmem,) * len(out_shape),
         scratch_shapes=list(scratch),
         compiler_params=pltpu.CompilerParams(vmem_limit_bytes=32 * 2**20),
@@ -215,7 +215,7 @@
     reach = min(-(-(powers - 1) // depth), slabs - 1)
     middle = max(reach + 1, slabs - 1)
     tiles = 2 * cells // LANES
-    half = (ranks, slabs // 2, tiles // ranks, depth, LANES)
+    half = (slabs // 2, ranks, tiles // ranks, depth, LANES)
     buffer = pltpu.VMEM((cells // NY, (2 * middle + 1) * depth, LANES), jnp.float32)
     packed = pltpu.VMEM((4 * steps, cells // NY, depth, LANES), jnp.float32)
     return vmem_call(
@@ -239,8 +239,18 @@
     )
 
 
-def first_kernel(iterate_ref, forcing_ref, first_ref, up_ref, down_ref):
+def first_kernel(iterate_hbm, forcing_hbm, first_ref, up_ref, down_ref, iterate_ref, forcing_ref, arrived):
     steps, depth, cells = iterate_ref.shape[1:]
+    copies = [
+        pltpu.make_async_copy(source.at[f, n], target.at[f, n], arrived.at[kind, f, n])
+        for kind, (source, target) in enumerate(((iterate_hbm, iterate_ref), (forcing_hbm, forcing_ref)))
+        for f in range(2)
+        for n in range(steps)
+    ]
+    for copy in copies:
+        copy.start()
+    for copy in copies:
+        copy.wait()
     columns = cells // LANES
     lane, sublane = lane_index(depth), sublane_index(depth)
     low = lane < NY
@@ -407,10 +417,24 @@
     ranks, slabs = lax.axis_size("tm"), 2 * lax.axis_size("pair")
     place = jnp.stack([lax.axis_index("tm"), lax.axis_index(("pair", "core")), jnp.zeros((), jnp.int32)]).astype(jnp.int32)
     first, up, down = vmem_call(
-        first_kernel, (iterate.shape, (4 * steps, cells), (4 * steps, cells)), (), (iterate, forcing)
+        first_kernel,
+        (iterate.shape, (4 * steps, cells), (4 * steps, cells)),
+        (),
+        [pltpu.with_memory_space_constraint(array, pltpu.HBM) for array in (iterate, forcing)],
+        (
+            pltpu.VMEM(iterate.shape, jnp.float32),
+            pltpu.VMEM(forcing.shape, jnp.float32),
+            pltpu.SemaphoreType.DMA((2, 2, steps)),
+        ),
+        space=pltpu.HBM,
     )
+    up, down, later_place = lax.optimization_barrier((up, down, place))
     above = shifted(up, ("pair", "core"), 1)
     below = shifted(down, ("pair", "core"), -1)
+    keep, send = coarse_part(later_place, iterate, forcing)
+    send, above, below = lax.optimization_barrier((send, above, below))
+    received = lax.ppermute(send, "core", [(0, 1), (1, 0)])
+
     payload = (2 * columns + 2 * columns // depth, depth, LANES)
     swept, edge, forth, back = vmem_call(
         functools.partial(second_kernel, steps, slabs),
@@ -418,17 +442,29 @@
         (place,),
         (iterate, first, up, down, above, below),
     )
+    pairs, pair = lax.axis_size("pair"), lax.axis_index("pair")
+
+    def half(array, index):
+        return lax.dynamic_index_in_dim(array, index, 0, keepdims=False)
+
+    total = None
+    for mask in range(1, pairs):
+        away = pair ^ mask
+        other = half(keep, away) + half(received, away)
+        if total is None:
+            other, forth, back = lax.optimization_barrier((other, forth, back))
+        term = lax.ppermute(other, "pair", [(i, i ^ mask) for i in range(pairs)])
+        total = term if total is None else total + term
+    own = half(keep, pair) + half(received, pair)
     forth = shifted(forth, "tm", 1)
     back = shifted(back, "tm", -1)
-
-    keep, send = coarse_part(place, iterate, forcing)
-    held = keep + lax.ppermute(send, "core", [(0, 1), (1, 0)])
-    shape = held.shape
-    parts = lax.all_to_all(held.reshape((-1,) + shape[2:]), ("tm", "pair"), 0, 0, tiled=True)
-    (copies,) = vmem_call(sum_kernel, ((ranks,) + shape[2:],), (), (parts,))
+    total = own + total
+    shape = total.shape
+    parts = lax.all_to_all(total, "tm", 0, 0, tiled=True)
+    (copies,) = vmem_call(sum_kernel, (shape,), (), (parts,))
+    copies, forth, back = lax.optimization_barrier((copies, forth, back))
     coarse = lax.all_to_all(copies, "tm", 0, 0, tiled=True).reshape(2, columns, depth, LANES)
     coarse = coarse.transpose(0, 2, 1, 3).reshape(2, depth, cells)
-
     (smoothed,) = vmem_call(
         functools.partial(third_kernel, steps, ranks),
         (iterate.shape,),

time: 68.2 us -> 70.3 us (1.031)
  the two profiles are of different devices: /device:TPU:9 before, /device:TPU:0 now
where the time goes in v5:
time: 70.3 us; the launch traced here: 69.7 us
  starting transfers between devices  26.4 us (38%)
  waiting for transfers between devices  25.3 us (36%)
  Pallas kernels  13.5 us (19%)
  other arithmetic  2.84 us (4%)
  local copies, waits for them, and re-layouts  0.86 us (1%)
  between operations  0.79 us (1%)
    pallas_call x5, Pallas kernels, vmem_call(): pl.pallas_call(kernel, out_shape=out_shape, in_specs=[smem] * len(smem_in...  13.5 us
    ppermute x4, starting transfers between devices, shifted(): lax.ppermute(value, axis, [(i, i + by) for i in range(size) if 0 <= i + b...  8.87 us
    ppermute x4, waiting for transfers between devices, shifted(): lax.ppermute(value, axis, [(i, i + by) for i in range(size) if 0 <= i + b...  7.58 us
    ppermute x1, waiting for transfers between devices, local(): term = lax.ppermute(other, 'pair', [(i, i ^ mask) for i in range(pairs)])  6.61 us
    all_to_all x1, waiting for transfers between devices, local(): lax.all_to_all(copies, 'tm', 0, 0, tiled=True)  6.59 us
    all_to_all x1, starting transfers between devices, local(): lax.all_to_all(copies, 'tm', 0, 0, tiled=True)  6.33 us
    all_to_all x1, starting transfers between devices, local(): parts = lax.all_to_all(total, 'tm', 0, 0, tiled=True)  5.97 us
    all_to_all x1, waiting for transfers between devices, local(): parts = lax.all_to_all(total, 'tm', 0, 0, tiled=True)  3.52 us
  transfers between devices with their start and end apart: 8, of which 5 were waited for; matrix products, arithmetic and copies ran while one was open for 0% of the time, Pallas kernels for 17%

profile of v5, /device:TPU:0, one launch (start us, length us, event | category | flops | bytes accessed | tf_op | source)
XLA Modules:
  0.0 69.7 jit_solution(18084033685078961819)
XLA Ops:
  0.7 1.9 %shard_map.50 = (f32[2,2,8,4096]{3,2,1,0:T(8,128)S(1)}, f32[8,4096]{1,0:T(8,128)S(1)}, f32[8,4096]{1,0:T(8,128)S(1)}) custom-call(f32[2,2,8,4096]{3,2,1,0:T(8,128)} %iterate_ref.5, f32[2,2,8,4096]{3,2,1,0:T(8,128)} %forcing_ref.3), custom_call_target="tpu_custom_call" | custom-call | flops 1000000 | bytes 1048576 | tf_op jit(solution)/shard_map/pallas_call | solution.py:194
  2.6 0.0 copy-start.2
  2.6 0.1 pad_add_fusion.place_ref
  2.7 2.4 %collective-permute-start = (f32[8,4096]{1,0:T(8,128)S(1)}, f32[8,4096]{1,0:T(8,128)S(1)}, u32[]{:S(2)}, u32[]{:S(2)}) collective-permute-start(f32[8,4096]{1,0:T(8,128)S(1)} %get-tuple-element.26.up_ref), channel_id=1, source_target_pairs={{0,1},{1,2},{2,3},{4,5},{5,6},{6,7},{8,9},{9,10},{10,11},{12,13},{... | collective-permute-start | bytes 393224 | tf_op jit(solution)/shard_map/ppermute | solution.py:403
  5.0 1.3 %collective-permute-start.1 = (f32[8,4096]{1,0:T(8,128)S(1)}, f32[8,4096]{1,0:T(8,128)S(1)}, u32[]{:S(2)}, u32[]{:S(2)}) collective-permute-start(f32[8,4096]{1,0:T(8,128)S(1)} %get-tuple-element.27.down_ref), channel_id=1, source_target_pairs={{1,0},{2,1},{3,2},{5,4},{6,5},{7,6},{9,8},{10,9},{11,10},{13,12},{... | collective-permute-start | bytes 393224 | tf_op jit(solution)/shard_map/ppermute | solution.py:403
  6.4 8.1 %shard_map.51 = (f32[2,8,8,8,128]{4,3,2,1,0:T(8,128)S(1)}, f32[2,8,8,8,128]{4,3,2,1,0:T(8,128)}) custom-call(s32[3]{0:T(128)S(1)} %pad_add_fusion.place_ref, f32[1408]{0:T(1024)S(1)} %copy-done.2, f32[2,2,8,4096]{3,2,1,0:T(8,128)S(1)} %copy-done, f32[2,2,8,4096]{3,2,1,0:T(8,128)S(1)} %copy-done.1), custom_call_target="tpu_custom_call" | custom-call | flops 100000000 | bytes 1048576 | tf_op jit(solution)/shard_map/pallas_call | solution.py:194
  14.5 3.2 %collective-permute-start.2 = (f32[2,8,8,8,128]{4,3,2,1,0:T(8,128)}, f32[2,8,8,8,128]{4,3,2,1,0:T(8,128)}, u32[]{:S(2)}, u32[]{:S(2)}) collective-permute-start(f32[2,8,8,8,128]{4,3,2,1,0:T(8,128)} %get-tuple-element.35), channel_id=1, source_target_pairs={{0,1},{1,0},{2,3},{3,2},{4,5},{5,4},{6,7},{7,6},{8,9},{9,8},{10,11... | collective-permute-start | bytes 1572872 | tf_op jit(solution)/shard_map/ppermute | solution.py:436
  17.7 0.8 %shard_map.52 = (f32[2,2,8,4096]{3,2,1,0:T(8,128)S(1)}, f32[8,4096]{1,0:T(8,128)S(1)}, f32[72,8,128]{2,1,0:T(8,128)S(1)}, f32[72,8,128]{2,1,0:T(8,128)S(1)}) custom-call(s32[3]{0:T(128)S(1)} %pad_add_fusion.place_ref, f32[2,2,8,4096]{3,2,1,0:T(8,128)S(1)} %copy-done, f32[2,2,8,4096]{3,2,1,0:T(8,128)S(1)} %get-tuple-element.23.first_ref, ...), custom_call_target="tpu_custom_call" | custom-call | flops 1000000 | bytes 1048576 | tf_op jit(solution)/shard_map/pallas_call | solution.py:194
  18.5 0.0 copy-start.5
  18.6 1.0 %collective-permute-done.2 = f32[2,8,8,8,128]{4,3,2,1,0:T(8,128)} collective-permute-done((f32[2,8,8,8,128]{4,3,2,1,0:T(8,128)}, f32[2,8,8,8,128]{4,3,2,1,0:T(8,128)}, u32[]{:S(2)}, u32[]{:S(2)}) %collective-permute-start.2) | collective-permute-done | bytes 524320 | tf_op jit(solution)/shard_map/ppermute | solution.py:436
  19.6 1.0 %add_bitcast_fusion = f32[8,8,8,128]{3,2,1,0:T(8,128)S(1)} fusion(f32[2,8,8,8,128]{4,3,2,1,0:T(8,128)} %collective-permute-done.2, s32[]{:T(128)S(6)} %select_n.10, f32[2,8,8,8,128]{4,3,2,1,0:T(8,128)S(1)} %get-tuple-element.34), kind=kLoop, calls=%fused_computation.1 | loop fusion | flops 65536 | bytes 786436 | tf_op jit(solution)/shard_map/add | solution.py:453
  20.6 2.1 %collective-permute-start.3 = (f32[8,8,8,128]{3,2,1,0:T(8,128)S(1)}, f32[8,8,8,128]{3,2,1,0:T(8,128)S(1)}, u32[]{:S(2)}, u32[]{:S(2)}) collective-permute-start(f32[8,8,8,128]{3,2,1,0:T(8,128)S(1)} %add_bitcast_fusion), channel_id=1, source_target_pairs={{0,2},{2,0},{1,3},{3,1},{4,6},{6,4},{5,7},{7,5},{8,10},{10,8},{9,1... | collective-permute-start | bytes 786440 | tf_op jit(solution)/shard_map/ppermute | solution.py:456
  22.6 6.6 %collective-permute-done.3 = f32[8,8,8,128]{3,2,1,0:T(8,128)S(1)} collective-permute-done((f32[8,8,8,128]{3,2,1,0:T(8,128)S(1)}, f32[8,8,8,128]{3,2,1,0:T(8,128)S(1)}, u32[]{:S(2)}, u32[]{:S(2)}) %collective-permute-start.3) | collective-permute-done | bytes 262176 | tf_op jit(solution)/shard_map/ppermute | solution.py:456
  29.3 1.8 %bitcast_add_fusion = f32[8,8,8,128]{3,2,1,0:T(8,128)} fusion(f32[8,8,8,128]{3,2,1,0:T(8,128)S(1)} %collective-permute-done.3, f32[2,8,8,8,128]{4,3,2,1,0:T(8,128)} %collective-permute-done.2, s32[]{:T(128)S(6)} %select_n.9, f32[2,8,8,8,128]{4,3,2,1,0:T(8,128)S(1)} %get-tuple-element.34), kind=kLoop, calls=%fused_computation | loop fusion | flops 131072 | bytes 1048580 | tf_op jit(solution)/shard_map/add | solution.py:461
  31.0 6.0 %all-to-all-start = ((f32[8,8,8,128]{3,2,1,0:T(8,128)}), f32[8,8,8,128]{3,2,1,0:T(8,128)S(1)}, u32[]{:S(2)}, u32[]{:S(2)}) async-start(f32[8,8,8,128]{3,2,1,0:T(8,128)} %bitcast_add_fusion), calls=%async_computation | async-start | bytes 524288 | tf_op jit(solution)/shard_map/all_to_all | solution.py:463
  37.0 3.9 %collective-permute-start.4 = (f32[72,8,128]{2,1,0:T(8,128)S(1)}, f32[72,8,128]{2,1,0:T(8,128)S(1)}, u32[]{:S(2)}, u32[]{:S(2)}) collective-permute-start(f32[72,8,128]{2,1,0:T(8,128)S(1)} %copy-done.6), channel_id=1, source_target_pairs={{0,4},{4,8},{8,12},{12,16},{16,20},{20,24},{24,28},{1,5},{5,9},{9,... | collective-permute-start | bytes 884744 | tf_op jit(solution)/shard_map/ppermute | solution.py:403
  40.9 1.3 %collective-permute-start.5 = (f32[72,8,128]{2,1,0:T(8,128)S(1)}, f32[72,8,128]{2,1,0:T(8,128)S(1)}, u32[]{:S(2)}, u32[]{:S(2)}) collective-permute-start(f32[72,8,128]{2,1,0:T(8,128)S(1)} %copy-done.4), channel_id=1, source_target_pairs={{4,0},{8,4},{12,8},{16,12},{20,16},{24,20},{28,24},{5,1},{9,5},{13... | collective-permute-start | bytes 884744 | tf_op jit(solution)/shard_map/ppermute | solution.py:403
  42.2 3.5 %all-to-all-done.parts_ref = f32[8,8,8,128]{3,2,1,0:T(8,128)S(1)} async-done(((f32[8,8,8,128]{3,2,1,0:T(8,128)}), f32[8,8,8,128]{3,2,1,0:T(8,128)S(1)}, u32[]{:S(2)}, u32[]{:S(2)}) %all-to-all-start) | async-done | bytes 262176 | tf_op jit(solution)/shard_map/all_to_all | solution.py:463
  45.8 0.7 %shard_map.53 = f32[8,8,8,128]{3,2,1,0:T(8,128)} custom-call(f32[8,8,8,128]{3,2,1,0:T(8,128)S(1)} %all-to-all-done.parts_ref), custom_call_target="tpu_custom_call" | custom-call | flops 1000000 | bytes 1048576 | tf_op jit(solution)/shard_map/pallas_call | solution.py:194
  46.5 7.6 %collective-permute-done.4.forth_ref = f32[72,8,128]{2,1,0:T(8,128)S(1)} collective-permute-done((f32[72,8,128]{2,1,0:T(8,128)S(1)}, f32[72,8,128]{2,1,0:T(8,128)S(1)}, u32[]{:S(2)}, u32[]{:S(2)}) %collective-permute-start.4) | collective-permute-done | bytes 294944 | tf_op jit(solution)/shard_map/ppermute | solution.py:403
  54.1 6.3 %all-to-all-start.1 = ((f32[8,8,8,128]{3,2,1,0:T(8,128)}), f32[8,8,8,128]{3,2,1,0:T(8,128)S(1)}, u32[]{:S(2)}, u32[]{:S(2)}) async-start(f32[8,8,8,128]{3,2,1,0:T(8,128)} %shard_map.53), calls=%async_computation.1 | async-start | bytes 524288 | tf_op jit(solution)/shard_map/all_to_all | solution.py:466
  60.4 1.9 %shard_map.54 = f32[2,2,8,4096]{3,2,1,0:T(8,128)} custom-call(s32[3]{0:T(128)S(1)} %pad_add_fusion.place_ref, f32[2,2,8,4096]{3,2,1,0:T(8,128)S(1)} %copy-done, f32[2,2,8,4096]{3,2,1,0:T(8,128)S(1)} %copy-done.1, f32[2,2,8,4096]{3,2,1,0:T(8,128)S(1)} %get-tuple-element.32.swept_ref, f32[8,4096]{1,0:T(8,128)S(1)} %get-tuple-element.33.edge_ref, ...), custom_call_target="tpu_custom_call" | custom-call | flops 1000000 | bytes 1048576 | tf_op jit(solution)/shard_map/pallas_call | solution.py:194
  62.3 6.6 %all-to-all-done.1 = f32[8,8,8,128]{3,2,1,0:T(8,128)S(1)} async-done(((f32[8,8,8,128]{3,2,1,0:T(8,128)}), f32[8,8,8,128]{3,2,1,0:T(8,128)S(1)}, u32[]{:S(2)}, u32[]{:S(2)}) %all-to-all-start.1) | async-done | bytes 262176 | tf_op jit(solution)/shard_map/all_to_all | solution.py:466
  68.9 0.8 %broadcast_in_dim.8 = f32[2,2,8,4096]{3,2,1,0:T(8,128)} broadcast(f32[2,8,4096]{2,1,0:T(8,128)S(1)} %bitcast.11), dimensions={0,2,3} | broadcast | bytes 786432 | tf_op jit(solution)/shard_map/broadcast_in_dim | solution.py:474
  (15 shorter events, 0.0 us)
Async XLA Ops:
  0.6 5.7 %copy-start = (f32[2,2,8,4096]{3,2,1,0:T(8,128)S(1)}, f32[2,2,8,4096]{3,2,1,0:T(8,128)}, u32[]{:S(2)}) copy-start(f32[2,2,8,4096]{3,2,1,0:T(8,128)} %iterate_ref.5) | copy-start | bytes 1572868
  0.7 5.7 %copy-start.1 = (f32[2,2,8,4096]{3,2,1,0:T(8,128)S(1)}, f32[2,2,8,4096]{3,2,1,0:T(8,128)}, u32[]{:S(2)}) copy-start(f32[2,2,8,4096]{3,2,1,0:T(8,128)} %forcing_ref.3) | copy-start | bytes 1572868
  2.6 3.8 %copy-start.2 = (f32[1408]{0:T(1024)S(1)}, f32[1408]{0:T(1024)}, u32[]{:S(2)}) copy-start(f32[1408]{0:T(1024)} %constant.31.clone.weights_ref) | copy-start | bytes 16900
  2.7 11.8 %collective-permute-start = (f32[8,4096]{1,0:T(8,128)S(1)}, f32[8,4096]{1,0:T(8,128)S(1)}, u32[]{:S(2)}, u32[]{:S(2)}) collective-permute-start(f32[8,4096]{1,0:T(8,128)S(1)} %get-tuple-element.26.up_ref), channel_id=1, source_target_pairs={{0,1},{1,2},{2,3},{4,5},{5,6},{6,7},{8,9},{9,10},{10,11},{12,13},{... | collective-permute-start | bytes 393224 | tf_op jit(solution)/shard_map/ppermute | solution.py:403
  5.0 9.4 %collective-permute-start.1 = (f32[8,4096]{1,0:T(8,128)S(1)}, f32[8,4096]{1,0:T(8,128)S(1)}, u32[]{:S(2)}, u32[]{:S(2)}) collective-permute-start(f32[8,4096]{1,0:T(8,128)S(1)} %get-tuple-element.27.down_ref), channel_id=1, source_target_pairs={{1,0},{2,1},{3,2},{5,4},{6,5},{7,6},{9,8},{10,9},{11,10},{13,12},{... | collective-permute-start | bytes 393224 | tf_op jit(solution)/shard_map/ppermute | solution.py:403
  14.5 5.1 %collective-permute-start.2 = (f32[2,8,8,8,128]{4,3,2,1,0:T(8,128)}, f32[2,8,8,8,128]{4,3,2,1,0:T(8,128)}, u32[]{:S(2)}, u32[]{:S(2)}) collective-permute-start(f32[2,8,8,8,128]{4,3,2,1,0:T(8,128)} %get-tuple-element.35), channel_id=1, source_target_pairs={{0,1},{1,0},{2,3},{3,2},{4,5},{5,4},{6,7},{7,6},{8,9},{9,8},{10,11... | collective-permute-start | bytes 1572872 | tf_op jit(solution)/shard_map/ppermute | solution.py:436
  18.5 2.0 %copy-start.3 = (f32[72,8,128]{2,1,0:T(8,128)}, f32[72,8,128]{2,1,0:T(8,128)S(1)}, u32[]{:S(2)}) copy-start(f32[72,8,128]{2,1,0:T(8,128)S(1)} %get-tuple-element.40) | copy-start | bytes 884740
  18.5 2.0 %copy-start.5 = (f32[72,8,128]{2,1,0:T(8,128)}, f32[72,8,128]{2,1,0:T(8,128)S(1)}, u32[]{:S(2)}) copy-start(f32[72,8,128]{2,1,0:T(8,128)S(1)} %get-tuple-element.39) | copy-start | bytes 884740
  20.6 8.7 %collective-permute-start.3 = (f32[8,8,8,128]{3,2,1,0:T(8,128)S(1)}, f32[8,8,8,128]{3,2,1,0:T(8,128)S(1)}, u32[]{:S(2)}, u32[]{:S(2)}) collective-permute-start(f32[8,8,8,128]{3,2,1,0:T(8,128)S(1)} %add_bitcast_fusion), channel_id=1, source_target_pairs={{0,2},{2,0},{1,3},{3,1},{4,6},{6,4},{5,7},{7,5},{8,10},{10,8},{9,1... | collective-permute-start | bytes 786440 | tf_op jit(solution)/shard_map/ppermute | solution.py:456
  29.3 7.7 %copy-start.6 = (f32[72,8,128]{2,1,0:T(8,128)S(1)}, f32[72,8,128]{2,1,0:T(8,128)}, u32[]{:S(2)}) copy-start(f32[72,8,128]{2,1,0:T(8,128)} %copy-done.5) | copy-start | bytes 884740
  31.0 9.9 %copy-start.4 = (f32[72,8,128]{2,1,0:T(8,128)S(1)}, f32[72,8,128]{2,1,0:T(8,128)}, u32[]{:S(2)}) copy-start(f32[72,8,128]{2,1,0:T(8,128)} %copy-done.3) | copy-start | bytes 884740
  31.0 14.7 %all-to-all-start = ((f32[8,8,8,128]{3,2,1,0:T(8,128)}), f32[8,8,8,128]{3,2,1,0:T(8,128)S(1)}, u32[]{:S(2)}, u32[]{:S(2)}) async-start(f32[8,8,8,128]{3,2,1,0:T(8,128)} %bitcast_add_fusion), calls=%async_computation | async-start | bytes 524288 | tf_op jit(solution)/shard_map/all_to_all | solution.py:463
  37.0 17.1 %collective-permute-start.4 = (f32[72,8,128]{2,1,0:T(8,128)S(1)}, f32[72,8,128]{2,1,0:T(8,128)S(1)}, u32[]{:S(2)}, u32[]{:S(2)}) collective-permute-start(f32[72,8,128]{2,1,0:T(8,128)S(1)} %copy-done.6), channel_id=1, source_target_pairs={{0,4},{4,8},{8,12},{12,16},{16,20},{20,24},{24,28},{1,5},{5,9},{9,... | collective-permute-start | bytes 884744 | tf_op jit(solution)/shard_map/ppermute | solution.py:403
  40.9 13.1 %collective-permute-start.5 = (f32[72,8,128]{2,1,0:T(8,128)S(1)}, f32[72,8,128]{2,1,0:T(8,128)S(1)}, u32[]{:S(2)}, u32[]{:S(2)}) collective-permute-start(f32[72,8,128]{2,1,0:T(8,128)S(1)} %copy-done.4), channel_id=1, source_target_pairs={{4,0},{8,4},{12,8},{16,12},{20,16},{24,20},{28,24},{5,1},{9,5},{13... | collective-permute-start | bytes 884744 | tf_op jit(solution)/shard_map/ppermute | solution.py:403
  54.1 14.9 %all-to-all-start.1 = ((f32[8,8,8,128]{3,2,1,0:T(8,128)}), f32[8,8,8,128]{3,2,1,0:T(8,128)S(1)}, u32[]{:S(2)}, u32[]{:S(2)}) async-start(f32[8,8,8,128]{3,2,1,0:T(8,128)} %shard_map.53), calls=%async_computation.1 | async-start | bytes 524288 | tf_op jit(solution)/shard_map/all_to_all | solution.py:466

commit v6 on v4

--- a/solution.py
+++ b/solution.py
@@ -86,7 +86,19 @@
     return terms[0]
 
 
-def coarse_kernel(powers, steps, slabs, middle, place_ref, weights_ref, iterate_ref, forcing_ref, keep_ref, send_ref, even, odd, packed):
+def coarse_kernel(
+    powers, steps, slabs, middle, place_ref, weights_ref, iterate_hbm, forcing_hbm, keep_ref, send_ref, even, odd, packed, iterate_ref, forcing_ref, arrived
+):
+    copies = {
+        (kind, f, n): pltpu.make_async_copy(source.at[f, n], target.at[f, n], arrived.at[kind, f, n])
+        for kind, (source, target) in enumerate(((iterate_hbm, iterate_ref), (forcing_hbm, forcing_ref)))
+        for n in range(steps)
+        for f in range(2)
+    }
+    for copy in copies.values():
+        copy.start()
+    even[...] = jnp.zeros_like(even)
+    odd[...] = jnp.zeros_like(odd)
     depth, cells = iterate_ref.shape[2:]
     columns = cells // LANES
     rows = cells // NY
@@ -101,9 +113,11 @@
         at = slab + away
         return jnp.where((at >= 0) & (at < slabs), 1.0, 0.0).astype(jnp.float32)
 
-    for j in range(columns):
-        for kind, ref in enumerate((iterate_ref, forcing_ref)):
-            for n in range(steps):
+    for kind, ref in enumerate((iterate_ref, forcing_ref)):
+        for n in range(steps):
+            copies[kind, 0, n].wait()
+            copies[kind, 1, n].wait()
+            for j in range(columns):
                 state, adjoint = ref[0, n, :, column(j)], ref[1, n, :, column(j)]
                 state_turned, adjoint_turned = swapped_halves(state), swapped_halves(adjoint)
                 k = 2 * (kind * steps + n)
@@ -147,8 +161,6 @@
                 target[i, pl.ds(start, depth), :] = value
             before, now = now, later
 
-    even[...] = jnp.zeros_like(even)
-    odd[...] = jnp.zeros_like(odd)
     factors = weights(powers - 1)
     for i in range(rows):
         even[i, pl.ds(middle * depth, depth), :] = injected(factors, i)
@@ -184,20 +196,20 @@
                     (1, jnp.where(low, swapped_halves(first), second)),
                 ):
                     tile = f * columns + j
-                    ref[tile // tiles, half, tile % tiles] = value
-
-
-def vmem_call(kernel, out_shapes, smem_inputs, inputs, scratch=(), flops=10**6):
+                    ref[half, tile // tiles, tile % tiles] = value
+
+
+def vmem_call(kernel, out_shapes, smem_inputs, inputs, scratch=(), flops=10**6, space=pltpu.VMEM, limit=6):
     smem = pl.BlockSpec(memory_space=pltpu.SMEM)
     vmem = pl.BlockSpec(memory_space=pltpu.VMEM)
     out_shape = tuple(jax.ShapeDtypeStruct(shape, jnp.float32) for shape in out_shapes)
     return pl.pallas_call(
         kernel,
         out_shape=out_shape,
-        in_specs=[smem] * len(smem_inputs) + [vmem] * len(inputs),
+        in_specs=[smem] * len(smem_inputs) + [pl.BlockSpec(memory_space=space)] * len(inputs),
         out_specs=(vmem,) * len(out_shape),
         scratch_shapes=list(scratch),
-        compiler_params=pltpu.CompilerParams(vmem_limit_bytes=32 * 2**20),
+        compiler_params=pltpu.CompilerParams(vmem_limit_bytes=limit * 2**20),
         cost_estimate=pl.CostEstimate(flops=flops, bytes_accessed=2**20, transcendentals=0),
     )(*smem_inputs, *inputs)
 
@@ -215,16 +227,25 @@
     reach = min(-(-(powers - 1) // depth), slabs - 1)
     middle = max(reach + 1, slabs - 1)
     tiles = 2 * cells // LANES
-    half = (ranks, slabs // 2, tiles // ranks, depth, LANES)
+    half = (slabs // 2, ranks, tiles // ranks, depth, LANES)
     buffer = pltpu.VMEM((cells // NY, (2 * middle + 1) * depth, LANES), jnp.float32)
     packed = pltpu.VMEM((4 * steps, cells // NY, depth, LANES), jnp.float32)
     return vmem_call(
         functools.partial(coarse_kernel, powers, steps, slabs, middle),
         (half, half),
         (place, jnp.asarray(weights.reshape(-1))),
-        (iterate, forcing),
-        (buffer, buffer, packed),
+        [pltpu.with_memory_space_constraint(array, pltpu.HBM) for array in (iterate, forcing)],
+        (
+            buffer,
+            buffer,
+            packed,
+            pltpu.VMEM(iterate.shape, jnp.float32),
+            pltpu.VMEM(forcing.shape, jnp.float32),
+            pltpu.SemaphoreType.DMA((2, 2, steps)),
+        ),
         flops=10**8,
+        space=pltpu.HBM,
+        limit=12,
     )
 
 
@@ -406,11 +427,31 @@
     columns = cells // LANES
     ranks, slabs = lax.axis_size("tm"), 2 * lax.axis_size("pair")
     place = jnp.stack([lax.axis_index("tm"), lax.axis_index(("pair", "core")), jnp.zeros((), jnp.int32)]).astype(jnp.int32)
+    keep, send = coarse_part(place, iterate, forcing)
+    received = lax.ppermute(send, "core", [(0, 1), (1, 0)])
+
+    keep, iterate_after, forcing_after = lax.optimization_barrier((keep, iterate, forcing))
     first, up, down = vmem_call(
-        first_kernel, (iterate.shape, (4 * steps, cells), (4 * steps, cells)), (), (iterate, forcing)
+        first_kernel, (iterate.shape, (4 * steps, cells), (4 * steps, cells)), (), (iterate_after, forcing_after)
     )
-    above = shifted(up, ("pair", "core"), 1)
-    below = shifted(down, ("pair", "core"), -1)
+    pairs, pair = lax.axis_size("pair"), lax.axis_index("pair")
+
+    def half(array, index):
+        return lax.dynamic_index_in_dim(array, index, 0, keepdims=False)
+
+    total = None
+    for mask in range(1, pairs):
+        away = pair ^ mask
+        other = half(keep, away) + half(received, away)
+        if total is None:
+            other, up, down = lax.optimization_barrier((other, up, down))
+            above = shifted(up, ("pair", "core"), 1)
+            below = shifted(down, ("pair", "core"), -1)
+        term = lax.ppermute(other, "pair", [(i, i ^ mask) for i in range(pairs)])
+        total = term if total is None else total + term
+    own = half(keep, pair) + half(received, pair)
+    total = own + total
+    total, above, below = lax.optimization_barrier((total, above, below))
     payload = (2 * columns + 2 * columns // depth, depth, LANES)
     swept, edge, forth, back = vmem_call(
         functools.partial(second_kernel, steps, slabs),
@@ -418,17 +459,14 @@
         (place,),
         (iterate, first, up, down, above, below),
     )
+    shape = total.shape
+    parts = lax.all_to_all(total, "tm", 0, 0, tiled=True)
+    (copies,) = vmem_call(sum_kernel, (shape,), (), (parts,))
+    copies, _, _ = lax.optimization_barrier((copies, forth, back))
     forth = shifted(forth, "tm", 1)
     back = shifted(back, "tm", -1)
-
-    keep, send = coarse_part(place, iterate, forcing)
-    held = keep + lax.ppermute(send, "core", [(0, 1), (1, 0)])
-    shape = held.shape
-    parts = lax.all_to_all(held.reshape((-1,) + shape[2:]), ("tm", "pair"), 0, 0, tiled=True)
-    (copies,) = vmem_call(sum_kernel, ((ranks,) + shape[2:],), (), (parts,))
     coarse = lax.all_to_all(copies, "tm", 0, 0, tiled=True).reshape(2, columns, depth, LANES)
     coarse = coarse.transpose(0, 2, 1, 3).reshape(2, depth, cells)
-
     (smoothed,) = vmem_call(
         functools.partial(third_kernel, steps, ranks),
         (iterate.shape,),

time: 68.2 us -> 65 us (0.953)
  the two profiles are of different devices: /device:TPU:9 before, /device:TPU:16 now
where the time goes in v6:
time: 65 us; the launch traced here: 64.5 us
  waiting for transfers between devices  23.9 us (37%)
  starting transfers between devices  23.2 us (36%)
  Pallas kernels  11.7 us (18%)
  other arithmetic  2.75 us (4%)
  local copies, waits for them, and re-layouts  2.16 us (3%)
  between operations  0.76 us (1%)
    ppermute x4, waiting for transfers between devices, shifted(): lax.ppermute(value, axis, [(i, i + by) for i in range(size) if 0 <= i + b...  12.7 us
    pallas_call x5, Pallas kernels, vmem_call(): pl.pallas_call(kernel, out_shape=out_shape, in_specs=[smem] * len(smem_in...  11.7 us
    ppermute x4, starting transfers between devices, shifted(): lax.ppermute(value, axis, [(i, i + by) for i in range(size) if 0 <= i + b...  9.78 us
    all_to_all x1, starting transfers between devices, local(): parts = lax.all_to_all(total, 'tm', 0, 0, tiled=True)  6.17 us
    all_to_all x1, waiting for transfers between devices, local(): parts = lax.all_to_all(total, 'tm', 0, 0, tiled=True)  5.87 us
    all_to_all x1, starting transfers between devices, local(): lax.all_to_all(copies, 'tm', 0, 0, tiled=True)  5.67 us
    ppermute x1, waiting for transfers between devices, local(): term = lax.ppermute(other, 'pair', [(i, i ^ mask) for i in range(pairs)])  3.79 us
    add x1, other arithmetic, local(): total = own + total  1.7 us
  transfers between devices with their start and end apart: 8, of which 5 were waited for; matrix products, arithmetic and copies ran while one was open for 3% of the time, Pallas kernels for 5%

profile of v6, /device:TPU:16, one launch (start us, length us, event | category | flops | bytes accessed | tf_op | source)
XLA Modules:
  0.0 64.5 jit_solution(10785668661024231008)
XLA Ops:
  0.7 0.1 pad_add_fusion.place_ref
  0.7 0.6 copy-done.2
  1.3 7.7 %shard_map.50 = (f32[2,8,8,8,128]{4,3,2,1,0:T(8,128)S(1)}, f32[2,8,8,8,128]{4,3,2,1,0:T(8,128)S(1)}) custom-call(s32[3]{0:T(128)S(1)} %pad_add_fusion.place_ref, f32[1408]{0:T(1024)S(1)} %copy-done.2, f32[2,2,8,4096]{3,2,1,0:T(8,128)} %iterate_ref.4, f32[2,2,8,4096]{3,2,1,0:T(8,128)} %forcing_ref.2), custom_call_target="tpu_custom_call" | custom-call | flops 100000000 | bytes 1048576 | tf_op jit(solution)/shard_map/pallas_call | solution.py:206
  9.1 0.1 collective-permute-start
  9.2 0.5 shard_map.51
  9.7 1.5 %collective-permute-done = f32[2,8,8,8,128]{4,3,2,1,0:T(8,128)} collective-permute-done((f32[2,8,8,8,128]{4,3,2,1,0:T(8,128)S(1)}, f32[2,8,8,8,128]{4,3,2,1,0:T(8,128)}, u32[]{:S(2)}, u32[]{:S(2)}) %collective-permute-start) | collective-permute-done | bytes 524320 | tf_op jit(solution)/shard_map/ppermute | solution.py:431
  11.2 1.0 %add_bitcast_fusion = f32[8,8,8,128]{3,2,1,0:T(8,128)S(1)} fusion(f32[2,8,8,8,128]{4,3,2,1,0:T(8,128)} %collective-permute-done, s32[]{:T(128)S(6)} %select_n.9, f32[2,8,8,8,128]{4,3,2,1,0:T(8,128)S(1)} %get-tuple-element.25), kind=kLoop, calls=%fused_computation.1 | loop fusion | flops 65536 | bytes 786436 | tf_op jit(solution)/shard_map/add | solution.py:445
  12.2 1.6 %collective-permute-start.1 = (f32[8,8,8,128]{3,2,1,0:T(8,128)S(1)}, f32[8,8,8,128]{3,2,1,0:T(8,128)S(1)}, u32[]{:S(2)}, u32[]{:S(2)}) collective-permute-start(f32[8,8,8,128]{3,2,1,0:T(8,128)S(1)} %add_bitcast_fusion), channel_id=1, source_target_pairs={{0,2},{2,0},{1,3},{3,1},{4,6},{6,4},{5,7},{7,5},{8,10},{10,8},{9,1... | collective-permute-start | bytes 786440 | tf_op jit(solution)/shard_map/ppermute | solution.py:450
  13.7 1.8 %collective-permute-start.2 = (f32[8,4096]{1,0:T(8,128)S(1)}, f32[8,4096]{1,0:T(8,128)S(1)}, u32[]{:S(2)}, u32[]{:S(2)}) collective-permute-start(f32[8,4096]{1,0:T(8,128)S(1)} %get-tuple-element.29.up_ref), channel_id=1, source_target_pairs={{0,1},{1,2},{2,3},{4,5},{5,6},{6,7},{8,9},{9,10},{10,11},{12,13},{... | collective-permute-start | bytes 393224 | tf_op jit(solution)/shard_map/ppermute | solution.py:414
  15.5 1.3 %collective-permute-start.3 = (f32[8,4096]{1,0:T(8,128)S(1)}, f32[8,4096]{1,0:T(8,128)S(1)}, u32[]{:S(2)}, u32[]{:S(2)}) collective-permute-start(f32[8,4096]{1,0:T(8,128)S(1)} %get-tuple-element.30.down_ref), channel_id=1, source_target_pairs={{1,0},{2,1},{3,2},{5,4},{6,5},{7,6},{9,8},{10,9},{11,10},{13,12},{... | collective-permute-start | bytes 393224 | tf_op jit(solution)/shard_map/ppermute | solution.py:414
  16.8 3.8 %collective-permute-done.1 = f32[8,8,8,128]{3,2,1,0:T(8,128)S(1)} collective-permute-done((f32[8,8,8,128]{3,2,1,0:T(8,128)S(1)}, f32[8,8,8,128]{3,2,1,0:T(8,128)S(1)}, u32[]{:S(2)}, u32[]{:S(2)}) %collective-permute-start.1) | collective-permute-done | bytes 262176 | tf_op jit(solution)/shard_map/ppermute | solution.py:450
  20.6 1.7 %bitcast_add_fusion = f32[8,8,8,128]{3,2,1,0:T(8,128)} fusion(f32[8,8,8,128]{3,2,1,0:T(8,128)S(1)} %collective-permute-done.1, f32[2,8,8,8,128]{4,3,2,1,0:T(8,128)} %collective-permute-done, s32[]{:T(128)S(6)} %select_n.10, f32[2,8,8,8,128]{4,3,2,1,0:T(8,128)S(1)} %get-tuple-element.25), kind=kLoop, calls=%fused_computation | loop fusion | flops 131072 | bytes 1048580 | tf_op jit(solution)/shard_map/add | solution.py:453
  22.3 6.2 %all-to-all-start = ((f32[8,8,8,128]{3,2,1,0:T(8,128)}), f32[8,8,8,128]{3,2,1,0:T(8,128)S(1)}, u32[]{:S(2)}, u32[]{:S(2)}) async-start(f32[8,8,8,128]{3,2,1,0:T(8,128)} %bitcast_add_fusion), calls=%async_computation | async-start | bytes 524288 | tf_op jit(solution)/shard_map/all_to_all | solution.py:463
  28.5 0.8 %shard_map.52 = (f32[2,2,8,4096]{3,2,1,0:T(8,128)S(1)}, f32[8,4096]{1,0:T(8,128)S(1)}, f32[72,8,128]{2,1,0:T(8,128)S(1)}, f32[72,8,128]{2,1,0:T(8,128)S(1)}) custom-call(s32[3]{0:T(128)S(1)} %pad_add_fusion.place_ref, f32[2,2,8,4096]{3,2,1,0:T(8,128)S(1)} %copy-done, f32[2,2,8,4096]{3,2,1,0:T(8,128)S(1)} %get-tuple-element.24.first_ref, ...), custom_call_target="tpu_custom_call" | custom-call | flops 1000000 | bytes 1048576 | tf_op jit(solution)/shard_map/pallas_call | solution.py:206
  29.3 0.7 %copy-done.3 = f32[72,8,128]{2,1,0:T(8,128)} copy-done((f32[72,8,128]{2,1,0:T(8,128)}, f32[72,8,128]{2,1,0:T(8,128)S(1)}, u32[]{:S(2)}) %copy-start.3) | copy-done | bytes 294936
  30.0 5.9 %all-to-all-done.parts_ref = f32[8,8,8,128]{3,2,1,0:T(8,128)S(1)} async-done(((f32[8,8,8,128]{3,2,1,0:T(8,128)}), f32[8,8,8,128]{3,2,1,0:T(8,128)S(1)}, u32[]{:S(2)}, u32[]{:S(2)}) %all-to-all-start) | async-done | bytes 262176 | tf_op jit(solution)/shard_map/all_to_all | solution.py:463
  35.9 0.7 %shard_map.54 = f32[8,8,8,128]{3,2,1,0:T(8,128)} custom-call(f32[8,8,8,128]{3,2,1,0:T(8,128)S(1)} %all-to-all-done.parts_ref), custom_call_target="tpu_custom_call" | custom-call | flops 1000000 | bytes 1048576 | tf_op jit(solution)/shard_map/pallas_call | solution.py:206
  36.6 5.7 %all-to-all-start.1 = ((f32[8,8,8,128]{3,2,1,0:T(8,128)}), f32[8,8,8,128]{3,2,1,0:T(8,128)S(1)}, u32[]{:S(2)}, u32[]{:S(2)}) async-start(f32[8,8,8,128]{3,2,1,0:T(8,128)} %shard_map.54), calls=%async_computation.1 | async-start | bytes 524288 | tf_op jit(solution)/shard_map/all_to_all | solution.py:468
  42.3 3.4 %collective-permute-start.4 = (f32[72,8,128]{2,1,0:T(8,128)S(1)}, f32[72,8,128]{2,1,0:T(8,128)S(1)}, u32[]{:S(2)}, u32[]{:S(2)}) collective-permute-start(f32[72,8,128]{2,1,0:T(8,128)S(1)} %copy-done.4), channel_id=1, source_target_pairs={{0,4},{4,8},{8,12},{12,16},{16,20},{20,24},{24,28},{1,5},{5,9},{9,... | collective-permute-start | bytes 884744 | tf_op jit(solution)/shard_map/ppermute | solution.py:414
  45.6 3.4 %collective-permute-start.5 = (f32[72,8,128]{2,1,0:T(8,128)S(1)}, f32[72,8,128]{2,1,0:T(8,128)S(1)}, u32[]{:S(2)}, u32[]{:S(2)}) collective-permute-start(f32[72,8,128]{2,1,0:T(8,128)S(1)} %get-tuple-element.37), channel_id=1, source_target_pairs={{4,0},{8,4},{12,8},{16,12},{20,16},{24,20},{28,24},{5,1},{9,5},{13... | collective-permute-start | bytes 884744 | tf_op jit(solution)/shard_map/ppermute | solution.py:414
  49.0 9.3 %collective-permute-done.4.forth_ref = f32[72,8,128]{2,1,0:T(8,128)S(1)} collective-permute-done((f32[72,8,128]{2,1,0:T(8,128)S(1)}, f32[72,8,128]{2,1,0:T(8,128)S(1)}, u32[]{:S(2)}, u32[]{:S(2)}) %collective-permute-start.4) | collective-permute-done | bytes 294944 | tf_op jit(solution)/shard_map/ppermute | solution.py:414
  58.3 3.4 %collective-permute-done.5.back_ref = f32[72,8,128]{2,1,0:T(8,128)S(1)} collective-permute-done((f32[72,8,128]{2,1,0:T(8,128)S(1)}, f32[72,8,128]{2,1,0:T(8,128)S(1)}, u32[]{:S(2)}, u32[]{:S(2)}) %collective-permute-start.5) | collective-permute-done | bytes 294944 | tf_op jit(solution)/shard_map/ppermute | solution.py:414
  61.8 1.9 %shard_map.53 = f32[2,2,8,4096]{3,2,1,0:T(8,128)} custom-call(s32[3]{0:T(128)S(1)} %pad_add_fusion.place_ref, f32[2,2,8,4096]{3,2,1,0:T(8,128)S(1)} %copy-done, f32[2,2,8,4096]{3,2,1,0:T(8,128)S(1)} %copy-done.1, f32[2,2,8,4096]{3,2,1,0:T(8,128)S(1)} %get-tuple-element.34.swept_ref, f32[8,4096]{1,0:T(8,128)S(1)} %get-tuple-element.35.edge_ref, ...), custom_call_target="tpu_custom_call" | custom-call | flops 1000000 | bytes 1048576 | tf_op jit(solution)/shard_map/pallas_call | solution.py:206
  63.7 0.8 %broadcast_in_dim.8 = f32[2,2,8,4096]{3,2,1,0:T(8,128)} broadcast(f32[2,8,4096]{2,1,0:T(8,128)S(1)} %bitcast.11), dimensions={0,2,3} | broadcast | bytes 786432 | tf_op jit(solution)/shard_map/broadcast_in_dim | solution.py:476
  (11 shorter events, 0.0 us)
Async XLA Ops:
  0.6 0.7 %copy-start.2 = (f32[1408]{0:T(1024)S(1)}, f32[1408]{0:T(1024)}, u32[]{:S(2)}) copy-start(f32[1408]{0:T(1024)} %constant.31.clone.weights_ref) | copy-start | bytes 16900
  1.3 7.8 %copy-start = (f32[2,2,8,4096]{3,2,1,0:T(8,128)S(1)}, f32[2,2,8,4096]{3,2,1,0:T(8,128)}, u32[]{:S(2)}) copy-start(f32[2,2,8,4096]{3,2,1,0:T(8,128)} %iterate_ref.4) | copy-start | bytes 1572868
  1.3 7.9 %copy-start.1 = (f32[2,2,8,4096]{3,2,1,0:T(8,128)S(1)}, f32[2,2,8,4096]{3,2,1,0:T(8,128)}, u32[]{:S(2)}) copy-start(f32[2,2,8,4096]{3,2,1,0:T(8,128)} %forcing_ref.2) | copy-start | bytes 1572868
  9.1 2.1 %collective-permute-start = (f32[2,8,8,8,128]{4,3,2,1,0:T(8,128)S(1)}, f32[2,8,8,8,128]{4,3,2,1,0:T(8,128)}, u32[]{:S(2)}, u32[]{:S(2)}) collective-permute-start(f32[2,8,8,8,128]{4,3,2,1,0:T(8,128)S(1)} %get-tuple-element.26), channel_id=1, source_target_pairs={{0,1},{1,0},{2,3},{3,2},{4,5},{5,4},{6,7},{7,6},{8,9},{9,8},{10,11... | collective-permute-start | bytes 1572872 | tf_op jit(solution)/shard_map/ppermute | solution.py:431
  12.2 8.4 %collective-permute-start.1 = (f32[8,8,8,128]{3,2,1,0:T(8,128)S(1)}, f32[8,8,8,128]{3,2,1,0:T(8,128)S(1)}, u32[]{:S(2)}, u32[]{:S(2)}) collective-permute-start(f32[8,8,8,128]{3,2,1,0:T(8,128)S(1)} %add_bitcast_fusion), channel_id=1, source_target_pairs={{0,2},{2,0},{1,3},{3,1},{4,6},{6,4},{5,7},{7,5},{8,10},{10,8},{9,1... | collective-permute-start | bytes 786440 | tf_op jit(solution)/shard_map/ppermute | solution.py:450
  13.7 8.6 %collective-permute-start.2 = (f32[8,4096]{1,0:T(8,128)S(1)}, f32[8,4096]{1,0:T(8,128)S(1)}, u32[]{:S(2)}, u32[]{:S(2)}) collective-permute-start(f32[8,4096]{1,0:T(8,128)S(1)} %get-tuple-element.29.up_ref), channel_id=1, source_target_pairs={{0,1},{1,2},{2,3},{4,5},{5,6},{6,7},{8,9},{9,10},{10,11},{12,13},{... | collective-permute-start | bytes 393224 | tf_op jit(solution)/shard_map/ppermute | solution.py:414
  15.5 6.8 %collective-permute-start.3 = (f32[8,4096]{1,0:T(8,128)S(1)}, f32[8,4096]{1,0:T(8,128)S(1)}, u32[]{:S(2)}, u32[]{:S(2)}) collective-permute-start(f32[8,4096]{1,0:T(8,128)S(1)} %get-tuple-element.30.down_ref), channel_id=1, source_target_pairs={{1,0},{2,1},{3,2},{5,4},{6,5},{7,6},{9,8},{10,9},{11,10},{13,12},{... | collective-permute-start | bytes 393224 | tf_op jit(solution)/shard_map/ppermute | solution.py:414
  22.3 13.6 %all-to-all-start = ((f32[8,8,8,128]{3,2,1,0:T(8,128)}), f32[8,8,8,128]{3,2,1,0:T(8,128)S(1)}, u32[]{:S(2)}, u32[]{:S(2)}) async-start(f32[8,8,8,128]{3,2,1,0:T(8,128)} %bitcast_add_fusion), calls=%async_computation | async-start | bytes 524288 | tf_op jit(solution)/shard_map/all_to_all | solution.py:463
  29.3 0.7 %copy-start.3 = (f32[72,8,128]{2,1,0:T(8,128)}, f32[72,8,128]{2,1,0:T(8,128)S(1)}, u32[]{:S(2)}) copy-start(f32[72,8,128]{2,1,0:T(8,128)S(1)} %get-tuple-element.36) | copy-start | bytes 884740
  36.6 5.7 %copy-start.4 = (f32[72,8,128]{2,1,0:T(8,128)S(1)}, f32[72,8,128]{2,1,0:T(8,128)}, u32[]{:S(2)}) copy-start(f32[72,8,128]{2,1,0:T(8,128)} %copy-done.3) | copy-start | bytes 884740
  36.6 27.1 %all-to-all-start.1 = ((f32[8,8,8,128]{3,2,1,0:T(8,128)}), f32[8,8,8,128]{3,2,1,0:T(8,128)S(1)}, u32[]{:S(2)}, u32[]{:S(2)}) async-start(f32[8,8,8,128]{3,2,1,0:T(8,128)} %shard_map.54), calls=%async_computation.1 | async-start | bytes 524288 | tf_op jit(solution)/shard_map/all_to_all | solution.py:468
  42.3 16.0 %collective-permute-start.4 = (f32[72,8,128]{2,1,0:T(8,128)S(1)}, f32[72,8,128]{2,1,0:T(8,128)S(1)}, u32[]{:S(2)}, u32[]{:S(2)}) collective-permute-start(f32[72,8,128]{2,1,0:T(8,128)S(1)} %copy-done.4), channel_id=1, source_target_pairs={{0,4},{4,8},{8,12},{12,16},{16,20},{20,24},{24,28},{1,5},{5,9},{9,... | collective-permute-start | bytes 884744 | tf_op jit(solution)/shard_map/ppermute | solution.py:414
  45.6 16.1 %collective-permute-start.5 = (f32[72,8,128]{2,1,0:T(8,128)S(1)}, f32[72,8,128]{2,1,0:T(8,128)S(1)}, u32[]{:S(2)}, u32[]{:S(2)}) collective-permute-start(f32[72,8,128]{2,1,0:T(8,128)S(1)} %get-tuple-element.37), channel_id=1, source_target_pairs={{4,0},{8,4},{12,8},{16,12},{20,16},{24,20},{28,24},{5,1},{9,5},{13... | collective-permute-start | bytes 884744 | tf_op jit(solution)/shard_map/ppermute | solution.py:414

commit v7 on v6

--- a/solution.py
+++ b/solution.py
@@ -87,7 +87,7 @@
 
 
 def coarse_kernel(
-    powers, steps, slabs, middle, place_ref, weights_ref, iterate_hbm, forcing_hbm, keep_ref, send_ref, even, odd, packed, iterate_ref, forcing_ref, arrived
+    powers, steps, slabs, middle, place_ref, weights_hbm, iterate_hbm, forcing_hbm, keep_ref, send_ref, even, odd, packed, iterate_ref, forcing_ref, weights_ref, arrived, weighed
 ):
     copies = {
         (kind, f, n): pltpu.make_async_copy(source.at[f, n], target.at[f, n], arrived.at[kind, f, n])
@@ -95,8 +95,10 @@
         for n in range(steps)
         for f in range(2)
     }
+    weighing = pltpu.make_async_copy(weights_hbm.at[place_ref[0]], weights_ref, weighed)
     for copy in copies.values():
         copy.start()
+    weighing.start()
     even[...] = jnp.zeros_like(even)
     odd[...] = jnp.zeros_like(odd)
     depth, cells = iterate_ref.shape[2:]
@@ -104,7 +106,6 @@
     rows = cells // NY
     inputs = 2 * steps
     slab, shift = place_ref[1], place_ref[2]
-    base = place_ref[0] * (powers * 4 * inputs)
     lane = lane_index(depth)
     low = lane < NY
     zero = jnp.zeros((depth, LANES), jnp.float32)
@@ -127,9 +128,8 @@
                 packed[k + 1, 2 * j + 1] = jnp.where(low, adjoint_turned, state)
 
     def weights(power):
-        first = base + power * 4 * inputs
         return [
-            jnp.where(low, weights_ref[first + 2 * k], weights_ref[first + 2 * k + 1]) for k in range(2 * inputs)
+            jnp.broadcast_to(weights_ref[pl.ds(power * 2 * inputs + k, 1), :], (depth, LANES)) for k in range(2 * inputs)
         ]
 
     def injected(factors, i):
@@ -161,6 +161,7 @@
                 target[i, pl.ds(start, depth), :] = value
             before, now = now, later
 
+    weighing.wait()
     factors = weights(powers - 1)
     for i in range(rows):
         even[i, pl.ds(middle * depth, depth), :] = injected(factors, i)
@@ -183,7 +184,6 @@
             buffers = buffers[::-1]
 
     final = buffers[0]
-    tiles = keep_ref.shape[2]
     bit = lax.rem(slab, 2)
     for half in range(slabs // 2):
         for ref, flag in ((keep_ref, bit), (send_ref, 1 - bit)):
@@ -195,22 +195,21 @@
                     (0, jnp.where(low, first, swapped_halves(second))),
                     (1, jnp.where(low, swapped_halves(first), second)),
                 ):
-                    tile = f * columns + j
-                    ref[half, tile // tiles, tile % tiles] = value
-
-
-def vmem_call(kernel, out_shapes, smem_inputs, inputs, scratch=(), flops=10**6, space=pltpu.VMEM, limit=6):
+                    ref[half, f, j] = value
+
+
+def vmem_call(kernel, out_shapes, smem_inputs, inputs, scratch=(), spaces=None, limit=6, cost=2**20):
     smem = pl.BlockSpec(memory_space=pltpu.SMEM)
     vmem = pl.BlockSpec(memory_space=pltpu.VMEM)
     out_shape = tuple(jax.ShapeDtypeStruct(shape, jnp.float32) for shape in out_shapes)
     return pl.pallas_call(
         kernel,
         out_shape=out_shape,
-        in_specs=[smem] * len(smem_inputs) + [pl.BlockSpec(memory_space=space)] * len(inputs),
+        in_specs=[smem] * len(smem_inputs) + [pl.BlockSpec(memory_space=space) for space in spaces or [pltpu.VMEM] * len(inputs)],
         out_specs=(vmem,) * len(out_shape),
         scratch_shapes=list(scratch),
         compiler_params=pltpu.CompilerParams(vmem_limit_bytes=limit * 2**20),
-        cost_estimate=pl.CostEstimate(flops=flops, bytes_accessed=2**20, transcendentals=0),
+        cost_estimate=pl.CostEstimate(flops=10**6, bytes_accessed=cost, transcendentals=0),
     )(*smem_inputs, *inputs)
 
 
@@ -226,26 +225,28 @@
     weights = np.stack([same, other], -2).transpose(1, 3, 0, 2, 4, 5).astype(np.float32)
     reach = min(-(-(powers - 1) // depth), slabs - 1)
     middle = max(reach + 1, slabs - 1)
-    tiles = 2 * cells // LANES
-    half = (slabs // 2, ranks, tiles // ranks, depth, LANES)
+    weights = np.repeat(weights.reshape(ranks, -1, 2), NY, -1)
+    half = (slabs // 2, 2, cells // LANES, depth, LANES)
     buffer = pltpu.VMEM((cells // NY, (2 * middle + 1) * depth, LANES), jnp.float32)
     packed = pltpu.VMEM((4 * steps, cells // NY, depth, LANES), jnp.float32)
     return vmem_call(
         functools.partial(coarse_kernel, powers, steps, slabs, middle),
         (half, half),
-        (place, jnp.asarray(weights.reshape(-1))),
-        [pltpu.with_memory_space_constraint(array, pltpu.HBM) for array in (iterate, forcing)],
+        (place,),
+        [pltpu.with_memory_space_constraint(array, pltpu.HBM) for array in (jnp.asarray(weights), iterate, forcing)],
         (
             buffer,
             buffer,
             packed,
             pltpu.VMEM(iterate.shape, jnp.float32),
             pltpu.VMEM(forcing.shape, jnp.float32),
+            pltpu.VMEM(weights.shape[1:], jnp.float32),
             pltpu.SemaphoreType.DMA((2, 2, steps)),
+            pltpu.SemaphoreType.DMA,
         ),
-        flops=10**8,
-        space=pltpu.HBM,
+        spaces=(pltpu.HBM,) * 3,
         limit=12,
+        cost=24 * 2**20,
     )
 
 
@@ -409,17 +410,36 @@
         now, pairs_before = later, pairs
 
 
+def swapped(value, axis, mask):
+    return lax.ppermute(value, axis, [(i, i ^ mask) for i in range(lax.axis_size(axis))])
+
+
 def shifted(value, axis, by):
     size = lax.axis_size(axis)
     return lax.ppermute(value, axis, [(i, i + by) for i in range(size) if 0 <= i + by < size])
 
 
-def sum_kernel(parts_ref, copies_ref):
-    tiles = copies_ref.shape[1]
-    for tile in range(tiles):
-        total = tree_sum([parts_ref[k, tile] for k in range(parts_ref.shape[0])])
-        for k in range(copies_ref.shape[0]):
-            copies_ref[k, tile] = total
+def add_kernel(place_ref, keep_ref, received_any, other_ref, own_ref, received_ref, arrived):
+    pair = lax.div(place_ref[1], 2)
+    parts = [(index, f) for index in (1 - pair, pair) for f in range(2)]
+    copies = [
+        pltpu.make_async_copy(received_any.at[index, f], received_ref.at[k], arrived.at[k])
+        for k, (index, f) in enumerate(parts)
+    ]
+    for copy in copies:
+        copy.start()
+    for k, (index, f) in enumerate(parts):
+        copies[k].wait()
+        (other_ref, own_ref)[k // 2][f] = keep_ref[index, f] + received_ref[k]
+
+
+def last_kernel(place_ref, mine_ref, given_ref, out_ref):
+    steps = out_ref.shape[1]
+    field = lax.rem(place_ref[0], 2)
+    for j in range(mine_ref.shape[0]):
+        for n in range(steps):
+            out_ref[field, n, :, column(j)] = mine_ref[j]
+            out_ref[1 - field, n, :, column(j)] = given_ref[j]
 
 
 def local(iterate, forcing):
@@ -434,24 +454,26 @@
     first, up, down = vmem_call(
         first_kernel, (iterate.shape, (4 * steps, cells), (4 * steps, cells)), (), (iterate_after, forcing_after)
     )
-    pairs, pair = lax.axis_size("pair"), lax.axis_index("pair")
-
-    def half(array, index):
+    other, own = vmem_call(
+        add_kernel,
+        (keep.shape[1:], keep.shape[1:]),
+        (place,),
+        (keep, received),
+        (pltpu.VMEM((4,) + keep.shape[2:], jnp.float32), pltpu.SemaphoreType.DMA((4,))),
+        spaces=(pltpu.VMEM, pl.ANY),
+    )
+    other, up, down = lax.optimization_barrier((other, up, down))
+    above = shifted(up, ("pair", "core"), 1)
+    below = shifted(down, ("pair", "core"), -1)
+    term = swapped(other, "pair", 1)
+    field = lax.rem(lax.axis_index("tm"), 2)
+
+    def chosen(array, index):
         return lax.dynamic_index_in_dim(array, index, 0, keepdims=False)
 
-    total = None
-    for mask in range(1, pairs):
-        away = pair ^ mask
-        other = half(keep, away) + half(received, away)
-        if total is None:
-            other, up, down = lax.optimization_barrier((other, up, down))
-            above = shifted(up, ("pair", "core"), 1)
-            below = shifted(down, ("pair", "core"), -1)
-        term = lax.ppermute(other, "pair", [(i, i ^ mask) for i in range(pairs)])
-        total = term if total is None else total + term
-    own = half(keep, pair) + half(received, pair)
-    total = own + total
-    total, above, below = lax.optimization_barrier((total, above, below))
+    half = chosen(own, 1 - field) + chosen(term, 1 - field)
+    half, above, below = lax.optimization_barrier((half, above, below))
+    mine = chosen(own, field) + chosen(term, field) + swapped(half, "tm", 1)
     payload = (2 * columns + 2 * columns // depth, depth, LANES)
     swept, edge, forth, back = vmem_call(
         functools.partial(second_kernel, steps, slabs),
@@ -459,21 +481,23 @@
         (place,),
         (iterate, first, up, down, above, below),
     )
-    shape = total.shape
-    parts = lax.all_to_all(total, "tm", 0, 0, tiled=True)
-    (copies,) = vmem_call(sum_kernel, (shape,), (), (parts,))
-    copies, _, _ = lax.optimization_barrier((copies, forth, back))
+    mine, _, _ = lax.optimization_barrier((mine, forth, back))
+    mask = 2
+    while mask < ranks:
+        mine = mine + swapped(mine, "tm", mask)
+        mask *= 2
+    given = swapped(mine, "tm", 1)
+    (coarse,) = vmem_call(last_kernel, (iterate.shape,), (place,), (mine, given))
     forth = shifted(forth, "tm", 1)
     back = shifted(back, "tm", -1)
-    coarse = lax.all_to_all(copies, "tm", 0, 0, tiled=True).reshape(2, columns, depth, LANES)
-    coarse = coarse.transpose(0, 2, 1, 3).reshape(2, depth, cells)
     (smoothed,) = vmem_call(
         functools.partial(third_kernel, steps, ranks),
         (iterate.shape,),
         (place,),
         (iterate, forcing, swept, edge, forth, back),
+        cost=64 * 2**20,
     )
-    return smoothed, jnp.broadcast_to(coarse[:, None], iterate.shape)
+    return smoothed, coarse
 
 
 def solution(mesh):

time: 65 us -> 57.6 us (0.89)
  the two profiles are of different devices: /device:TPU:16 before, /device:TPU:0 now
where the time goes in v7:
time: 57.6 us; the launch traced here: 57.4 us
  waiting for transfers between devices  23.2 us (40%)
  starting transfers between devices  19.5 us (34%)
  Pallas kernels  13.8 us (24%)
  between operations  0.77 us (1%)
    ppermute x5, waiting for transfers between devices, swapped(): lax.ppermute(value, axis, [(i, i ^ mask) for i in range(lax.axis_size(axi...  22.1 us
    pallas_call x6, Pallas kernels, vmem_call(): pl.pallas_call(kernel, out_shape=out_shape, in_specs=[smem] * len(smem_in...  13.8 us
    ppermute x5, starting transfers between devices, swapped(): lax.ppermute(value, axis, [(i, i ^ mask) for i in range(lax.axis_size(axi...  11.2 us
    ppermute x4, starting transfers between devices, shifted(): lax.ppermute(value, axis, [(i, i + by) for i in range(size) if 0 <= i + b...  7.77 us
  transfers between devices with their start and end apart: 10, of which 5 were waited for; matrix products, arithmetic and copies ran while one was open for 0% of the time, Pallas kernels for 6%

profile of v7, /device:TPU:0, one launch (start us, length us, event | category | flops | bytes accessed | tf_op | source)
XLA Modules:
  0.0 57.4 jit_solution(14328546629734486707)
XLA Ops:
  0.6 0.1 pad_add_fusion.place_ref
  0.7 7.8 %shard_map.50 = (f32[2,2,32,8,128]{4,3,2,1,0:T(8,128)S(1)}, f32[2,2,32,8,128]{4,3,2,1,0:T(8,128)S(1)}) custom-call(s32[3]{0:T(128)S(1)} %pad_add_fusion.place_ref, f32[8,88,128]{2,1,0:T(8,128)} %constant.35.clone.weights_hbm, f32[2,2,8,4096]{3,2,1,0:T(8,128)} %iterate_ref.4, f32[2,2,8,4096]{3,2,1,0:T(8,128)} %forcing_ref.2), custom_call_target="tpu_custom_call" | custom-call | flops 1000000 | bytes 25165824 | tf_op jit(solution)/shard_map/pallas_call | solution.py:205
  8.6 0.5 collective-permute-start
  9.1 0.5 shard_map.51
  9.6 1.0 %collective-permute-done.received_any = f32[2,2,32,8,128]{4,3,2,1,0:T(8,128)S(1)} collective-permute-done((f32[2,2,32,8,128]{4,3,2,1,0:T(8,128)S(1)}, f32[2,2,32,8,128]{4,3,2,1,0:T(8,128)S(1)}, u32[]{:S(2)}, u32[]{:S(2)}) %collective-permute-start) | collective-permute-done | bytes 524320 | tf_op jit(solution)/shard_map/ppermute | solution.py:451
  10.6 1.3 %shard_map.52 = (f32[2,32,8,128]{3,2,1,0:T(8,128)S(1)}, f32[2,32,8,128]{3,2,1,0:T(8,128)S(1)}) custom-call(s32[3]{0:T(128)S(1)} %pad_add_fusion.place_ref, f32[2,2,32,8,128]{4,3,2,1,0:T(8,128)S(1)} %get-tuple-element.27.keep_ref, f32[2,2,32,8,128]{4,3,2,1,0:T(8,128)S(1)} %collective-permute-done.received_any), custom_call_target="tpu_custom_call" | custom-call | flops 1000000 | bytes 1048576 | tf_op jit(solution)/shard_map/pallas_call | solution.py:205
  11.9 2.9 %collective-permute-start.1 = (f32[2,32,8,128]{3,2,1,0:T(8,128)S(1)}, f32[2,32,8,128]{3,2,1,0:T(8,128)S(1)}, u32[]{:S(2)}, u32[]{:S(2)}) collective-permute-start(f32[2,32,8,128]{3,2,1,0:T(8,128)S(1)} %get-tuple-element.35), channel_id=1, source_target_pairs={{0,2},{2,0},{1,3},{3,1},{4,6},{6,4},{5,7},{7,5},{8,10},{10,8},{9,1... | collective-permute-start | bytes 786440 | tf_op jit(solution)/shard_map/ppermute | solution.py:414
  14.9 1.8 %collective-permute-start.2 = (f32[8,4096]{1,0:T(8,128)S(1)}, f32[8,4096]{1,0:T(8,128)S(1)}, u32[]{:S(2)}, u32[]{:S(2)}) collective-permute-start(f32[8,4096]{1,0:T(8,128)S(1)} %get-tuple-element.32.up_ref), channel_id=1, source_target_pairs={{0,1},{1,2},{2,3},{4,5},{5,6},{6,7},{8,9},{9,10},{10,11},{12,13},{... | collective-permute-start | bytes 393224 | tf_op jit(solution)/shard_map/ppermute | solution.py:419
  16.6 1.3 %collective-permute-start.3 = (f32[8,4096]{1,0:T(8,128)S(1)}, f32[8,4096]{1,0:T(8,128)S(1)}, u32[]{:S(2)}, u32[]{:S(2)}) collective-permute-start(f32[8,4096]{1,0:T(8,128)S(1)} %get-tuple-element.33.down_ref), channel_id=1, source_target_pairs={{1,0},{2,1},{3,2},{5,4},{6,5},{7,6},{9,8},{10,9},{11,10},{13,12},{... | collective-permute-start | bytes 393224 | tf_op jit(solution)/shard_map/ppermute | solution.py:419
  17.9 3.6 %collective-permute-done.1 = f32[2,32,8,128]{3,2,1,0:T(8,128)S(1)} collective-permute-done((f32[2,32,8,128]{3,2,1,0:T(8,128)S(1)}, f32[2,32,8,128]{3,2,1,0:T(8,128)S(1)}, u32[]{:S(2)}, u32[]{:S(2)}) %collective-permute-start.1) | collective-permute-done | bytes 262176 | tf_op jit(solution)/shard_map/ppermute | solution.py:414
  21.6 0.0 collective-permute-done.2.above_ref
  21.6 0.0 collective-permute-done.3.below_ref
  21.6 1.8 %collective-permute-start.6 = (f32[32,8,128]{2,1,0:T(8,128)S(1)}, f32[32,8,128]{2,1,0:T(8,128)S(1)}, u32[]{:S(2)}, u32[]{:S(2)}) collective-permute-start(f32[32,8,128]{2,1,0:T(8,128)S(1)} %add_bitcast_fusion), channel_id=1, source_target_pairs={{0,4},{4,0},{8,12},{12,8},{16,20},{20,16},{24,28},{28,24},{1,5},{5... | collective-permute-start | bytes 393224 | tf_op jit(solution)/shard_map/ppermute | solution.py:414
  23.4 0.8 %shard_map.53 = (f32[2,2,8,4096]{3,2,1,0:T(8,128)S(1)}, f32[8,4096]{1,0:T(8,128)S(1)}, f32[72,8,128]{2,1,0:T(8,128)S(1)}, f32[72,8,128]{2,1,0:T(8,128)S(1)}) custom-call(s32[3]{0:T(128)S(1)} %pad_add_fusion.place_ref, f32[2,2,8,4096]{3,2,1,0:T(8,128)S(1)} %copy-done, f32[2,2,8,4096]{3,2,1,0:T(8,128)S(1)} %get-tuple-element.26.first_ref, ...), custom_call_target="tpu_custom_call" | custom-call | flops 1000000 | bytes 1048576 | tf_op jit(solution)/shard_map/pallas_call | solution.py:205
  24.2 3.0 %collective-permute-done.6 = f32[32,8,128]{2,1,0:T(8,128)S(1)} collective-permute-done((f32[32,8,128]{2,1,0:T(8,128)S(1)}, f32[32,8,128]{2,1,0:T(8,128)S(1)}, u32[]{:S(2)}, u32[]{:S(2)}) %collective-permute-start.6) | collective-permute-done | bytes 131104 | tf_op jit(solution)/shard_map/ppermute | solution.py:414
  27.2 1.8 %collective-permute-start.7 = (f32[32,8,128]{2,1,0:T(8,128)S(1)}, f32[32,8,128]{2,1,0:T(8,128)S(1)}, u32[]{:S(2)}, u32[]{:S(2)}) collective-permute-start(f32[32,8,128]{2,1,0:T(8,128)S(1)} %bitcast_add_fusion), channel_id=1, source_target_pairs={{0,8},{4,12},{8,0},{12,4},{16,24},{20,28},{24,16},{28,20},{1,9},{5... | collective-permute-start | bytes 393224 | tf_op jit(solution)/shard_map/ppermute | solution.py:414
  29.0 3.4 %collective-permute-start.4 = (f32[72,8,128]{2,1,0:T(8,128)S(1)}, f32[72,8,128]{2,1,0:T(8,128)S(1)}, u32[]{:S(2)}, u32[]{:S(2)}) collective-permute-start(f32[72,8,128]{2,1,0:T(8,128)S(1)} %get-tuple-element.40), channel_id=1, source_target_pairs={{0,4},{4,8},{8,12},{12,16},{16,20},{20,24},{24,28},{1,5},{5,9},{9,... | collective-permute-start | bytes 884744 | tf_op jit(solution)/shard_map/ppermute | solution.py:419
  32.4 1.3 %collective-permute-start.5 = (f32[72,8,128]{2,1,0:T(8,128)S(1)}, f32[72,8,128]{2,1,0:T(8,128)S(1)}, u32[]{:S(2)}, u32[]{:S(2)}) collective-permute-start(f32[72,8,128]{2,1,0:T(8,128)S(1)} %get-tuple-element.41), channel_id=1, source_target_pairs={{4,0},{8,4},{12,8},{16,12},{20,16},{24,20},{28,24},{5,1},{9,5},{13... | collective-permute-start | bytes 884744 | tf_op jit(solution)/shard_map/ppermute | solution.py:419
  33.8 4.7 %collective-permute-start.8 = (f32[32,8,128]{2,1,0:T(8,128)S(1)}, f32[32,8,128]{2,1,0:T(8,128)S(1)}, u32[]{:S(2)}, u32[]{:S(2)}) collective-permute-start(f32[32,8,128]{2,1,0:T(8,128)S(1)} %add.42), channel_id=1, source_target_pairs={{0,16},{4,20},{8,24},{12,28},{16,0},{20,4},{24,8},{28,12},{1,17},{... | collective-permute-start | bytes 393224 | tf_op jit(solution)/shard_map/ppermute | solution.py:414
  38.4 12.6 %collective-permute-done.8 = f32[32,8,128]{2,1,0:T(8,128)S(1)} collective-permute-done((f32[32,8,128]{2,1,0:T(8,128)S(1)}, f32[32,8,128]{2,1,0:T(8,128)S(1)}, u32[]{:S(2)}, u32[]{:S(2)}) %collective-permute-start.8) | collective-permute-done | bytes 131104 | tf_op jit(solution)/shard_map/ppermute | solution.py:414
  51.0 0.1 collective-permute-start.9
  51.1 1.9 %shard_map.54 = f32[2,2,8,4096]{3,2,1,0:T(8,128)} custom-call(s32[3]{0:T(128)S(1)} %pad_add_fusion.place_ref, f32[2,2,8,4096]{3,2,1,0:T(8,128)S(1)} %copy-done, f32[2,2,8,4096]{3,2,1,0:T(8,128)S(1)} %copy-done.1, f32[2,2,8,4096]{3,2,1,0:T(8,128)S(1)} %get-tuple-element.38.swept_ref, f32[8,4096]{1,0:T(8,128)S(1)} %get-tuple-element.39.edge_ref, ...), custom_call_target="tpu_custom_call" | custom-call | flops 1000000 | bytes 67108864 | tf_op jit(solution)/shard_map/pallas_call | solution.py:205
  53.1 3.0 %collective-permute-done.9.given_ref = f32[32,8,128]{2,1,0:T(8,128)S(1)} collective-permute-done((f32[32,8,128]{2,1,0:T(8,128)S(1)}, f32[32,8,128]{2,1,0:T(8,128)S(1)}, u32[]{:S(2)}, u32[]{:S(2)}) %collective-permute-start.9) | collective-permute-done | bytes 131104 | tf_op jit(solution)/shard_map/ppermute | solution.py:414
  56.1 1.4 %shard_map.55 = f32[2,2,8,4096]{3,2,1,0:T(8,128)} custom-call(s32[3]{0:T(128)S(1)} %pad_add_fusion.place_ref, f32[32,8,128]{2,1,0:T(8,128)S(1)} %add.43.mine_ref, f32[32,8,128]{2,1,0:T(8,128)S(1)} %collective-permute-done.9.given_ref), custom_call_target="tpu_custom_call" | custom-call | flops 1000000 | bytes 1048576 | tf_op jit(solution)/shard_map/pallas_call | solution.py:205
  (11 shorter events, 0.1 us)
Async XLA Ops:
  0.7 8.4 %copy-start = (f32[2,2,8,4096]{3,2,1,0:T(8,128)S(1)}, f32[2,2,8,4096]{3,2,1,0:T(8,128)}, u32[]{:S(2)}) copy-start(f32[2,2,8,4096]{3,2,1,0:T(8,128)} %iterate_ref.4) | copy-start | bytes 1572868
  0.7 8.4 %copy-start.1 = (f32[2,2,8,4096]{3,2,1,0:T(8,128)S(1)}, f32[2,2,8,4096]{3,2,1,0:T(8,128)}, u32[]{:S(2)}) copy-start(f32[2,2,8,4096]{3,2,1,0:T(8,128)} %forcing_ref.2) | copy-start | bytes 1572868
  8.6 2.1 %collective-permute-start = (f32[2,2,32,8,128]{4,3,2,1,0:T(8,128)S(1)}, f32[2,2,32,8,128]{4,3,2,1,0:T(8,128)S(1)}, u32[]{:S(2)}, u32[]{:S(2)}) collective-permute-start(f32[2,2,32,8,128]{4,3,2,1,0:T(8,128)S(1)} %get-tuple-element.28), channel_id=1, source_target_pairs={{0,1},{1,0},{2,3},{3,2},{4,5},{5,4},{6,7},{7,6},{8,9},{9,8},{10,11... | collective-permute-start | bytes 1572872 | tf_op jit(solution)/shard_map/ppermute | solution.py:451
  11.9 9.6 %collective-permute-start.1 = (f32[2,32,8,128]{3,2,1,0:T(8,128)S(1)}, f32[2,32,8,128]{3,2,1,0:T(8,128)S(1)}, u32[]{:S(2)}, u32[]{:S(2)}) collective-permute-start(f32[2,32,8,128]{3,2,1,0:T(8,128)S(1)} %get-tuple-element.35), channel_id=1, source_target_pairs={{0,2},{2,0},{1,3},{3,1},{4,6},{6,4},{5,7},{7,5},{8,10},{10,8},{9,1... | collective-permute-start | bytes 786440 | tf_op jit(solution)/shard_map/ppermute | solution.py:414
  14.9 6.7 %collective-permute-start.2 = (f32[8,4096]{1,0:T(8,128)S(1)}, f32[8,4096]{1,0:T(8,128)S(1)}, u32[]{:S(2)}, u32[]{:S(2)}) collective-permute-start(f32[8,4096]{1,0:T(8,128)S(1)} %get-tuple-element.32.up_ref), channel_id=1, source_target_pairs={{0,1},{1,2},{2,3},{4,5},{5,6},{6,7},{8,9},{9,10},{10,11},{12,13},{... | collective-permute-start | bytes 393224 | tf_op jit(solution)/shard_map/ppermute | solution.py:419
  16.6 4.9 %collective-permute-start.3 = (f32[8,4096]{1,0:T(8,128)S(1)}, f32[8,4096]{1,0:T(8,128)S(1)}, u32[]{:S(2)}, u32[]{:S(2)}) collective-permute-start(f32[8,4096]{1,0:T(8,128)S(1)} %get-tuple-element.33.down_ref), channel_id=1, source_target_pairs={{1,0},{2,1},{3,2},{5,4},{6,5},{7,6},{9,8},{10,9},{11,10},{13,12},{... | collective-permute-start | bytes 393224 | tf_op jit(solution)/shard_map/ppermute | solution.py:419
  21.6 5.6 %collective-permute-start.6 = (f32[32,8,128]{2,1,0:T(8,128)S(1)}, f32[32,8,128]{2,1,0:T(8,128)S(1)}, u32[]{:S(2)}, u32[]{:S(2)}) collective-permute-start(f32[32,8,128]{2,1,0:T(8,128)S(1)} %add_bitcast_fusion), channel_id=1, source_target_pairs={{0,4},{4,0},{8,12},{12,8},{16,20},{20,16},{24,28},{28,24},{1,5},{5... | collective-permute-start | bytes 393224 | tf_op jit(solution)/shard_map/ppermute | solution.py:414
  27.2 6.5 %collective-permute-start.7 = (f32[32,8,128]{2,1,0:T(8,128)S(1)}, f32[32,8,128]{2,1,0:T(8,128)S(1)}, u32[]{:S(2)}, u32[]{:S(2)}) collective-permute-start(f32[32,8,128]{2,1,0:T(8,128)S(1)} %bitcast_add_fusion), channel_id=1, source_target_pairs={{0,8},{4,12},{8,0},{12,4},{16,24},{20,28},{24,16},{28,20},{1,9},{5... | collective-permute-start | bytes 393224 | tf_op jit(solution)/shard_map/ppermute | solution.py:414
  29.0 22.1 %collective-permute-start.4 = (f32[72,8,128]{2,1,0:T(8,128)S(1)}, f32[72,8,128]{2,1,0:T(8,128)S(1)}, u32[]{:S(2)}, u32[]{:S(2)}) collective-permute-start(f32[72,8,128]{2,1,0:T(8,128)S(1)} %get-tuple-element.40), channel_id=1, source_target_pairs={{0,4},{4,8},{8,12},{12,16},{16,20},{20,24},{24,28},{1,5},{5,9},{9,... | collective-permute-start | bytes 884744 | tf_op jit(solution)/shard_map/ppermute | solution.py:419
  32.4 18.7 %collective-permute-start.5 = (f32[72,8,128]{2,1,0:T(8,128)S(1)}, f32[72,8,128]{2,1,0:T(8,128)S(1)}, u32[]{:S(2)}, u32[]{:S(2)}) collective-permute-start(f32[72,8,128]{2,1,0:T(8,128)S(1)} %get-tuple-element.41), channel_id=1, source_target_pairs={{4,0},{8,4},{12,8},{16,12},{20,16},{24,20},{28,24},{5,1},{9,5},{13... | collective-permute-start | bytes 884744 | tf_op jit(solution)/shard_map/ppermute | solution.py:419
  33.8 17.2 %collective-permute-start.8 = (f32[32,8,128]{2,1,0:T(8,128)S(1)}, f32[32,8,128]{2,1,0:T(8,128)S(1)}, u32[]{:S(2)}, u32[]{:S(2)}) collective-permute-start(f32[32,8,128]{2,1,0:T(8,128)S(1)} %add.42), channel_id=1, source_target_pairs={{0,16},{4,20},{8,24},{12,28},{16,0},{20,4},{24,8},{28,12},{1,17},{... | collective-permute-start | bytes 393224 | tf_op jit(solution)/shard_map/ppermute | solution.py:414
  51.0 5.0 %collective-permute-start.9 = (f32[32,8,128]{2,1,0:T(8,128)S(1)}, f32[32,8,128]{2,1,0:T(8,128)S(1)}, u32[]{:S(2)}, u32[]{:S(2)}) collective-permute-start(f32[32,8,128]{2,1,0:T(8,128)S(1)} %add.43.mine_ref), channel_id=1, source_target_pairs={{0,4},{4,0},{8,12},{12,8},{16,20},{20,16},{24,28},{28,24},{1,5},{5... | collective-permute-start | bytes 393224 | tf_op jit(solution)/shard_map/ppermute | solution.py:414

commit v8 on v7

--- a/solution.py
+++ b/solution.py
@@ -261,7 +261,7 @@
     )
 
 
-def first_kernel(iterate_ref, forcing_ref, first_ref, up_ref, down_ref):
+def first_kernel(iterate_ref, forcing_ref, first_ref, up_ref, down_ref, forth_ref, back_ref):
     steps, depth, cells = iterate_ref.shape[1:]
     columns = cells // LANES
     lane, sublane = lane_index(depth), sublane_index(depth)
@@ -293,6 +293,10 @@
             )
             for f in range(2):
                 first_ref[f, n, :, column(j)] = values[f]
+                for ref, field, step in ((forth_ref, 0, steps - 1), (back_ref, 1, 0)):
+                    if (f, n) == (field, step):
+                        ref[j] = now[f, n]
+                        ref[columns + j] = values[f]
                 slot = f * steps + n
                 for ref, plane in ((up_ref, depth - 1), (down_ref, 0)):
                     ref[slot : slot + 1, column(j)] = now[f, n][plane : plane + 1]
@@ -302,10 +306,10 @@
 
 
 def second_kernel(
-    steps, slabs, place_ref, iterate_ref, first_ref, up_ref, down_ref, above_ref, below_ref, swept_ref, edge_ref, forth_ref, back_ref
+    steps, slabs, place_ref, first_ref, up_ref, down_ref, above_ref, below_ref, swept_ref, edge_ref, forth_ref, back_ref
 ):
     diffusion, _, _, along, across = level_terms(0)
-    depth, cells = iterate_ref.shape[2:]
+    depth, cells = first_ref.shape[2:]
     columns = cells // LANES
     slab = place_ref[1]
     sublane = sublane_index(depth)
@@ -338,18 +342,17 @@
                 value = value + jnp.where(sublane == 0, add_above[k : k + 1], 0.0)
                 value = value + jnp.where(sublane == depth - 1, add_below[k : k + 1], 0.0)
                 swept_ref[f, n, :, one(j)] = value
-                for ref, field, step in ((forth_ref, 0, steps - 1), (back_ref, 1, 0)):
-                    if (f, n) == (field, step):
-                        ref[j] = iterate_ref[f, n, :, one(j)]
-                        ref[columns + j] = value
-                        block, row = 2 * columns + j // depth, j % depth
-                        ref[block, row : row + 1] = from_above[k : k + 1]
-                        block += columns // depth
-                        ref[block, row : row + 1] = from_below[k : k + 1]
-
-
-def third_kernel(steps, ranks, place_ref, iterate_ref, forcing_ref, swept_ref, edge_ref, forth_ref, back_ref, out_ref):
-    _, _, _, along, across = level_terms(0)
+                for ref, step in ((forth_ref, steps - 1), (back_ref, 0)):
+                    if n == step:
+                        for side, rows in enumerate((from_above, from_below)):
+                            block, row = (2 * side + f) * (columns // depth) + j // depth, j % depth
+                            ref[block, row : row + 1] = rows[k : k + 1]
+
+
+def third_kernel(
+    steps, ranks, place_ref, iterate_ref, forcing_ref, swept_ref, edge_ref, forth_ref, back_ref, forth_edge_ref, back_edge_ref, out_ref
+):
+    diffusion, _, _, along, across = level_terms(0)
     depth, cells = iterate_ref.shape[2:]
     columns = cells // LANES
     rank = place_ref[0]
@@ -372,9 +375,12 @@
                 values[s] = values[s] + gain[s][1] * near[gain[s][0]]
         return values
 
+    def edge_row(ref, j, side, f):
+        block, row = (2 * side + f) * (columns // depth) + j // depth, j % depth
+        return ref[block, row : row + 1]
+
     def edges(j, side):
-        block, row = 2 * columns + side * (columns // depth) + j // depth, j % depth
-        near = {"forth": forth_ref[block, row : row + 1], "back": back_ref[block, row : row + 1]}
+        near = {"forth": edge_row(forth_edge_ref, j, side, 0), "back": edge_row(back_edge_ref, j, side, 1)}
         values = {}
         for s in slots:
             k = side * 2 * steps + s[0] * steps + s[1]
@@ -395,8 +401,14 @@
             above = jnp.where(sublane == 0, over[s], pltpu.roll(now[s], 1, 0))
             below = jnp.where(sublane == depth - 1, under[s], pltpu.roll(now[s], depth - 1, 0))
             around[s] = across_rows + beside(now[s], lane) + (above + below)
-        before = (forth_ref[columns + j] - across * iterate_ref[1, 0, :, column(j)]) * has_before
-        after = (back_ref[columns + j] + across * iterate_ref[0, steps - 1, :, column(j)]) * has_after
+        before = forth_ref[columns + j] - across * iterate_ref[1, 0, :, column(j)]
+        after = back_ref[columns + j] + across * iterate_ref[0, steps - 1, :, column(j)]
+        for side, at in ((0, sublane == 0), (1, sublane == depth - 1)):
+            state, adjoint = (edge_row(forth_edge_ref, j, side, f) for f in range(2))
+            before = before + jnp.where(at, (along * diffusion) * state - (across * diffusion) * adjoint, 0.0)
+            state, adjoint = (edge_row(back_edge_ref, j, side, f) for f in range(2))
+            after = after + jnp.where(at, (across * diffusion) * state + (along * diffusion) * adjoint, 0.0)
+        before, after = before * has_before, after * has_after
         for n in range(steps):
             values = relaxed(
                 (now[0, n], now[1, n]),
@@ -451,8 +463,12 @@
     received = lax.ppermute(send, "core", [(0, 1), (1, 0)])
 
     keep, iterate_after, forcing_after = lax.optimization_barrier((keep, iterate, forcing))
-    first, up, down = vmem_call(
-        first_kernel, (iterate.shape, (4 * steps, cells), (4 * steps, cells)), (), (iterate_after, forcing_after)
+    last = (2 * columns, depth, LANES)
+    first, up, down, forth, back = vmem_call(
+        first_kernel,
+        (iterate.shape, (4 * steps, cells), (4 * steps, cells), last, last),
+        (),
+        (iterate_after, forcing_after),
     )
     other, own = vmem_call(
         add_kernel,
@@ -462,7 +478,9 @@
         (pltpu.VMEM((4,) + keep.shape[2:], jnp.float32), pltpu.SemaphoreType.DMA((4,))),
         spaces=(pltpu.VMEM, pl.ANY),
     )
-    other, up, down = lax.optimization_barrier((other, up, down))
+    other, up, down, forth, back = lax.optimization_barrier((other, up, down, forth, back))
+    forth = shifted(forth, "tm", 1)
+    back = shifted(back, "tm", -1)
     above = shifted(up, ("pair", "core"), 1)
     below = shifted(down, ("pair", "core"), -1)
     term = swapped(other, "pair", 1)
@@ -474,28 +492,30 @@
     half = chosen(own, 1 - field) + chosen(term, 1 - field)
     half, above, below = lax.optimization_barrier((half, above, below))
     mine = chosen(own, field) + chosen(term, field) + swapped(half, "tm", 1)
-    payload = (2 * columns + 2 * columns // depth, depth, LANES)
-    swept, edge, forth, back = vmem_call(
+    rows = (4 * columns // depth, depth, LANES)
+    swept, edge, forth_edge, back_edge = vmem_call(
         functools.partial(second_kernel, steps, slabs),
-        (iterate.shape, (4 * steps, cells), payload, payload),
+        (iterate.shape, (4 * steps, cells), rows, rows),
         (place,),
-        (iterate, first, up, down, above, below),
+        (first, up, down, above, below),
     )
-    mine, _, _ = lax.optimization_barrier((mine, forth, back))
+    mine, forth_edge, back_edge = lax.optimization_barrier((mine, forth_edge, back_edge))
+    forth_edge = shifted(forth_edge, "tm", 1)
+    back_edge = shifted(back_edge, "tm", -1)
+    mine, forth, back = lax.optimization_barrier((mine, forth, back))
     mask = 2
     while mask < ranks:
         mine = mine + swapped(mine, "tm", mask)
         mask *= 2
+    mine, forth_edge, back_edge = lax.optimization_barrier((mine, forth_edge, back_edge))
     given = swapped(mine, "tm", 1)
     (coarse,) = vmem_call(last_kernel, (iterate.shape,), (place,), (mine, given))
-    forth = shifted(forth, "tm", 1)
-    back = shifted(back, "tm", -1)
     (smoothed,) = vmem_call(
         functools.partial(third_kernel, steps, ranks),
         (iterate.shape,),
         (place,),
-        (iterate, forcing, swept, edge, forth, back),
-        cost=64 * 2**20,
+        (iterate, forcing, swept, edge, forth, back, forth_edge, back_edge),
+        cost=8 * 2**20,
     )
     return smoothed, coarse
 

time: 57.6 us -> 64.5 us (1.12)
  starting transfers between devices: 19.5 us -> 26.8 us
  waiting for transfers between devices: 23.2 us -> 21.8 us
  other arithmetic: 0.16 us -> 0.87 us
    ppermute x5, waiting for transfers between devices: 22.1 us -> 9.35 us  [swapped(): lax.ppermute(value, axis, [(i, i ^ mask) for i in range(lax.axis_size(axi...]
    ppermute x4 -> x6, waiting for transfers between devices: 0.01 us -> 11.4 us  [shifted(): lax.ppermute(value, axis, [(i, i + by) for i in range(size) if 0 <= i + b...]
    ppermute x4 -> x6, starting transfers between devices: 7.77 us -> 12.4 us  [shifted(): lax.ppermute(value, axis, [(i, i + by) for i in range(size) if 0 <= i + b...]
    ppermute x5, starting transfers between devices: 11.2 us -> 13.9 us  [swapped(): lax.ppermute(value, axis, [(i, i ^ mask) for i in range(lax.axis_size(axi...]
    add x1, other arithmetic: 0.02 us -> 0.73 us  [local(): half = chosen(own, 1 - field) + chosen(term, 1 - field)]
  transfers between devices with their start and end apart: 10 -> 12, of which waited for: 5 -> 8; matrix products, arithmetic and copies ran while one was open for 0% -> 1% of each run, Pallas kernels for 6% -> 5%
where the time goes in v8:
time: 64.5 us; the launch traced here: 64.2 us
  starting transfers between devices  26.8 us (42%)
  waiting for transfers between devices  21.8 us (34%)
  Pallas kernels  13.9 us (22%)
  other arithmetic  0.87 us (1%)
  between operations  0.76 us (1%)
    ppermute x5, starting transfers between devices, swapped(): lax.ppermute(value, axis, [(i, i ^ mask) for i in range(lax.axis_size(axi...  13.9 us
    pallas_call x6, Pallas kernels, vmem_call(): pl.pallas_call(kernel, out_shape=out_shape, in_specs=[smem] * len(smem_in...  13.9 us
    ppermute x6, starting transfers between devices, shifted(): lax.ppermute(value, axis, [(i, i + by) for i in range(size) if 0 <= i + b...  12.4 us
    ppermute x6, waiting for transfers between devices, shifted(): lax.ppermute(value, axis, [(i, i + by) for i in range(size) if 0 <= i + b...  11.4 us
    ppermute x5, waiting for transfers between devices, swapped(): lax.ppermute(value, axis, [(i, i ^ mask) for i in range(lax.axis_size(axi...  9.35 us
  transfers between devices with their start and end apart: 12, of which 8 were waited for; matrix products, arithmetic and copies ran while one was open for 1% of the time, Pallas kernels for 5%

profile of v8, /device:TPU:0, one launch (start us, length us, event | category | flops | bytes accessed | tf_op | source)
XLA Modules:
  0.0 64.2 jit_solution(16429649395497506662)
XLA Ops:
  0.7 7.8 %shard_map.50 = (f32[2,2,32,8,128]{4,3,2,1,0:T(8,128)S(1)}, f32[2,2,32,8,128]{4,3,2,1,0:T(8,128)S(1)}) custom-call(s32[3]{0:T(128)S(1)} %pad_add_fusion.place_ref, f32[8,88,128]{2,1,0:T(8,128)} %constant.35.clone.weights_hbm, f32[2,2,8,4096]{3,2,1,0:T(8,128)} %iterate_ref.2, f32[2,2,8,4096]{3,2,1,0:T(8,128)} %forcing_ref.2), custom_call_target="tpu_custom_call" | custom-call | flops 1000000 | bytes 25165824 | tf_op jit(solution)/shard_map/pallas_call | solution.py:205
  9.6 1.0 %collective-permute-done.received_any = f32[2,2,32,8,128]{4,3,2,1,0:T(8,128)S(1)} collective-permute-done((f32[2,2,32,8,128]{4,3,2,1,0:T(8,128)S(1)}, f32[2,2,32,8,128]{4,3,2,1,0:T(8,128)S(1)}, u32[]{:S(2)}, u32[]{:S(2)}) %collective-permute-start) | collective-permute-done | bytes 524320 | tf_op jit(solution)/shard_map/ppermute | solution.py:463
  10.6 1.3 %shard_map.52 = (f32[2,32,8,128]{3,2,1,0:T(8,128)S(1)}, f32[2,32,8,128]{3,2,1,0:T(8,128)S(1)}) custom-call(s32[3]{0:T(128)S(1)} %pad_add_fusion.place_ref, f32[2,2,32,8,128]{4,3,2,1,0:T(8,128)S(1)} %get-tuple-element.39.keep_ref, f32[2,2,32,8,128]{4,3,2,1,0:T(8,128)S(1)} %collective-permute-done.received_any), custom_call_target="tpu_custom_call" | custom-call | flops 1000000 | bytes 1048576 | tf_op jit(solution)/shard_map/pallas_call | solution.py:205
  11.9 2.9 %collective-permute-start.1 = (f32[2,32,8,128]{3,2,1,0:T(8,128)S(1)}, f32[2,32,8,128]{3,2,1,0:T(8,128)S(1)}, u32[]{:S(2)}, u32[]{:S(2)}) collective-permute-start(f32[2,32,8,128]{3,2,1,0:T(8,128)S(1)} %get-tuple-element.49), channel_id=1, source_target_pairs={{0,2},{2,0},{1,3},{3,1},{4,6},{6,4},{5,7},{7,5},{8,10},{10,8},{9,1... | collective-permute-start | bytes 786440 | tf_op jit(solution)/shard_map/ppermute | solution.py:426
  14.9 1.8 %collective-permute-start.2 = (f32[8,4096]{1,0:T(8,128)S(1)}, f32[8,4096]{1,0:T(8,128)S(1)}, u32[]{:S(2)}, u32[]{:S(2)}) collective-permute-start(f32[8,4096]{1,0:T(8,128)S(1)} %get-tuple-element.46.up_ref), channel_id=1, source_target_pairs={{0,1},{1,2},{2,3},{4,5},{5,6},{6,7},{8,9},{9,10},{10,11},{12,13},{... | collective-permute-start | bytes 393224 | tf_op jit(solution)/shard_map/ppermute | solution.py:431
  16.6 1.3 %collective-permute-start.3 = (f32[8,4096]{1,0:T(8,128)S(1)}, f32[8,4096]{1,0:T(8,128)S(1)}, u32[]{:S(2)}, u32[]{:S(2)}) collective-permute-start(f32[8,4096]{1,0:T(8,128)S(1)} %get-tuple-element.47.down_ref), channel_id=1, source_target_pairs={{1,0},{2,1},{3,2},{5,4},{6,5},{7,6},{9,8},{10,9},{11,10},{13,12},{... | collective-permute-start | bytes 393224 | tf_op jit(solution)/shard_map/ppermute | solution.py:431
  17.9 3.6 %collective-permute-done.1 = f32[2,32,8,128]{3,2,1,0:T(8,128)S(1)} collective-permute-done((f32[2,32,8,128]{3,2,1,0:T(8,128)S(1)}, f32[2,32,8,128]{3,2,1,0:T(8,128)S(1)}, u32[]{:S(2)}, u32[]{:S(2)}) %collective-permute-start.1) | collective-permute-done | bytes 262176 | tf_op jit(solution)/shard_map/ppermute | solution.py:426
  21.5 0.7 %add_bitcast_fusion = f32[32,8,128]{2,1,0:T(8,128)} fusion(f32[2,32,8,128]{3,2,1,0:T(8,128)S(1)} %collective-permute-done.1, s32[]{:T(128)S(6)} %select_n.9, f32[2,32,8,128]{3,2,1,0:T(8,128)S(1)} %get-tuple-element.48), kind=kLoop, calls=%fused_computation.1 | loop fusion | flops 32768 | bytes 393220 | tf_op jit(solution)/shard_map/add | solution.py:492
  22.3 1.7 %collective-permute-start.4 = (f32[32,8,128]{2,1,0:T(8,128)}, f32[32,8,128]{2,1,0:T(8,128)S(1)}, u32[]{:S(2)}, u32[]{:S(2)}) collective-permute-start(f32[32,8,128]{2,1,0:T(8,128)} %add_bitcast_fusion), channel_id=1, source_target_pairs={{0,4},{4,0},{8,12},{12,8},{16,20},{20,16},{24,28},{28,24},{1,5},{5... | collective-permute-start | bytes 393224 | tf_op jit(solution)/shard_map/ppermute | solution.py:426
  24.0 2.2 %collective-permute-start.5 = (f32[64,8,128]{2,1,0:T(8,128)S(1)}, f32[64,8,128]{2,1,0:T(8,128)S(1)}, u32[]{:S(2)}, u32[]{:S(2)}) collective-permute-start(f32[64,8,128]{2,1,0:T(8,128)S(1)} %get-tuple-element.58), channel_id=1, source_target_pairs={{0,4},{4,8},{8,12},{12,16},{16,20},{20,24},{24,28},{1,5},{5,9},{9,... | collective-permute-start | bytes 786440 | tf_op jit(solution)/shard_map/ppermute | solution.py:431
  26.2 1.3 %collective-permute-start.6 = (f32[64,8,128]{2,1,0:T(8,128)S(1)}, f32[64,8,128]{2,1,0:T(8,128)S(1)}, u32[]{:S(2)}, u32[]{:S(2)}) collective-permute-start(f32[64,8,128]{2,1,0:T(8,128)S(1)} %get-tuple-element.59), channel_id=1, source_target_pairs={{4,0},{8,4},{12,8},{16,12},{20,16},{24,20},{28,24},{5,1},{9,5},{13... | collective-permute-start | bytes 786440 | tf_op jit(solution)/shard_map/ppermute | solution.py:431
  27.5 0.8 %shard_map.53 = (f32[2,2,8,4096]{3,2,1,0:T(8,128)S(1)}, f32[8,4096]{1,0:T(8,128)S(1)}, f32[16,8,128]{2,1,0:T(8,128)S(1)}, f32[16,8,128]{2,1,0:T(8,128)S(1)}) custom-call(s32[3]{0:T(128)S(1)} %pad_add_fusion.place_ref, f32[2,2,8,4096]{3,2,1,0:T(8,128)S(1)} %get-tuple-element.38.first_ref, f32[8,4096]{1,0:T(8,128)S(1)} %get-tuple-element.46.up_ref, ...), custom_call_target="tpu_custom_call" | custom-call | flops 1000000 | bytes 1048576 | tf_op jit(solution)/shard_map/pallas_call | solution.py:205
  28.7 10.4 %collective-permute-done.5.forth_ref = f32[64,8,128]{2,1,0:T(8,128)S(1)} collective-permute-done((f32[64,8,128]{2,1,0:T(8,128)S(1)}, f32[64,8,128]{2,1,0:T(8,128)S(1)}, u32[]{:S(2)}, u32[]{:S(2)}) %collective-permute-start.5) | collective-permute-done | bytes 262176 | tf_op jit(solution)/shard_map/ppermute | solution.py:431
  39.1 4.1 %collective-permute-start.7 = (f32[32,8,128]{2,1,0:T(8,128)S(1)}, f32[32,8,128]{2,1,0:T(8,128)S(1)}, u32[]{:S(2)}, u32[]{:S(2)}) collective-permute-start(f32[32,8,128]{2,1,0:T(8,128)S(1)} %bitcast_add_fusion), channel_id=1, source_target_pairs={{0,8},{4,12},{8,0},{12,4},{16,24},{20,28},{24,16},{28,20},{1,9},{5... | collective-permute-start | bytes 393224 | tf_op jit(solution)/shard_map/ppermute | solution.py:426
  43.1 3.8 %collective-permute-done.7 = f32[32,8,128]{2,1,0:T(8,128)S(1)} collective-permute-done((f32[32,8,128]{2,1,0:T(8,128)S(1)}, f32[32,8,128]{2,1,0:T(8,128)S(1)}, u32[]{:S(2)}, u32[]{:S(2)}) %collective-permute-start.7) | collective-permute-done | bytes 131104 | tf_op jit(solution)/shard_map/ppermute | solution.py:426
  46.9 2.8 %collective-permute-start.8 = (f32[32,8,128]{2,1,0:T(8,128)S(1)}, f32[32,8,128]{2,1,0:T(8,128)S(1)}, u32[]{:S(2)}, u32[]{:S(2)}) collective-permute-start(f32[32,8,128]{2,1,0:T(8,128)S(1)} %add.42), channel_id=1, source_target_pairs={{0,16},{4,20},{8,24},{12,28},{16,0},{20,4},{24,8},{28,12},{1,17},{... | collective-permute-start | bytes 393224 | tf_op jit(solution)/shard_map/ppermute | solution.py:426
  49.8 1.3 %collective-permute-start.10 = (f32[16,8,128]{2,1,0:T(8,128)S(1)}, f32[16,8,128]{2,1,0:T(8,128)S(1)}, u32[]{:S(2)}, u32[]{:S(2)}) collective-permute-start(f32[16,8,128]{2,1,0:T(8,128)S(1)} %get-tuple-element.64), channel_id=1, source_target_pairs={{4,0},{8,4},{12,8},{16,12},{20,16},{24,20},{28,24},{5,1},{9,5},{13... | collective-permute-start | bytes 196616 | tf_op jit(solution)/shard_map/ppermute | solution.py:431
  51.0 4.5 %collective-permute-start.9 = (f32[16,8,128]{2,1,0:T(8,128)S(1)}, f32[16,8,128]{2,1,0:T(8,128)S(1)}, u32[]{:S(2)}, u32[]{:S(2)}) collective-permute-start(f32[16,8,128]{2,1,0:T(8,128)S(1)} %get-tuple-element.63), channel_id=1, source_target_pairs={{0,4},{4,8},{8,12},{12,16},{16,20},{20,24},{24,28},{1,5},{5,9},{9,... | collective-permute-start | bytes 196616 | tf_op jit(solution)/shard_map/ppermute | solution.py:431
  55.6 0.8 %collective-permute-done.8 = f32[32,8,128]{2,1,0:T(8,128)S(1)} collective-permute-done((f32[32,8,128]{2,1,0:T(8,128)S(1)}, f32[32,8,128]{2,1,0:T(8,128)S(1)}, u32[]{:S(2)}, u32[]{:S(2)}) %collective-permute-start.8) | collective-permute-done | bytes 131104 | tf_op jit(solution)/shard_map/ppermute | solution.py:426
  56.5 1.0 %collective-permute-done.9.forth_edge_ref = f32[16,8,128]{2,1,0:T(8,128)S(1)} collective-permute-done((f32[16,8,128]{2,1,0:T(8,128)S(1)}, f32[16,8,128]{2,1,0:T(8,128)S(1)}, u32[]{:S(2)}, u32[]{:S(2)}) %collective-permute-start.9) | collective-permute-done | bytes 65568 | tf_op jit(solution)/shard_map/ppermute | solution.py:431
  57.5 2.4 %collective-permute-start.11 = (f32[32,8,128]{2,1,0:T(8,128)S(1)}, f32[32,8,128]{2,1,0:T(8,128)S(1)}, u32[]{:S(2)}, u32[]{:S(2)}) collective-permute-start(f32[32,8,128]{2,1,0:T(8,128)S(1)} %add.43.mine_ref), channel_id=1, source_target_pairs={{0,4},{4,0},{8,12},{12,8},{16,20},{20,16},{24,28},{28,24},{1,5},{5... | collective-permute-start | bytes 393224 | tf_op jit(solution)/shard_map/ppermute | solution.py:426
  59.8 2.0 %shard_map.54 = f32[2,2,8,4096]{3,2,1,0:T(8,128)} custom-call(s32[3]{0:T(128)S(1)} %pad_add_fusion.place_ref, f32[2,2,8,4096]{3,2,1,0:T(8,128)S(1)} %copy-done, f32[2,2,8,4096]{3,2,1,0:T(8,128)S(1)} %copy-done.1, f32[2,2,8,4096]{3,2,1,0:T(8,128)S(1)} %get-tuple-element.52.swept_ref, f32[8,4096]{1,0:T(8,128)S(1)} %get-tuple-element.53.edge_ref, ...), custom_call_target="tpu_custom_call" | custom-call | flops 1000000 | bytes 8388608 | tf_op jit(solution)/shard_map/pallas_call | solution.py:205
  61.9 0.9 %collective-permute-done.11.given_ref = f32[32,8,128]{2,1,0:T(8,128)S(1)} collective-permute-done((f32[32,8,128]{2,1,0:T(8,128)S(1)}, f32[32,8,128]{2,1,0:T(8,128)S(1)}, u32[]{:S(2)}, u32[]{:S(2)}) %collective-permute-start.11) | collective-permute-done | bytes 131104 | tf_op jit(solution)/shard_map/ppermute | solution.py:426
  62.8 1.4 %shard_map.55 = f32[2,2,8,4096]{3,2,1,0:T(8,128)} custom-call(s32[3]{0:T(128)S(1)} %pad_add_fusion.place_ref, f32[32,8,128]{2,1,0:T(8,128)S(1)} %add.43.mine_ref, f32[32,8,128]{2,1,0:T(8,128)S(1)} %collective-permute-done.11.given_ref), custom_call_target="tpu_custom_call" | custom-call | flops 1000000 | bytes 1048576 | tf_op jit(solution)/shard_map/pallas_call | solution.py:205
  (19 shorter events, 1.4 us)
Async XLA Ops:
  0.7 8.4 %copy-start = (f32[2,2,8,4096]{3,2,1,0:T(8,128)S(1)}, f32[2,2,8,4096]{3,2,1,0:T(8,128)}, u32[]{:S(2)}) copy-start(f32[2,2,8,4096]{3,2,1,0:T(8,128)} %iterate_ref.2) | copy-start | bytes 1572868
  0.7 8.4 %copy-start.1 = (f32[2,2,8,4096]{3,2,1,0:T(8,128)S(1)}, f32[2,2,8,4096]{3,2,1,0:T(8,128)}, u32[]{:S(2)}) copy-start(f32[2,2,8,4096]{3,2,1,0:T(8,128)} %forcing_ref.2) | copy-start | bytes 1572868
  8.6 2.1 %collective-permute-start = (f32[2,2,32,8,128]{4,3,2,1,0:T(8,128)S(1)}, f32[2,2,32,8,128]{4,3,2,1,0:T(8,128)S(1)}, u32[]{:S(2)}, u32[]{:S(2)}) collective-permute-start(f32[2,2,32,8,128]{4,3,2,1,0:T(8,128)S(1)} %get-tuple-element.40), channel_id=1, source_target_pairs={{0,1},{1,0},{2,3},{3,2},{4,5},{5,4},{6,7},{7,6},{8,9},{9,8},{10,11... | collective-permute-start | bytes 1572872 | tf_op jit(solution)/shard_map/ppermute | solution.py:463
  11.9 9.6 %collective-permute-start.1 = (f32[2,32,8,128]{3,2,1,0:T(8,128)S(1)}, f32[2,32,8,128]{3,2,1,0:T(8,128)S(1)}, u32[]{:S(2)}, u32[]{:S(2)}) collective-permute-start(f32[2,32,8,128]{3,2,1,0:T(8,128)S(1)} %get-tuple-element.49), channel_id=1, source_target_pairs={{0,2},{2,0},{1,3},{3,1},{4,6},{6,4},{5,7},{7,5},{8,10},{10,8},{9,1... | collective-permute-start | bytes 786440 | tf_op jit(solution)/shard_map/ppermute | solution.py:426
  14.9 7.4 %collective-permute-start.2 = (f32[8,4096]{1,0:T(8,128)S(1)}, f32[8,4096]{1,0:T(8,128)S(1)}, u32[]{:S(2)}, u32[]{:S(2)}) collective-permute-start(f32[8,4096]{1,0:T(8,128)S(1)} %get-tuple-element.46.up_ref), channel_id=1, source_target_pairs={{0,1},{1,2},{2,3},{4,5},{5,6},{6,7},{8,9},{9,10},{10,11},{12,13},{... | collective-permute-start | bytes 393224 | tf_op jit(solution)/shard_map/ppermute | solution.py:431
  16.6 5.6 %collective-permute-start.3 = (f32[8,4096]{1,0:T(8,128)S(1)}, f32[8,4096]{1,0:T(8,128)S(1)}, u32[]{:S(2)}, u32[]{:S(2)}) collective-permute-start(f32[8,4096]{1,0:T(8,128)S(1)} %get-tuple-element.47.down_ref), channel_id=1, source_target_pairs={{1,0},{2,1},{3,2},{5,4},{6,5},{7,6},{9,8},{10,9},{11,10},{13,12},{... | collective-permute-start | bytes 393224 | tf_op jit(solution)/shard_map/ppermute | solution.py:431
  21.5 2.5 %copy-start.2 = (f32[2,32,8,128]{3,2,1,0:T(8,128)}, f32[2,32,8,128]{3,2,1,0:T(8,128)S(1)}, u32[]{:S(2)}) copy-start(f32[2,32,8,128]{3,2,1,0:T(8,128)S(1)} %collective-permute-done.1) | copy-start | bytes 786436
  22.3 6.3 %collective-permute-start.4 = (f32[32,8,128]{2,1,0:T(8,128)}, f32[32,8,128]{2,1,0:T(8,128)S(1)}, u32[]{:S(2)}, u32[]{:S(2)}) collective-permute-start(f32[32,8,128]{2,1,0:T(8,128)} %add_bitcast_fusion), channel_id=1, source_target_pairs={{0,4},{4,0},{8,12},{12,8},{16,20},{20,16},{24,28},{28,24},{1,5},{5... | collective-permute-start | bytes 393224 | tf_op jit(solution)/shard_map/ppermute | solution.py:426
  24.0 15.1 %collective-permute-start.5 = (f32[64,8,128]{2,1,0:T(8,128)S(1)}, f32[64,8,128]{2,1,0:T(8,128)S(1)}, u32[]{:S(2)}, u32[]{:S(2)}) collective-permute-start(f32[64,8,128]{2,1,0:T(8,128)S(1)} %get-tuple-element.58), channel_id=1, source_target_pairs={{0,4},{4,8},{8,12},{12,16},{16,20},{20,24},{24,28},{1,5},{5,9},{9,... | collective-permute-start | bytes 786440 | tf_op jit(solution)/shard_map/ppermute | solution.py:431
  26.2 12.8 %collective-permute-start.6 = (f32[64,8,128]{2,1,0:T(8,128)S(1)}, f32[64,8,128]{2,1,0:T(8,128)S(1)}, u32[]{:S(2)}, u32[]{:S(2)}) collective-permute-start(f32[64,8,128]{2,1,0:T(8,128)S(1)} %get-tuple-element.59), channel_id=1, source_target_pairs={{4,0},{8,4},{12,8},{16,12},{20,16},{24,20},{28,24},{5,1},{9,5},{13... | collective-permute-start | bytes 786440 | tf_op jit(solution)/shard_map/ppermute | solution.py:431
  27.5 1.1 %copy-start.3 = (f32[2,32,8,128]{3,2,1,0:T(8,128)S(1)}, f32[2,32,8,128]{3,2,1,0:T(8,128)}, u32[]{:S(2)}) copy-start(f32[2,32,8,128]{3,2,1,0:T(8,128)} %copy-done.2) | copy-start | bytes 786436
  39.1 7.9 %collective-permute-start.7 = (f32[32,8,128]{2,1,0:T(8,128)S(1)}, f32[32,8,128]{2,1,0:T(8,128)S(1)}, u32[]{:S(2)}, u32[]{:S(2)}) collective-permute-start(f32[32,8,128]{2,1,0:T(8,128)S(1)} %bitcast_add_fusion), channel_id=1, source_target_pairs={{0,8},{4,12},{8,0},{12,4},{16,24},{20,28},{24,16},{28,20},{1,9},{5... | collective-permute-start | bytes 393224 | tf_op jit(solution)/shard_map/ppermute | solution.py:426
  46.9 9.5 %collective-permute-start.8 = (f32[32,8,128]{2,1,0:T(8,128)S(1)}, f32[32,8,128]{2,1,0:T(8,128)S(1)}, u32[]{:S(2)}, u32[]{:S(2)}) collective-permute-start(f32[32,8,128]{2,1,0:T(8,128)S(1)} %add.42), channel_id=1, source_target_pairs={{0,16},{4,20},{8,24},{12,28},{16,0},{20,4},{24,8},{28,12},{1,17},{... | collective-permute-start | bytes 393224 | tf_op jit(solution)/shard_map/ppermute | solution.py:426
  49.8 6.7 %collective-permute-start.10 = (f32[16,8,128]{2,1,0:T(8,128)S(1)}, f32[16,8,128]{2,1,0:T(8,128)S(1)}, u32[]{:S(2)}, u32[]{:S(2)}) collective-permute-start(f32[16,8,128]{2,1,0:T(8,128)S(1)} %get-tuple-element.64), channel_id=1, source_target_pairs={{4,0},{8,4},{12,8},{16,12},{20,16},{24,20},{28,24},{5,1},{9,5},{13... | collective-permute-start | bytes 196616 | tf_op jit(solution)/shard_map/ppermute | solution.py:431
  51.0 6.4 %collective-permute-start.9 = (f32[16,8,128]{2,1,0:T(8,128)S(1)}, f32[16,8,128]{2,1,0:T(8,128)S(1)}, u32[]{:S(2)}, u32[]{:S(2)}) collective-permute-start(f32[16,8,128]{2,1,0:T(8,128)S(1)} %get-tuple-element.63), channel_id=1, source_target_pairs={{0,4},{4,8},{8,12},{12,16},{16,20},{20,24},{24,28},{1,5},{5,9},{9,... | collective-permute-start | bytes 196616 | tf_op jit(solution)/shard_map/ppermute | solution.py:431
  57.5 5.3 %collective-permute-start.11 = (f32[32,8,128]{2,1,0:T(8,128)S(1)}, f32[32,8,128]{2,1,0:T(8,128)S(1)}, u32[]{:S(2)}, u32[]{:S(2)}) collective-permute-start(f32[32,8,128]{2,1,0:T(8,128)S(1)} %add.43.mine_ref), channel_id=1, source_target_pairs={{0,4},{4,0},{8,12},{12,8},{16,20},{20,16},{24,28},{28,24},{1,5},{5... | collective-permute-start | bytes 393224 | tf_op jit(solution)/shard_map/ppermute | solution.py:426

commit v9 on v8

--- a/solution.py
+++ b/solution.py
@@ -198,15 +198,14 @@
                     ref[half, f, j] = value
 
 
-def vmem_call(kernel, out_shapes, smem_inputs, inputs, scratch=(), spaces=None, limit=6, cost=2**20):
+def vmem_call(kernel, out_shapes, smem_inputs, inputs, scratch=(), spaces=None, target=pltpu.VMEM, limit=6, cost=2**20):
     smem = pl.BlockSpec(memory_space=pltpu.SMEM)
-    vmem = pl.BlockSpec(memory_space=pltpu.VMEM)
     out_shape = tuple(jax.ShapeDtypeStruct(shape, jnp.float32) for shape in out_shapes)
     return pl.pallas_call(
         kernel,
         out_shape=out_shape,
         in_specs=[smem] * len(smem_inputs) + [pl.BlockSpec(memory_space=space) for space in spaces or [pltpu.VMEM] * len(inputs)],
-        out_specs=(vmem,) * len(out_shape),
+        out_specs=(pl.BlockSpec(memory_space=target),) * len(out_shape),
         scratch_shapes=list(scratch),
         compiler_params=pltpu.CompilerParams(vmem_limit_bytes=limit * 2**20),
         cost_estimate=pl.CostEstimate(flops=10**6, bytes_accessed=cost, transcendentals=0),
@@ -445,13 +444,18 @@
         (other_ref, own_ref)[k // 2][f] = keep_ref[index, f] + received_ref[k]
 
 
-def last_kernel(place_ref, mine_ref, given_ref, out_ref):
-    steps = out_ref.shape[1]
+def last_kernel(place_ref, mine_ref, given_ref, out_hbm, whole_ref, left):
+    steps = out_hbm.shape[1]
     field = lax.rem(place_ref[0], 2)
-    for j in range(mine_ref.shape[0]):
+    copies = []
+    for k, (ref, f) in enumerate(((mine_ref, field), (given_ref, 1 - field))):
+        for j in range(ref.shape[0]):
+            whole_ref[k, :, column(j)] = ref[j]
         for n in range(steps):
-            out_ref[field, n, :, column(j)] = mine_ref[j]
-            out_ref[1 - field, n, :, column(j)] = given_ref[j]
+            copies.append(pltpu.make_async_copy(whole_ref.at[k], out_hbm.at[f, n], left.at[k, n]))
+            copies[-1].start()
+    for copy in copies:
+        copy.wait()
 
 
 def local(iterate, forcing):
@@ -480,18 +484,19 @@
     )
     other, up, down, forth, back = lax.optimization_barrier((other, up, down, forth, back))
     forth = shifted(forth, "tm", 1)
-    back = shifted(back, "tm", -1)
+    term = swapped(other, "pair", 1)
+    field = lax.rem(lax.axis_index("tm"), 2)
+
+    def chosen(array, index):
+        return lax.dynamic_index_in_dim(array, index, 0, keepdims=False)
+
+    half = chosen(own, 1 - field) + chosen(term, 1 - field)
+    half, forth = lax.optimization_barrier((half, forth))
+    half, up, down = lax.optimization_barrier((half, up, down))
+    mine = chosen(own, field) + chosen(term, field) + swapped(half, "tm", 1)
     above = shifted(up, ("pair", "core"), 1)
     below = shifted(down, ("pair", "core"), -1)
-    term = swapped(other, "pair", 1)
-    field = lax.rem(lax.axis_index("tm"), 2)
-
-    def chosen(array, index):
-        return lax.dynamic_index_in_dim(array, index, 0, keepdims=False)
-
-    half = chosen(own, 1 - field) + chosen(term, 1 - field)
-    half, above, below = lax.optimization_barrier((half, above, below))
-    mine = chosen(own, field) + chosen(term, field) + swapped(half, "tm", 1)
+    mine, above, below, back = lax.optimization_barrier((mine, above, below, back))
     rows = (4 * columns // depth, depth, LANES)
     swept, edge, forth_edge, back_edge = vmem_call(
         functools.partial(second_kernel, steps, slabs),
@@ -499,17 +504,25 @@
         (place,),
         (first, up, down, above, below),
     )
-    mine, forth_edge, back_edge = lax.optimization_barrier((mine, forth_edge, back_edge))
+    back = shifted(back, "tm", -1)
+    mask = 2
+    while mask < ranks:
+        if 2 * mask == ranks:
+            mine, back, forth_edge, back_edge = lax.optimization_barrier((mine, back, forth_edge, back_edge))
+        mine = mine + swapped(mine, "tm", mask)
+        mask *= 2
     forth_edge = shifted(forth_edge, "tm", 1)
     back_edge = shifted(back_edge, "tm", -1)
-    mine, forth, back = lax.optimization_barrier((mine, forth, back))
-    mask = 2
-    while mask < ranks:
-        mine = mine + swapped(mine, "tm", mask)
-        mask *= 2
     mine, forth_edge, back_edge = lax.optimization_barrier((mine, forth_edge, back_edge))
     given = swapped(mine, "tm", 1)
-    (coarse,) = vmem_call(last_kernel, (iterate.shape,), (place,), (mine, given))
+    (coarse,) = vmem_call(
+        last_kernel,
+        (iterate.shape,),
+        (place,),
+        (mine, given),
+        (pltpu.VMEM((2, depth, cells), jnp.float32), pltpu.SemaphoreType.DMA((2, steps))),
+        target=pltpu.HBM,
+    )
     (smoothed,) = vmem_call(
         functools.partial(third_kernel, steps, ranks),
         (iterate.shape,),

time: 64.5 us -> 62.1 us (0.963)
  the two profiles are of different devices: /device:TPU:0 before, /device:TPU:6 now
where the time goes in v9:
time: 62.1 us; the launch traced here: 61.9 us
  starting transfers between devices  26.2 us (42%)
  waiting for transfers between devices  20.9 us (34%)
  Pallas kernels  13.9 us (22%)
  between operations  0.78 us (1%)
    ppermute x6, starting transfers between devices, shifted(): lax.ppermute(value, axis, [(i, i + by) for i in range(size) if 0 <= i + b...  18.7 us
    pallas_call x6, Pallas kernels, vmem_call(): pl.pallas_call(kernel, out_shape=out_shape, in_specs=[smem] * len(smem_in...  13.9 us
    ppermute x5, waiting for transfers between devices, swapped(): lax.ppermute(value, axis, [(i, i ^ mask) for i in range(lax.axis_size(axi...  9.78 us
    ppermute x6, waiting for transfers between devices, shifted(): lax.ppermute(value, axis, [(i, i + by) for i in range(size) if 0 <= i + b...  9.73 us
    ppermute x5, starting transfers between devices, swapped(): lax.ppermute(value, axis, [(i, i ^ mask) for i in range(lax.axis_size(axi...  7.37 us
    ppermute x1, waiting for transfers between devices, local(): received = lax.ppermute(send, 'core', [(0, 1), (1, 0)])  1.37 us
  transfers between devices with their start and end apart: 12, of which 10 were waited for; matrix products, arithmetic and copies ran while one was open for 0% of the time, Pallas kernels for 5%

profile of v9, /device:TPU:6, one launch (start us, length us, event | category | flops | bytes accessed | tf_op | source)
XLA Modules:
  0.0 61.9 jit_solution(17726267484428944882)
XLA Ops:
  0.7 7.8 %shard_map.50 = (f32[2,2,32,8,128]{4,3,2,1,0:T(8,128)S(1)}, f32[2,2,32,8,128]{4,3,2,1,0:T(8,128)S(1)}) custom-call(s32[3]{0:T(128)S(1)} %pad_add_fusion.place_ref, f32[8,88,128]{2,1,0:T(8,128)} %constant.35.clone.weights_hbm, f32[2,2,8,4096]{3,2,1,0:T(8,128)} %iterate_ref.2, f32[2,2,8,4096]{3,2,1,0:T(8,128)} %forcing_ref.2), custom_call_target="tpu_custom_call" | custom-call | flops 1000000 | bytes 25165824 | tf_op jit(solution)/shard_map/pallas_call | solution.py:204
  8.7 0.5 shard_map.51
  9.2 1.4 %collective-permute-done.received_any = f32[2,2,32,8,128]{4,3,2,1,0:T(8,128)S(1)} collective-permute-done((f32[2,2,32,8,128]{4,3,2,1,0:T(8,128)S(1)}, f32[2,2,32,8,128]{4,3,2,1,0:T(8,128)S(1)}, u32[]{:S(2)}, u32[]{:S(2)}) %collective-permute-start) | collective-permute-done | bytes 524320 | tf_op jit(solution)/shard_map/ppermute | solution.py:467
  10.5 1.3 %shard_map.52 = (f32[2,32,8,128]{3,2,1,0:T(8,128)S(1)}, f32[2,32,8,128]{3,2,1,0:T(8,128)S(1)}) custom-call(s32[3]{0:T(128)S(1)} %pad_add_fusion.place_ref, f32[2,2,32,8,128]{4,3,2,1,0:T(8,128)S(1)} %get-tuple-element.43.keep_ref, f32[2,2,32,8,128]{4,3,2,1,0:T(8,128)S(1)} %collective-permute-done.received_any), custom_call_target="tpu_custom_call" | custom-call | flops 1000000 | bytes 1048576 | tf_op jit(solution)/shard_map/pallas_call | solution.py:204
  11.9 0.6 collective-permute-start.1
  12.5 3.4 %collective-permute-start.2 = (f32[64,8,128]{2,1,0:T(8,128)S(1)}, f32[64,8,128]{2,1,0:T(8,128)S(1)}, u32[]{:S(2)}, u32[]{:S(2)}) collective-permute-start(f32[64,8,128]{2,1,0:T(8,128)S(1)} %get-tuple-element.52), channel_id=1, source_target_pairs={{0,4},{4,8},{8,12},{12,16},{16,20},{20,24},{24,28},{1,5},{5,9},{9,... | collective-permute-start | bytes 786440 | tf_op jit(solution)/shard_map/ppermute | solution.py:430
  15.9 4.4 %collective-permute-done.1 = f32[2,32,8,128]{3,2,1,0:T(8,128)S(1)} collective-permute-done((f32[2,32,8,128]{3,2,1,0:T(8,128)S(1)}, f32[2,32,8,128]{3,2,1,0:T(8,128)S(1)}, u32[]{:S(2)}, u32[]{:S(2)}) %collective-permute-start.1) | collective-permute-done | bytes 262176 | tf_op jit(solution)/shard_map/ppermute | solution.py:425
  20.3 2.1 %collective-permute-done.2.forth_ref = f32[64,8,128]{2,1,0:T(8,128)S(1)} collective-permute-done((f32[64,8,128]{2,1,0:T(8,128)S(1)}, f32[64,8,128]{2,1,0:T(8,128)S(1)}, u32[]{:S(2)}, u32[]{:S(2)}) %collective-permute-start.2) | collective-permute-done | bytes 262176 | tf_op jit(solution)/shard_map/ppermute | solution.py:430
  22.4 1.9 %collective-permute-start.4 = (f32[8,4096]{1,0:T(8,128)S(1)}, f32[8,4096]{1,0:T(8,128)S(1)}, u32[]{:S(2)}, u32[]{:S(2)}) collective-permute-start(f32[8,4096]{1,0:T(8,128)S(1)} %get-tuple-element.56.up_ref), channel_id=1, source_target_pairs={{0,1},{1,2},{2,3},{4,5},{5,6},{6,7},{8,9},{9,10},{10,11},{12,13},{... | collective-permute-start | bytes 393224 | tf_op jit(solution)/shard_map/ppermute | solution.py:430
  24.3 3.6 %collective-permute-start.5 = (f32[8,4096]{1,0:T(8,128)S(1)}, f32[8,4096]{1,0:T(8,128)S(1)}, u32[]{:S(2)}, u32[]{:S(2)}) collective-permute-start(f32[8,4096]{1,0:T(8,128)S(1)} %get-tuple-element.57.down_ref), channel_id=1, source_target_pairs={{1,0},{2,1},{3,2},{5,4},{6,5},{7,6},{9,8},{10,9},{11,10},{13,12},{... | collective-permute-start | bytes 393224 | tf_op jit(solution)/shard_map/ppermute | solution.py:430
  28.0 0.7 %collective-permute-done.4.above_ref = f32[8,4096]{1,0:T(8,128)S(1)} collective-permute-done((f32[8,4096]{1,0:T(8,128)S(1)}, f32[8,4096]{1,0:T(8,128)S(1)}, u32[]{:S(2)}, u32[]{:S(2)}) %collective-permute-start.4) | collective-permute-done | bytes 131104 | tf_op jit(solution)/shard_map/ppermute | solution.py:430
  28.7 1.8 %collective-permute-done.5.below_ref = f32[8,4096]{1,0:T(8,128)S(1)} collective-permute-done((f32[8,4096]{1,0:T(8,128)S(1)}, f32[8,4096]{1,0:T(8,128)S(1)}, u32[]{:S(2)}, u32[]{:S(2)}) %collective-permute-start.5) | collective-permute-done | bytes 131104 | tf_op jit(solution)/shard_map/ppermute | solution.py:430
  30.5 3.9 %collective-permute-start.7 = (f32[64,8,128]{2,1,0:T(8,128)S(1)}, f32[64,8,128]{2,1,0:T(8,128)S(1)}, u32[]{:S(2)}, u32[]{:S(2)}) collective-permute-start(f32[64,8,128]{2,1,0:T(8,128)S(1)} %get-tuple-element.66), channel_id=1, source_target_pairs={{4,0},{8,4},{12,8},{16,12},{20,16},{24,20},{28,24},{5,1},{9,5},{13... | collective-permute-start | bytes 786440 | tf_op jit(solution)/shard_map/ppermute | solution.py:430
  34.4 1.6 %collective-permute-start.6 = (f32[32,8,128]{2,1,0:T(8,128)S(1)}, f32[32,8,128]{2,1,0:T(8,128)S(1)}, u32[]{:S(2)}, u32[]{:S(2)}) collective-permute-start(f32[32,8,128]{2,1,0:T(8,128)S(1)} %bitcast_add_fusion), channel_id=1, source_target_pairs={{0,8},{4,12},{8,0},{12,4},{16,24},{20,28},{24,16},{28,20},{1,9},{5... | collective-permute-start | bytes 393224 | tf_op jit(solution)/shard_map/ppermute | solution.py:425
  36.1 0.8 %shard_map.53 = (f32[2,2,8,4096]{3,2,1,0:T(8,128)S(1)}, f32[8,4096]{1,0:T(8,128)S(1)}, f32[16,8,128]{2,1,0:T(8,128)S(1)}, f32[16,8,128]{2,1,0:T(8,128)S(1)}) custom-call(s32[3]{0:T(128)S(1)} %pad_add_fusion.place_ref, f32[2,2,8,4096]{3,2,1,0:T(8,128)S(1)} %get-tuple-element.42.first_ref, f32[8,4096]{1,0:T(8,128)S(1)} %get-tuple-element.56.up_ref, ...), custom_call_target="tpu_custom_call" | custom-call | flops 1000000 | bytes 1048576 | tf_op jit(solution)/shard_map/pallas_call | solution.py:204
  36.9 2.6 %collective-permute-done.6 = f32[32,8,128]{2,1,0:T(8,128)S(1)} collective-permute-done((f32[32,8,128]{2,1,0:T(8,128)S(1)}, f32[32,8,128]{2,1,0:T(8,128)S(1)}, u32[]{:S(2)}, u32[]{:S(2)}) %collective-permute-start.6) | collective-permute-done | bytes 131104 | tf_op jit(solution)/shard_map/ppermute | solution.py:425
  39.5 1.1 %collective-permute-done.7.back_ref = f32[64,8,128]{2,1,0:T(8,128)S(1)} collective-permute-done((f32[64,8,128]{2,1,0:T(8,128)S(1)}, f32[64,8,128]{2,1,0:T(8,128)S(1)}, u32[]{:S(2)}, u32[]{:S(2)}) %collective-permute-start.7) | collective-permute-done | bytes 262176 | tf_op jit(solution)/shard_map/ppermute | solution.py:430
  40.5 5.0 %collective-permute-start.8 = (f32[32,8,128]{2,1,0:T(8,128)S(1)}, f32[32,8,128]{2,1,0:T(8,128)S(1)}, u32[]{:S(2)}, u32[]{:S(2)}) collective-permute-start(f32[32,8,128]{2,1,0:T(8,128)S(1)} %add.42), channel_id=1, source_target_pairs={{0,16},{4,20},{8,24},{12,28},{16,0},{20,4},{24,8},{28,12},{1,17},{... | collective-permute-start | bytes 393224 | tf_op jit(solution)/shard_map/ppermute | solution.py:425
  45.5 2.9 %collective-permute-start.9 = (f32[16,8,128]{2,1,0:T(8,128)S(1)}, f32[16,8,128]{2,1,0:T(8,128)S(1)}, u32[]{:S(2)}, u32[]{:S(2)}) collective-permute-start(f32[16,8,128]{2,1,0:T(8,128)S(1)} %get-tuple-element.71), channel_id=1, source_target_pairs={{0,4},{4,8},{8,12},{12,16},{16,20},{20,24},{24,28},{1,5},{5,9},{9,... | collective-permute-start | bytes 196616 | tf_op jit(solution)/shard_map/ppermute | solution.py:430
  48.5 2.9 %collective-permute-start.10 = (f32[16,8,128]{2,1,0:T(8,128)S(1)}, f32[16,8,128]{2,1,0:T(8,128)S(1)}, u32[]{:S(2)}, u32[]{:S(2)}) collective-permute-start(f32[16,8,128]{2,1,0:T(8,128)S(1)} %get-tuple-element.72), channel_id=1, source_target_pairs={{4,0},{8,4},{12,8},{16,12},{20,16},{24,20},{28,24},{5,1},{9,5},{13... | collective-permute-start | bytes 196616 | tf_op jit(solution)/shard_map/ppermute | solution.py:430
  51.7 3.8 %collective-permute-done.10.back_edge_ref = f32[16,8,128]{2,1,0:T(8,128)S(1)} collective-permute-done((f32[16,8,128]{2,1,0:T(8,128)S(1)}, f32[16,8,128]{2,1,0:T(8,128)S(1)}, u32[]{:S(2)}, u32[]{:S(2)}) %collective-permute-start.10) | collective-permute-done | bytes 65568 | tf_op jit(solution)/shard_map/ppermute | solution.py:430
  55.6 2.0 %shard_map.54 = f32[2,2,8,4096]{3,2,1,0:T(8,128)} custom-call(s32[3]{0:T(128)S(1)} %pad_add_fusion.place_ref, f32[2,2,8,4096]{3,2,1,0:T(8,128)S(1)} %copy-done, f32[2,2,8,4096]{3,2,1,0:T(8,128)S(1)} %copy-done.1, f32[2,2,8,4096]{3,2,1,0:T(8,128)S(1)} %get-tuple-element.62.swept_ref, f32[8,4096]{1,0:T(8,128)S(1)} %get-tuple-element.63.edge_ref, ...), custom_call_target="tpu_custom_call" | custom-call | flops 1000000 | bytes 8388608 | tf_op jit(solution)/shard_map/pallas_call | solution.py:204
  57.7 2.8 %collective-permute-done.11.given_ref = f32[32,8,128]{2,1,0:T(8,128)S(1)} collective-permute-done((f32[32,8,128]{2,1,0:T(8,128)S(1)}, f32[32,8,128]{2,1,0:T(8,128)S(1)}, u32[]{:S(2)}, u32[]{:S(2)}) %collective-permute-start.11) | collective-permute-done | bytes 131104 | tf_op jit(solution)/shard_map/ppermute | solution.py:425
  60.5 1.4 %shard_map.55 = f32[2,2,8,4096]{3,2,1,0:T(8,128)} custom-call(s32[3]{0:T(128)S(1)} %pad_add_fusion.place_ref, f32[32,8,128]{2,1,0:T(8,128)S(1)} %add.43.mine_ref, f32[32,8,128]{2,1,0:T(8,128)S(1)} %collective-permute-done.11.given_ref), custom_call_target="tpu_custom_call" | custom-call | flops 1000000 | bytes 1048576 | tf_op jit(solution)/shard_map/pallas_call | solution.py:204
  (15 shorter events, 0.6 us)
Async XLA Ops:
  0.7 7.9 %copy-start = (f32[2,2,8,4096]{3,2,1,0:T(8,128)S(1)}, f32[2,2,8,4096]{3,2,1,0:T(8,128)}, u32[]{:S(2)}) copy-start(f32[2,2,8,4096]{3,2,1,0:T(8,128)} %iterate_ref.2) | copy-start | bytes 1572868
  0.7 7.9 %copy-start.1 = (f32[2,2,8,4096]{3,2,1,0:T(8,128)S(1)}, f32[2,2,8,4096]{3,2,1,0:T(8,128)}, u32[]{:S(2)}) copy-start(f32[2,2,8,4096]{3,2,1,0:T(8,128)} %forcing_ref.2) | copy-start | bytes 1572868
  8.6 2.0 %collective-permute-start = (f32[2,2,32,8,128]{4,3,2,1,0:T(8,128)S(1)}, f32[2,2,32,8,128]{4,3,2,1,0:T(8,128)S(1)}, u32[]{:S(2)}, u32[]{:S(2)}) collective-permute-start(f32[2,2,32,8,128]{4,3,2,1,0:T(8,128)S(1)} %get-tuple-element.44), channel_id=1, source_target_pairs={{0,1},{1,0},{2,3},{3,2},{4,5},{5,4},{6,7},{7,6},{8,9},{9,8},{10,11... | collective-permute-start | bytes 1572872 | tf_op jit(solution)/shard_map/ppermute | solution.py:467
  11.9 8.4 %collective-permute-start.1 = (f32[2,32,8,128]{3,2,1,0:T(8,128)S(1)}, f32[2,32,8,128]{3,2,1,0:T(8,128)S(1)}, u32[]{:S(2)}, u32[]{:S(2)}) collective-permute-start(f32[2,32,8,128]{3,2,1,0:T(8,128)S(1)} %get-tuple-element.51), channel_id=1, source_target_pairs={{0,2},{2,0},{1,3},{3,1},{4,6},{6,4},{5,7},{7,5},{8,10},{10,8},{9,1... | collective-permute-start | bytes 786440 | tf_op jit(solution)/shard_map/ppermute | solution.py:425
  12.5 9.9 %collective-permute-start.2 = (f32[64,8,128]{2,1,0:T(8,128)S(1)}, f32[64,8,128]{2,1,0:T(8,128)S(1)}, u32[]{:S(2)}, u32[]{:S(2)}) collective-permute-start(f32[64,8,128]{2,1,0:T(8,128)S(1)} %get-tuple-element.52), channel_id=1, source_target_pairs={{0,4},{4,8},{8,12},{12,16},{16,20},{20,24},{24,28},{1,5},{5,9},{9,... | collective-permute-start | bytes 786440 | tf_op jit(solution)/shard_map/ppermute | solution.py:430
  22.4 5.6 %collective-permute-start.3 = (f32[32,8,128]{2,1,0:T(8,128)S(1)}, f32[32,8,128]{2,1,0:T(8,128)S(1)}, u32[]{:S(2)}, u32[]{:S(2)}) collective-permute-start(f32[32,8,128]{2,1,0:T(8,128)S(1)} %add_bitcast_fusion), channel_id=1, source_target_pairs={{0,4},{4,0},{8,12},{12,8},{16,20},{20,16},{24,28},{28,24},{1,5},{5... | collective-permute-start | bytes 393224 | tf_op jit(solution)/shard_map/ppermute | solution.py:425
  22.4 6.3 %collective-permute-start.4 = (f32[8,4096]{1,0:T(8,128)S(1)}, f32[8,4096]{1,0:T(8,128)S(1)}, u32[]{:S(2)}, u32[]{:S(2)}) collective-permute-start(f32[8,4096]{1,0:T(8,128)S(1)} %get-tuple-element.56.up_ref), channel_id=1, source_target_pairs={{0,1},{1,2},{2,3},{4,5},{5,6},{6,7},{8,9},{9,10},{10,11},{12,13},{... | collective-permute-start | bytes 393224 | tf_op jit(solution)/shard_map/ppermute | solution.py:430
  24.3 6.1 %collective-permute-start.5 = (f32[8,4096]{1,0:T(8,128)S(1)}, f32[8,4096]{1,0:T(8,128)S(1)}, u32[]{:S(2)}, u32[]{:S(2)}) collective-permute-start(f32[8,4096]{1,0:T(8,128)S(1)} %get-tuple-element.57.down_ref), channel_id=1, source_target_pairs={{1,0},{2,1},{3,2},{5,4},{6,5},{7,6},{9,8},{10,9},{11,10},{13,12},{... | collective-permute-start | bytes 393224 | tf_op jit(solution)/shard_map/ppermute | solution.py:430
  30.5 10.0 %collective-permute-start.7 = (f32[64,8,128]{2,1,0:T(8,128)S(1)}, f32[64,8,128]{2,1,0:T(8,128)S(1)}, u32[]{:S(2)}, u32[]{:S(2)}) collective-permute-start(f32[64,8,128]{2,1,0:T(8,128)S(1)} %get-tuple-element.66), channel_id=1, source_target_pairs={{4,0},{8,4},{12,8},{16,12},{20,16},{24,20},{28,24},{5,1},{9,5},{13... | collective-permute-start | bytes 786440 | tf_op jit(solution)/shard_map/ppermute | solution.py:430
  34.4 5.0 %collective-permute-start.6 = (f32[32,8,128]{2,1,0:T(8,128)S(1)}, f32[32,8,128]{2,1,0:T(8,128)S(1)}, u32[]{:S(2)}, u32[]{:S(2)}) collective-permute-start(f32[32,8,128]{2,1,0:T(8,128)S(1)} %bitcast_add_fusion), channel_id=1, source_target_pairs={{0,8},{4,12},{8,0},{12,4},{16,24},{20,28},{24,16},{28,20},{1,9},{5... | collective-permute-start | bytes 393224 | tf_op jit(solution)/shard_map/ppermute | solution.py:425
  40.5 10.9 %collective-permute-start.8 = (f32[32,8,128]{2,1,0:T(8,128)S(1)}, f32[32,8,128]{2,1,0:T(8,128)S(1)}, u32[]{:S(2)}, u32[]{:S(2)}) collective-permute-start(f32[32,8,128]{2,1,0:T(8,128)S(1)} %add.42), channel_id=1, source_target_pairs={{0,16},{4,20},{8,24},{12,28},{16,0},{20,4},{24,8},{28,12},{1,17},{... | collective-permute-start | bytes 393224 | tf_op jit(solution)/shard_map/ppermute | solution.py:425
  45.5 6.1 %collective-permute-start.9 = (f32[16,8,128]{2,1,0:T(8,128)S(1)}, f32[16,8,128]{2,1,0:T(8,128)S(1)}, u32[]{:S(2)}, u32[]{:S(2)}) collective-permute-start(f32[16,8,128]{2,1,0:T(8,128)S(1)} %get-tuple-element.71), channel_id=1, source_target_pairs={{0,4},{4,8},{8,12},{12,16},{16,20},{20,24},{24,28},{1,5},{5,9},{9,... | collective-permute-start | bytes 196616 | tf_op jit(solution)/shard_map/ppermute | solution.py:430
  48.5 7.1 %collective-permute-start.10 = (f32[16,8,128]{2,1,0:T(8,128)S(1)}, f32[16,8,128]{2,1,0:T(8,128)S(1)}, u32[]{:S(2)}, u32[]{:S(2)}) collective-permute-start(f32[16,8,128]{2,1,0:T(8,128)S(1)} %get-tuple-element.72), channel_id=1, source_target_pairs={{4,0},{8,4},{12,8},{16,12},{20,16},{24,20},{28,24},{5,1},{9,5},{13... | collective-permute-start | bytes 196616 | tf_op jit(solution)/shard_map/ppermute | solution.py:430
  55.5 5.0 %collective-permute-start.11 = (f32[32,8,128]{2,1,0:T(8,128)S(1)}, f32[32,8,128]{2,1,0:T(8,128)S(1)}, u32[]{:S(2)}, u32[]{:S(2)}) collective-permute-start(f32[32,8,128]{2,1,0:T(8,128)S(1)} %add.43.mine_ref), channel_id=1, source_target_pairs={{0,4},{4,0},{8,12},{12,8},{16,20},{20,16},{24,28},{28,24},{1,5},{5... | collective-permute-start | bytes 393224 | tf_op jit(solution)/shard_map/ppermute | solution.py:425

commit v10 on v9

--- a/solution.py
+++ b/solution.py
@@ -484,6 +484,8 @@
     )
     other, up, down, forth, back = lax.optimization_barrier((other, up, down, forth, back))
     forth = shifted(forth, "tm", 1)
+    above = shifted(up, ("pair", "core"), 1)
+    below = shifted(down, ("pair", "core"), -1)
     term = swapped(other, "pair", 1)
     field = lax.rem(lax.axis_index("tm"), 2)
 
@@ -491,12 +493,9 @@
         return lax.dynamic_index_in_dim(array, index, 0, keepdims=False)
 
     half = chosen(own, 1 - field) + chosen(term, 1 - field)
-    half, forth = lax.optimization_barrier((half, forth))
-    half, up, down = lax.optimization_barrier((half, up, down))
+    half, forth, above, below, back = lax.optimization_barrier((half, forth, above, below, back))
+    back = shifted(back, "tm", -1)
     mine = chosen(own, field) + chosen(term, field) + swapped(half, "tm", 1)
-    above = shifted(up, ("pair", "core"), 1)
-    below = shifted(down, ("pair", "core"), -1)
-    mine, above, below, back = lax.optimization_barrier((mine, above, below, back))
     rows = (4 * columns // depth, depth, LANES)
     swept, edge, forth_edge, back_edge = vmem_call(
         functools.partial(second_kernel, steps, slabs),
@@ -504,16 +503,15 @@
         (place,),
         (first, up, down, above, below),
     )
-    back = shifted(back, "tm", -1)
+    mine, forth_edge, back_edge = lax.optimization_barrier((mine, forth_edge, back_edge))
+    forth_edge = shifted(forth_edge, "tm", 1)
+    back_edge = shifted(back_edge, "tm", -1)
     mask = 2
     while mask < ranks:
         if 2 * mask == ranks:
             mine, back, forth_edge, back_edge = lax.optimization_barrier((mine, back, forth_edge, back_edge))
         mine = mine + swapped(mine, "tm", mask)
         mask *= 2
-    forth_edge = shifted(forth_edge, "tm", 1)
-    back_edge = shifted(back_edge, "tm", -1)
-    mine, forth_edge, back_edge = lax.optimization_barrier((mine, forth_edge, back_edge))
     given = swapped(mine, "tm", 1)
     (coarse,) = vmem_call(
         last_kernel,

time: 62.1 us -> 61.4 us (0.989)
  the two profiles are of different devices: /device:TPU:6 before, /device:TPU:2 now
where the time goes in v10:
time: 61.4 us; the launch traced here: 61.1 us
  starting transfers between devices  24.2 us (39%)
  waiting for transfers between devices  20.2 us (33%)
  Pallas kernels  13.9 us (23%)
  other arithmetic  1.97 us (3%)
  between operations  0.8 us (1%)
    ppermute x6, starting transfers between devices, shifted(): lax.ppermute(value, axis, [(i, i + by) for i in range(size) if 0 <= i + b...  16.5 us
    pallas_call x6, Pallas kernels, vmem_call(): pl.pallas_call(kernel, out_shape=out_shape, in_specs=[smem] * len(smem_in...  13.9 us
    ppermute x5, waiting for transfers between devices, swapped(): lax.ppermute(value, axis, [(i, i ^ mask) for i in range(lax.axis_size(axi...  12.5 us
    ppermute x5, starting transfers between devices, swapped(): lax.ppermute(value, axis, [(i, i ^ mask) for i in range(lax.axis_size(axi...  7.7 us
    ppermute x6, waiting for transfers between devices, shifted(): lax.ppermute(value, axis, [(i, i + by) for i in range(size) if 0 <= i + b...  6.38 us
    ppermute x1, waiting for transfers between devices, local(): received = lax.ppermute(send, 'core', [(0, 1), (1, 0)])  1.37 us
  transfers between devices with their start and end apart: 12, of which 7 were waited for; matrix products, arithmetic and copies ran while one was open for 3% of the time, Pallas kernels for 5%

profile of v10, /device:TPU:2, one launch (start us, length us, event | category | flops | bytes accessed | tf_op | source)
XLA Modules:
  0.0 61.1 jit_solution(11274991731848104902)
XLA Ops:
  0.7 7.8 %shard_map.50 = (f32[2,2,32,8,128]{4,3,2,1,0:T(8,128)S(1)}, f32[2,2,32,8,128]{4,3,2,1,0:T(8,128)S(1)}) custom-call(s32[3]{0:T(128)S(1)} %pad_add_fusion.place_ref, f32[8,88,128]{2,1,0:T(8,128)} %constant.35.clone.weights_hbm, f32[2,2,8,4096]{3,2,1,0:T(8,128)} %iterate_ref.2, f32[2,2,8,4096]{3,2,1,0:T(8,128)} %forcing_ref.2), custom_call_target="tpu_custom_call" | custom-call | flops 1000000 | bytes 25165824 | tf_op jit(solution)/shard_map/pallas_call | solution.py:204
  8.7 0.5 shard_map.51
  9.2 1.4 %collective-permute-done.received_any = f32[2,2,32,8,128]{4,3,2,1,0:T(8,128)S(1)} collective-permute-done((f32[2,2,32,8,128]{4,3,2,1,0:T(8,128)S(1)}, f32[2,2,32,8,128]{4,3,2,1,0:T(8,128)S(1)}, u32[]{:S(2)}, u32[]{:S(2)}) %collective-permute-start) | collective-permute-done | bytes 524320 | tf_op jit(solution)/shard_map/ppermute | solution.py:467
  10.5 1.3 %shard_map.52 = (f32[2,32,8,128]{3,2,1,0:T(8,128)S(1)}, f32[2,32,8,128]{3,2,1,0:T(8,128)S(1)}) custom-call(s32[3]{0:T(128)S(1)} %pad_add_fusion.place_ref, f32[2,2,32,8,128]{4,3,2,1,0:T(8,128)S(1)} %get-tuple-element.39.keep_ref, f32[2,2,32,8,128]{4,3,2,1,0:T(8,128)S(1)} %collective-permute-done.received_any), custom_call_target="tpu_custom_call" | custom-call | flops 1000000 | bytes 1048576 | tf_op jit(solution)/shard_map/pallas_call | solution.py:204
  11.9 3.9 %collective-permute-start.2 = (f32[64,8,128]{2,1,0:T(8,128)S(1)}, f32[64,8,128]{2,1,0:T(8,128)S(1)}, u32[]{:S(2)}, u32[]{:S(2)}) collective-permute-start(f32[64,8,128]{2,1,0:T(8,128)S(1)} %get-tuple-element.50), channel_id=1, source_target_pairs={{0,4},{4,8},{8,12},{12,16},{16,20},{20,24},{24,28},{1,5},{5,9},{9,... | collective-permute-start | bytes 786440 | tf_op jit(solution)/shard_map/ppermute | solution.py:430
  15.9 1.9 %collective-permute-start.3 = (f32[8,4096]{1,0:T(8,128)S(1)}, f32[8,4096]{1,0:T(8,128)S(1)}, u32[]{:S(2)}, u32[]{:S(2)}) collective-permute-start(f32[8,4096]{1,0:T(8,128)S(1)} %get-tuple-element.46.up_ref), channel_id=1, source_target_pairs={{0,1},{1,2},{2,3},{4,5},{5,6},{6,7},{8,9},{9,10},{10,11},{12,13},{... | collective-permute-start | bytes 393224 | tf_op jit(solution)/shard_map/ppermute | solution.py:430
  17.8 3.6 %collective-permute-start.4 = (f32[8,4096]{1,0:T(8,128)S(1)}, f32[8,4096]{1,0:T(8,128)S(1)}, u32[]{:S(2)}, u32[]{:S(2)}) collective-permute-start(f32[8,4096]{1,0:T(8,128)S(1)} %get-tuple-element.47.down_ref), channel_id=1, source_target_pairs={{1,0},{2,1},{3,2},{5,4},{6,5},{7,6},{9,8},{10,9},{11,10},{13,12},{... | collective-permute-start | bytes 393224 | tf_op jit(solution)/shard_map/ppermute | solution.py:430
  21.5 0.9 %add_bitcast_fusion = f32[32,8,128]{2,1,0:T(8,128)S(1)} fusion(f32[2,32,8,128]{3,2,1,0:T(8,128)} %collective-permute-done.1, s32[]{:T(128)S(6)} %select_n.9, f32[2,32,8,128]{3,2,1,0:T(8,128)S(1)} %get-tuple-element.48), kind=kLoop, calls=%fused_computation.1 | loop fusion | flops 32768 | bytes 393220 | tf_op jit(solution)/shard_map/add | solution.py:495
  22.4 1.5 %collective-permute-done.4.below_ref = f32[8,4096]{1,0:T(8,128)S(1)} collective-permute-done((f32[8,4096]{1,0:T(8,128)S(1)}, f32[8,4096]{1,0:T(8,128)S(1)}, u32[]{:S(2)}, u32[]{:S(2)}) %collective-permute-start.4) | collective-permute-done | bytes 131104 | tf_op jit(solution)/shard_map/ppermute | solution.py:430
  24.0 1.5 %collective-permute-start.5 = (f32[32,8,128]{2,1,0:T(8,128)S(1)}, f32[32,8,128]{2,1,0:T(8,128)S(1)}, u32[]{:S(2)}, u32[]{:S(2)}) collective-permute-start(f32[32,8,128]{2,1,0:T(8,128)S(1)} %add_bitcast_fusion), channel_id=1, source_target_pairs={{0,4},{4,0},{8,12},{12,8},{16,20},{20,16},{24,28},{28,24},{1,5},{5... | collective-permute-start | bytes 393224 | tf_op jit(solution)/shard_map/ppermute | solution.py:425
  25.5 1.3 %collective-permute-start.7 = (f32[64,8,128]{2,1,0:T(8,128)S(1)}, f32[64,8,128]{2,1,0:T(8,128)S(1)}, u32[]{:S(2)}, u32[]{:S(2)}) collective-permute-start(f32[64,8,128]{2,1,0:T(8,128)S(1)} %get-tuple-element.61), channel_id=1, source_target_pairs={{4,0},{8,4},{12,8},{16,12},{20,16},{24,20},{28,24},{5,1},{9,5},{13... | collective-permute-start | bytes 786440 | tf_op jit(solution)/shard_map/ppermute | solution.py:430
  26.8 0.8 %shard_map.53 = (f32[2,2,8,4096]{3,2,1,0:T(8,128)S(1)}, f32[8,4096]{1,0:T(8,128)S(1)}, f32[16,8,128]{2,1,0:T(8,128)S(1)}, f32[16,8,128]{2,1,0:T(8,128)S(1)}) custom-call(s32[3]{0:T(128)S(1)} %pad_add_fusion.place_ref, f32[2,2,8,4096]{3,2,1,0:T(8,128)S(1)} %get-tuple-element.38.first_ref, f32[8,4096]{1,0:T(8,128)S(1)} %get-tuple-element.46.up_ref, ...), custom_call_target="tpu_custom_call" | custom-call | flops 1000000 | bytes 1048576 | tf_op jit(solution)/shard_map/pallas_call | solution.py:204
  27.6 2.6 %collective-permute-done.5 = f32[32,8,128]{2,1,0:T(8,128)S(1)} collective-permute-done((f32[32,8,128]{2,1,0:T(8,128)S(1)}, f32[32,8,128]{2,1,0:T(8,128)S(1)}, u32[]{:S(2)}, u32[]{:S(2)}) %collective-permute-start.5) | collective-permute-done | bytes 131104 | tf_op jit(solution)/shard_map/ppermute | solution.py:425
  30.3 0.9 %bitcast_add_fusion = f32[32,8,128]{2,1,0:T(8,128)S(1)} fusion(f32[32,8,128]{2,1,0:T(8,128)S(1)} %collective-permute-done.5, f32[2,32,8,128]{3,2,1,0:T(8,128)} %collective-permute-done.1, s32[]{:T(128)S(6)} %select_n.10, f32[2,32,8,128]{3,2,1,0:T(8,128)S(1)} %get-tuple-element.48), kind=kLoop, calls=%fused_computation | loop fusion | flops 65536 | bytes 524292 | tf_op jit(solution)/shard_map/add | solution.py:498
  31.2 5.7 %collective-permute-start.6 = (f32[32,8,128]{2,1,0:T(8,128)S(1)}, f32[32,8,128]{2,1,0:T(8,128)S(1)}, u32[]{:S(2)}, u32[]{:S(2)}) collective-permute-start(f32[32,8,128]{2,1,0:T(8,128)S(1)} %bitcast_add_fusion), channel_id=1, source_target_pairs={{0,8},{4,12},{8,0},{12,4},{16,24},{20,28},{24,16},{28,20},{1,9},{5... | collective-permute-start | bytes 393224 | tf_op jit(solution)/shard_map/ppermute | solution.py:425
  36.9 4.4 %collective-permute-start.8 = (f32[16,8,128]{2,1,0:T(8,128)S(1)}, f32[16,8,128]{2,1,0:T(8,128)S(1)}, u32[]{:S(2)}, u32[]{:S(2)}) collective-permute-start(f32[16,8,128]{2,1,0:T(8,128)S(1)} %get-tuple-element.62), channel_id=1, source_target_pairs={{0,4},{4,8},{8,12},{12,16},{16,20},{20,24},{24,28},{1,5},{5,9},{9,... | collective-permute-start | bytes 196616 | tf_op jit(solution)/shard_map/ppermute | solution.py:430
  41.3 1.3 %collective-permute-start.9 = (f32[16,8,128]{2,1,0:T(8,128)S(1)}, f32[16,8,128]{2,1,0:T(8,128)S(1)}, u32[]{:S(2)}, u32[]{:S(2)}) collective-permute-start(f32[16,8,128]{2,1,0:T(8,128)S(1)} %get-tuple-element.63), channel_id=1, source_target_pairs={{4,0},{8,4},{12,8},{16,12},{20,16},{24,20},{28,24},{5,1},{9,5},{13... | collective-permute-start | bytes 196616 | tf_op jit(solution)/shard_map/ppermute | solution.py:430
  42.6 0.6 collective-permute-done.8.forth_edge_ref
  43.1 4.3 %collective-permute-done.9.back_edge_ref = f32[16,8,128]{2,1,0:T(8,128)S(1)} collective-permute-done((f32[16,8,128]{2,1,0:T(8,128)S(1)}, f32[16,8,128]{2,1,0:T(8,128)S(1)}, u32[]{:S(2)}, u32[]{:S(2)}) %collective-permute-start.9) | collective-permute-done | bytes 65568 | tf_op jit(solution)/shard_map/ppermute | solution.py:430
  47.4 7.3 %collective-permute-done.10 = f32[32,8,128]{2,1,0:T(8,128)S(1)} collective-permute-done((f32[32,8,128]{2,1,0:T(8,128)S(1)}, f32[32,8,128]{2,1,0:T(8,128)S(1)}, u32[]{:S(2)}, u32[]{:S(2)}) %collective-permute-start.10) | collective-permute-done | bytes 131104 | tf_op jit(solution)/shard_map/ppermute | solution.py:425
  54.7 0.4 collective-permute-start.11
  55.2 2.0 %shard_map.54 = f32[2,2,8,4096]{3,2,1,0:T(8,128)} custom-call(s32[3]{0:T(128)S(1)} %pad_add_fusion.place_ref, f32[2,2,8,4096]{3,2,1,0:T(8,128)S(1)} %copy-done, f32[2,2,8,4096]{3,2,1,0:T(8,128)S(1)} %copy-done.1, f32[2,2,8,4096]{3,2,1,0:T(8,128)S(1)} %get-tuple-element.54.swept_ref, f32[8,4096]{1,0:T(8,128)S(1)} %get-tuple-element.55.edge_ref, ...), custom_call_target="tpu_custom_call" | custom-call | flops 1000000 | bytes 8388608 | tf_op jit(solution)/shard_map/pallas_call | solution.py:204
  57.2 2.6 %collective-permute-done.11.given_ref = f32[32,8,128]{2,1,0:T(8,128)S(1)} collective-permute-done((f32[32,8,128]{2,1,0:T(8,128)S(1)}, f32[32,8,128]{2,1,0:T(8,128)S(1)}, u32[]{:S(2)}, u32[]{:S(2)}) %collective-permute-start.11) | collective-permute-done | bytes 131104 | tf_op jit(solution)/shard_map/ppermute | solution.py:425
  59.8 1.4 %shard_map.55 = f32[2,2,8,4096]{3,2,1,0:T(8,128)} custom-call(s32[3]{0:T(128)S(1)} %pad_add_fusion.place_ref, f32[32,8,128]{2,1,0:T(8,128)S(1)} %add.43.mine_ref, f32[32,8,128]{2,1,0:T(8,128)S(1)} %collective-permute-done.11.given_ref), custom_call_target="tpu_custom_call" | custom-call | flops 1000000 | bytes 1048576 | tf_op jit(solution)/shard_map/pallas_call | solution.py:204
  (15 shorter events, 0.3 us)
Async XLA Ops:
  0.7 7.9 %copy-start = (f32[2,2,8,4096]{3,2,1,0:T(8,128)S(1)}, f32[2,2,8,4096]{3,2,1,0:T(8,128)}, u32[]{:S(2)}) copy-start(f32[2,2,8,4096]{3,2,1,0:T(8,128)} %iterate_ref.2) | copy-start | bytes 1572868
  0.7 7.9 %copy-start.1 = (f32[2,2,8,4096]{3,2,1,0:T(8,128)S(1)}, f32[2,2,8,4096]{3,2,1,0:T(8,128)}, u32[]{:S(2)}) copy-start(f32[2,2,8,4096]{3,2,1,0:T(8,128)} %forcing_ref.2) | copy-start | bytes 1572868
  8.6 2.0 %collective-permute-start = (f32[2,2,32,8,128]{4,3,2,1,0:T(8,128)S(1)}, f32[2,2,32,8,128]{4,3,2,1,0:T(8,128)S(1)}, u32[]{:S(2)}, u32[]{:S(2)}) collective-permute-start(f32[2,2,32,8,128]{4,3,2,1,0:T(8,128)S(1)} %get-tuple-element.40), channel_id=1, source_target_pairs={{0,1},{1,0},{2,3},{3,2},{4,5},{5,4},{6,7},{7,6},{8,9},{9,8},{10,11... | collective-permute-start | bytes 1572872 | tf_op jit(solution)/shard_map/ppermute | solution.py:467
  11.9 9.6 %collective-permute-start.1 = (f32[2,32,8,128]{3,2,1,0:T(8,128)S(1)}, f32[2,32,8,128]{3,2,1,0:T(8,128)}, u32[]{:S(2)}, u32[]{:S(2)}) collective-permute-start(f32[2,32,8,128]{3,2,1,0:T(8,128)S(1)} %get-tuple-element.49), channel_id=1, source_target_pairs={{0,2},{2,0},{1,3},{3,1},{4,6},{6,4},{5,7},{7,5},{8,10},{10,8},{9,1... | collective-permute-start | bytes 786440 | tf_op jit(solution)/shard_map/ppermute | solution.py:425
  11.9 12.0 %collective-permute-start.2 = (f32[64,8,128]{2,1,0:T(8,128)S(1)}, f32[64,8,128]{2,1,0:T(8,128)S(1)}, u32[]{:S(2)}, u32[]{:S(2)}) collective-permute-start(f32[64,8,128]{2,1,0:T(8,128)S(1)} %get-tuple-element.50), channel_id=1, source_target_pairs={{0,4},{4,8},{8,12},{12,16},{16,20},{20,24},{24,28},{1,5},{5,9},{9,... | collective-permute-start | bytes 786440 | tf_op jit(solution)/shard_map/ppermute | solution.py:430
  15.9 6.5 %collective-permute-start.3 = (f32[8,4096]{1,0:T(8,128)S(1)}, f32[8,4096]{1,0:T(8,128)S(1)}, u32[]{:S(2)}, u32[]{:S(2)}) collective-permute-start(f32[8,4096]{1,0:T(8,128)S(1)} %get-tuple-element.46.up_ref), channel_id=1, source_target_pairs={{0,1},{1,2},{2,3},{4,5},{5,6},{6,7},{8,9},{9,10},{10,11},{12,13},{... | collective-permute-start | bytes 393224 | tf_op jit(solution)/shard_map/ppermute | solution.py:430
  17.8 6.1 %collective-permute-start.4 = (f32[8,4096]{1,0:T(8,128)S(1)}, f32[8,4096]{1,0:T(8,128)S(1)}, u32[]{:S(2)}, u32[]{:S(2)}) collective-permute-start(f32[8,4096]{1,0:T(8,128)S(1)} %get-tuple-element.47.down_ref), channel_id=1, source_target_pairs={{1,0},{2,1},{3,2},{5,4},{6,5},{7,6},{9,8},{10,9},{11,10},{13,12},{... | collective-permute-start | bytes 393224 | tf_op jit(solution)/shard_map/ppermute | solution.py:430
  24.0 6.3 %collective-permute-start.5 = (f32[32,8,128]{2,1,0:T(8,128)S(1)}, f32[32,8,128]{2,1,0:T(8,128)S(1)}, u32[]{:S(2)}, u32[]{:S(2)}) collective-permute-start(f32[32,8,128]{2,1,0:T(8,128)S(1)} %add_bitcast_fusion), channel_id=1, source_target_pairs={{0,4},{4,0},{8,12},{12,8},{16,20},{20,16},{24,28},{28,24},{1,5},{5... | collective-permute-start | bytes 393224 | tf_op jit(solution)/shard_map/ppermute | solution.py:425
  25.5 21.9 %collective-permute-start.7 = (f32[64,8,128]{2,1,0:T(8,128)S(1)}, f32[64,8,128]{2,1,0:T(8,128)S(1)}, u32[]{:S(2)}, u32[]{:S(2)}) collective-permute-start(f32[64,8,128]{2,1,0:T(8,128)S(1)} %get-tuple-element.61), channel_id=1, source_target_pairs={{4,0},{8,4},{12,8},{16,12},{20,16},{24,20},{28,24},{5,1},{9,5},{13... | collective-permute-start | bytes 786440 | tf_op jit(solution)/shard_map/ppermute | solution.py:430
  31.2 11.4 %collective-permute-start.6 = (f32[32,8,128]{2,1,0:T(8,128)S(1)}, f32[32,8,128]{2,1,0:T(8,128)S(1)}, u32[]{:S(2)}, u32[]{:S(2)}) collective-permute-start(f32[32,8,128]{2,1,0:T(8,128)S(1)} %bitcast_add_fusion), channel_id=1, source_target_pairs={{0,8},{4,12},{8,0},{12,4},{16,24},{20,28},{24,16},{28,20},{1,9},{5... | collective-permute-start | bytes 393224 | tf_op jit(solution)/shard_map/ppermute | solution.py:425
  36.9 6.3 %collective-permute-start.8 = (f32[16,8,128]{2,1,0:T(8,128)S(1)}, f32[16,8,128]{2,1,0:T(8,128)S(1)}, u32[]{:S(2)}, u32[]{:S(2)}) collective-permute-start(f32[16,8,128]{2,1,0:T(8,128)S(1)} %get-tuple-element.62), channel_id=1, source_target_pairs={{0,4},{4,8},{8,12},{12,16},{16,20},{20,24},{24,28},{1,5},{5,9},{9,... | collective-permute-start | bytes 196616 | tf_op jit(solution)/shard_map/ppermute | solution.py:430
  41.3 6.2 %collective-permute-start.9 = (f32[16,8,128]{2,1,0:T(8,128)S(1)}, f32[16,8,128]{2,1,0:T(8,128)S(1)}, u32[]{:S(2)}, u32[]{:S(2)}) collective-permute-start(f32[16,8,128]{2,1,0:T(8,128)S(1)} %get-tuple-element.63), channel_id=1, source_target_pairs={{4,0},{8,4},{12,8},{16,12},{20,16},{24,20},{28,24},{5,1},{9,5},{13... | collective-permute-start | bytes 196616 | tf_op jit(solution)/shard_map/ppermute | solution.py:430
  47.4 7.3 %collective-permute-start.10 = (f32[32,8,128]{2,1,0:T(8,128)S(1)}, f32[32,8,128]{2,1,0:T(8,128)S(1)}, u32[]{:S(2)}, u32[]{:S(2)}) collective-permute-start(f32[32,8,128]{2,1,0:T(8,128)S(1)} %add.42), channel_id=1, source_target_pairs={{0,16},{4,20},{8,24},{12,28},{16,0},{20,4},{24,8},{28,12},{1,17},{... | collective-permute-start | bytes 393224 | tf_op jit(solution)/shard_map/ppermute | solution.py:425
  54.7 5.0 %collective-permute-start.11 = (f32[32,8,128]{2,1,0:T(8,128)S(1)}, f32[32,8,128]{2,1,0:T(8,128)S(1)}, u32[]{:S(2)}, u32[]{:S(2)}) collective-permute-start(f32[32,8,128]{2,1,0:T(8,128)S(1)} %add.43.mine_ref), channel_id=1, source_target_pairs={{0,4},{4,0},{8,12},{12,8},{16,20},{20,16},{24,28},{28,24},{1,5},{5... | collective-permute-start | bytes 393224 | tf_op jit(solution)/shard_map/ppermute | solution.py:425

commit v11 on v7

--- a/solution.py
+++ b/solution.py
@@ -486,10 +486,11 @@
     while mask < ranks:
         mine = mine + swapped(mine, "tm", mask)
         mask *= 2
+    forth = shifted(forth, "tm", 1)
+    back = shifted(back, "tm", -1)
+    mine, forth, back = lax.optimization_barrier((mine, forth, back))
     given = swapped(mine, "tm", 1)
     (coarse,) = vmem_call(last_kernel, (iterate.shape,), (place,), (mine, given))
-    forth = shifted(forth, "tm", 1)
-    back = shifted(back, "tm", -1)
     (smoothed,) = vmem_call(
         functools.partial(third_kernel, steps, ranks),
         (iterate.shape,),

time: 57.6 us -> 58.6 us (1.017)
  waiting for transfers between devices: 23.2 us -> 24.3 us
    ppermute x4, starting transfers between devices: 7.77 us -> 6.58 us  [shifted(): lax.ppermute(value, axis, [(i, i + by) for i in range(size) if 0 <= i + b...]
    ppermute x5, waiting for transfers between devices: 22.1 us -> 23.3 us  [swapped(): lax.ppermute(value, axis, [(i, i ^ mask) for i in range(lax.axis_size(axi...]
    ppermute x5, starting transfers between devices: 11.2 us -> 12.3 us  [swapped(): lax.ppermute(value, axis, [(i, i ^ mask) for i in range(lax.axis_size(axi...]
where the time goes in v11:
time: 58.6 us; the launch traced here: 58.4 us
  waiting for transfers between devices  24.3 us (41%)
  starting transfers between devices  19.4 us (33%)
  Pallas kernels  13.8 us (24%)
  between operations  0.77 us (1%)
    ppermute x5, waiting for transfers between devices, swapped(): lax.ppermute(value, axis, [(i, i ^ mask) for i in range(lax.axis_size(axi...  23.3 us
    pallas_call x6, Pallas kernels, vmem_call(): pl.pallas_call(kernel, out_shape=out_shape, in_specs=[smem] * len(smem_in...  13.8 us
    ppermute x5, starting transfers between devices, swapped(): lax.ppermute(value, axis, [(i, i ^ mask) for i in range(lax.axis_size(axi...  12.3 us
    ppermute x4, starting transfers between devices, shifted(): lax.ppermute(value, axis, [(i, i + by) for i in range(size) if 0 <= i + b...  6.58 us
  transfers between devices with their start and end apart: 10, of which 5 were waited for; matrix products, arithmetic and copies ran while one was open for 0% of the time, Pallas kernels for 6%

profile of v11, /device:TPU:0, one launch (start us, length us, event | category | flops | bytes accessed | tf_op | source)
XLA Modules:
  0.0 58.4 jit_solution(15968183005904342450)
XLA Ops:
  0.6 0.1 pad_add_fusion.place_ref
  0.7 7.8 %shard_map.50 = (f32[2,2,32,8,128]{4,3,2,1,0:T(8,128)S(1)}, f32[2,2,32,8,128]{4,3,2,1,0:T(8,128)S(1)}) custom-call(s32[3]{0:T(128)S(1)} %pad_add_fusion.place_ref, f32[8,88,128]{2,1,0:T(8,128)} %constant.35.clone.weights_hbm, f32[2,2,8,4096]{3,2,1,0:T(8,128)} %iterate_ref.4, f32[2,2,8,4096]{3,2,1,0:T(8,128)} %forcing_ref.2), custom_call_target="tpu_custom_call" | custom-call | flops 1000000 | bytes 25165824 | tf_op jit(solution)/shard_map/pallas_call | solution.py:205
  8.6 0.5 collective-permute-start
  9.1 0.5 shard_map.51
  9.6 1.0 %collective-permute-done.received_any = f32[2,2,32,8,128]{4,3,2,1,0:T(8,128)S(1)} collective-permute-done((f32[2,2,32,8,128]{4,3,2,1,0:T(8,128)S(1)}, f32[2,2,32,8,128]{4,3,2,1,0:T(8,128)S(1)}, u32[]{:S(2)}, u32[]{:S(2)}) %collective-permute-start) | collective-permute-done | bytes 524320 | tf_op jit(solution)/shard_map/ppermute | solution.py:451
  10.6 1.3 %shard_map.52 = (f32[2,32,8,128]{3,2,1,0:T(8,128)S(1)}, f32[2,32,8,128]{3,2,1,0:T(8,128)S(1)}) custom-call(s32[3]{0:T(128)S(1)} %pad_add_fusion.place_ref, f32[2,2,32,8,128]{4,3,2,1,0:T(8,128)S(1)} %get-tuple-element.30.keep_ref, f32[2,2,32,8,128]{4,3,2,1,0:T(8,128)S(1)} %collective-permute-done.received_any), custom_call_target="tpu_custom_call" | custom-call | flops 1000000 | bytes 1048576 | tf_op jit(solution)/shard_map/pallas_call | solution.py:205
  11.9 2.9 %collective-permute-start.1 = (f32[2,32,8,128]{3,2,1,0:T(8,128)S(1)}, f32[2,32,8,128]{3,2,1,0:T(8,128)S(1)}, u32[]{:S(2)}, u32[]{:S(2)}) collective-permute-start(f32[2,32,8,128]{3,2,1,0:T(8,128)S(1)} %get-tuple-element.38), channel_id=1, source_target_pairs={{0,2},{2,0},{1,3},{3,1},{4,6},{6,4},{5,7},{7,5},{8,10},{10,8},{9,1... | collective-permute-start | bytes 786440 | tf_op jit(solution)/shard_map/ppermute | solution.py:414
  14.9 1.8 %collective-permute-start.2 = (f32[8,4096]{1,0:T(8,128)S(1)}, f32[8,4096]{1,0:T(8,128)S(1)}, u32[]{:S(2)}, u32[]{:S(2)}) collective-permute-start(f32[8,4096]{1,0:T(8,128)S(1)} %get-tuple-element.35.up_ref), channel_id=1, source_target_pairs={{0,1},{1,2},{2,3},{4,5},{5,6},{6,7},{8,9},{9,10},{10,11},{12,13},{... | collective-permute-start | bytes 393224 | tf_op jit(solution)/shard_map/ppermute | solution.py:419
  16.6 1.3 %collective-permute-start.3 = (f32[8,4096]{1,0:T(8,128)S(1)}, f32[8,4096]{1,0:T(8,128)S(1)}, u32[]{:S(2)}, u32[]{:S(2)}) collective-permute-start(f32[8,4096]{1,0:T(8,128)S(1)} %get-tuple-element.36.down_ref), channel_id=1, source_target_pairs={{1,0},{2,1},{3,2},{5,4},{6,5},{7,6},{9,8},{10,9},{11,10},{13,12},{... | collective-permute-start | bytes 393224 | tf_op jit(solution)/shard_map/ppermute | solution.py:419
  17.9 3.6 %collective-permute-done.1 = f32[2,32,8,128]{3,2,1,0:T(8,128)S(1)} collective-permute-done((f32[2,32,8,128]{3,2,1,0:T(8,128)S(1)}, f32[2,32,8,128]{3,2,1,0:T(8,128)S(1)}, u32[]{:S(2)}, u32[]{:S(2)}) %collective-permute-start.1) | collective-permute-done | bytes 262176 | tf_op jit(solution)/shard_map/ppermute | solution.py:414
  21.6 0.0 collective-permute-done.2.above_ref
  21.6 0.0 collective-permute-done.3.below_ref
  21.6 1.8 %collective-permute-start.4 = (f32[32,8,128]{2,1,0:T(8,128)S(1)}, f32[32,8,128]{2,1,0:T(8,128)S(1)}, u32[]{:S(2)}, u32[]{:S(2)}) collective-permute-start(f32[32,8,128]{2,1,0:T(8,128)S(1)} %add_bitcast_fusion), channel_id=1, source_target_pairs={{0,4},{4,0},{8,12},{12,8},{16,20},{20,16},{24,28},{28,24},{1,5},{5... | collective-permute-start | bytes 393224 | tf_op jit(solution)/shard_map/ppermute | solution.py:414
  23.4 0.8 %shard_map.53 = (f32[2,2,8,4096]{3,2,1,0:T(8,128)S(1)}, f32[8,4096]{1,0:T(8,128)S(1)}, f32[72,8,128]{2,1,0:T(8,128)S(1)}, f32[72,8,128]{2,1,0:T(8,128)S(1)}) custom-call(s32[3]{0:T(128)S(1)} %pad_add_fusion.place_ref, f32[2,2,8,4096]{3,2,1,0:T(8,128)S(1)} %copy-done, f32[2,2,8,4096]{3,2,1,0:T(8,128)S(1)} %get-tuple-element.29.first_ref, ...), custom_call_target="tpu_custom_call" | custom-call | flops 1000000 | bytes 1048576 | tf_op jit(solution)/shard_map/pallas_call | solution.py:205
  24.2 2.2 %collective-permute-start.7 = (f32[72,8,128]{2,1,0:T(8,128)S(1)}, f32[72,8,128]{2,1,0:T(8,128)S(1)}, u32[]{:S(2)}, u32[]{:S(2)}) collective-permute-start(f32[72,8,128]{2,1,0:T(8,128)S(1)} %get-tuple-element.44), channel_id=1, source_target_pairs={{0,4},{4,8},{8,12},{12,16},{16,20},{20,24},{24,28},{1,5},{5,9},{9,... | collective-permute-start | bytes 884744 | tf_op jit(solution)/shard_map/ppermute | solution.py:419
  26.4 1.3 %collective-permute-start.8 = (f32[72,8,128]{2,1,0:T(8,128)S(1)}, f32[72,8,128]{2,1,0:T(8,128)S(1)}, u32[]{:S(2)}, u32[]{:S(2)}) collective-permute-start(f32[72,8,128]{2,1,0:T(8,128)S(1)} %get-tuple-element.45), channel_id=1, source_target_pairs={{4,0},{8,4},{12,8},{16,12},{20,16},{24,20},{28,24},{5,1},{9,5},{13... | collective-permute-start | bytes 884744 | tf_op jit(solution)/shard_map/ppermute | solution.py:419
  27.8 4.9 %collective-permute-start.5 = (f32[32,8,128]{2,1,0:T(8,128)S(1)}, f32[32,8,128]{2,1,0:T(8,128)S(1)}, u32[]{:S(2)}, u32[]{:S(2)}) collective-permute-start(f32[32,8,128]{2,1,0:T(8,128)S(1)} %bitcast_add_fusion), channel_id=1, source_target_pairs={{0,8},{4,12},{8,0},{12,4},{16,24},{20,28},{24,16},{28,20},{1,9},{5... | collective-permute-start | bytes 393224 | tf_op jit(solution)/shard_map/ppermute | solution.py:414
  32.6 10.3 %collective-permute-done.5 = f32[32,8,128]{2,1,0:T(8,128)S(1)} collective-permute-done((f32[32,8,128]{2,1,0:T(8,128)S(1)}, f32[32,8,128]{2,1,0:T(8,128)S(1)}, u32[]{:S(2)}, u32[]{:S(2)}) %collective-permute-start.5) | collective-permute-done | bytes 131104 | tf_op jit(solution)/shard_map/ppermute | solution.py:414
  43.0 2.7 %collective-permute-start.6 = (f32[32,8,128]{2,1,0:T(8,128)S(1)}, f32[32,8,128]{2,1,0:T(8,128)S(1)}, u32[]{:S(2)}, u32[]{:S(2)}) collective-permute-start(f32[32,8,128]{2,1,0:T(8,128)S(1)} %add.42), channel_id=1, source_target_pairs={{0,16},{4,20},{8,24},{12,28},{16,0},{20,4},{24,8},{28,12},{1,17},{... | collective-permute-start | bytes 393224 | tf_op jit(solution)/shard_map/ppermute | solution.py:414
  45.6 5.9 %collective-permute-done.6 = f32[32,8,128]{2,1,0:T(8,128)S(1)} collective-permute-done((f32[32,8,128]{2,1,0:T(8,128)S(1)}, f32[32,8,128]{2,1,0:T(8,128)S(1)}, u32[]{:S(2)}, u32[]{:S(2)}) %collective-permute-start.6) | collective-permute-done | bytes 131104 | tf_op jit(solution)/shard_map/ppermute | solution.py:414
  51.5 0.1 collective-permute-start.9
  51.6 1.9 %shard_map.54 = f32[2,2,8,4096]{3,2,1,0:T(8,128)} custom-call(s32[3]{0:T(128)S(1)} %pad_add_fusion.place_ref, f32[2,2,8,4096]{3,2,1,0:T(8,128)S(1)} %copy-done, f32[2,2,8,4096]{3,2,1,0:T(8,128)S(1)} %copy-done.1, f32[2,2,8,4096]{3,2,1,0:T(8,128)S(1)} %get-tuple-element.41.swept_ref, f32[8,4096]{1,0:T(8,128)S(1)} %get-tuple-element.42.edge_ref, ...), custom_call_target="tpu_custom_call" | custom-call | flops 1000000 | bytes 67108864 | tf_op jit(solution)/shard_map/pallas_call | solution.py:205
  53.6 3.5 %collective-permute-done.9.given_ref = f32[32,8,128]{2,1,0:T(8,128)S(1)} collective-permute-done((f32[32,8,128]{2,1,0:T(8,128)S(1)}, f32[32,8,128]{2,1,0:T(8,128)S(1)}, u32[]{:S(2)}, u32[]{:S(2)}) %collective-permute-start.9) | collective-permute-done | bytes 131104 | tf_op jit(solution)/shard_map/ppermute | solution.py:414
  57.1 1.4 %shard_map.55 = f32[2,2,8,4096]{3,2,1,0:T(8,128)} custom-call(s32[3]{0:T(128)S(1)} %pad_add_fusion.place_ref, f32[32,8,128]{2,1,0:T(8,128)S(1)} %add.43.mine_ref, f32[32,8,128]{2,1,0:T(8,128)S(1)} %collective-permute-done.9.given_ref), custom_call_target="tpu_custom_call" | custom-call | flops 1000000 | bytes 1048576 | tf_op jit(solution)/shard_map/pallas_call | solution.py:205
  (11 shorter events, 0.1 us)
Async XLA Ops:
  0.7 8.4 %copy-start = (f32[2,2,8,4096]{3,2,1,0:T(8,128)S(1)}, f32[2,2,8,4096]{3,2,1,0:T(8,128)}, u32[]{:S(2)}) copy-start(f32[2,2,8,4096]{3,2,1,0:T(8,128)} %iterate_ref.4) | copy-start | bytes 1572868
  0.7 8.4 %copy-start.1 = (f32[2,2,8,4096]{3,2,1,0:T(8,128)S(1)}, f32[2,2,8,4096]{3,2,1,0:T(8,128)}, u32[]{:S(2)}) copy-start(f32[2,2,8,4096]{3,2,1,0:T(8,128)} %forcing_ref.2) | copy-start | bytes 1572868
  8.6 2.1 %collective-permute-start = (f32[2,2,32,8,128]{4,3,2,1,0:T(8,128)S(1)}, f32[2,2,32,8,128]{4,3,2,1,0:T(8,128)S(1)}, u32[]{:S(2)}, u32[]{:S(2)}) collective-permute-start(f32[2,2,32,8,128]{4,3,2,1,0:T(8,128)S(1)} %get-tuple-element.31), channel_id=1, source_target_pairs={{0,1},{1,0},{2,3},{3,2},{4,5},{5,4},{6,7},{7,6},{8,9},{9,8},{10,11... | collective-permute-start | bytes 1572872 | tf_op jit(solution)/shard_map/ppermute | solution.py:451
  11.9 9.6 %collective-permute-start.1 = (f32[2,32,8,128]{3,2,1,0:T(8,128)S(1)}, f32[2,32,8,128]{3,2,1,0:T(8,128)S(1)}, u32[]{:S(2)}, u32[]{:S(2)}) collective-permute-start(f32[2,32,8,128]{3,2,1,0:T(8,128)S(1)} %get-tuple-element.38), channel_id=1, source_target_pairs={{0,2},{2,0},{1,3},{3,1},{4,6},{6,4},{5,7},{7,5},{8,10},{10,8},{9,1... | collective-permute-start | bytes 786440 | tf_op jit(solution)/shard_map/ppermute | solution.py:414
  14.9 6.7 %collective-permute-start.2 = (f32[8,4096]{1,0:T(8,128)S(1)}, f32[8,4096]{1,0:T(8,128)S(1)}, u32[]{:S(2)}, u32[]{:S(2)}) collective-permute-start(f32[8,4096]{1,0:T(8,128)S(1)} %get-tuple-element.35.up_ref), channel_id=1, source_target_pairs={{0,1},{1,2},{2,3},{4,5},{5,6},{6,7},{8,9},{9,10},{10,11},{12,13},{... | collective-permute-start | bytes 393224 | tf_op jit(solution)/shard_map/ppermute | solution.py:419
  16.6 4.9 %collective-permute-start.3 = (f32[8,4096]{1,0:T(8,128)S(1)}, f32[8,4096]{1,0:T(8,128)S(1)}, u32[]{:S(2)}, u32[]{:S(2)}) collective-permute-start(f32[8,4096]{1,0:T(8,128)S(1)} %get-tuple-element.36.down_ref), channel_id=1, source_target_pairs={{1,0},{2,1},{3,2},{5,4},{6,5},{7,6},{9,8},{10,9},{11,10},{13,12},{... | collective-permute-start | bytes 393224 | tf_op jit(solution)/shard_map/ppermute | solution.py:419
  21.6 6.2 %collective-permute-start.4 = (f32[32,8,128]{2,1,0:T(8,128)S(1)}, f32[32,8,128]{2,1,0:T(8,128)S(1)}, u32[]{:S(2)}, u32[]{:S(2)}) collective-permute-start(f32[32,8,128]{2,1,0:T(8,128)S(1)} %add_bitcast_fusion), channel_id=1, source_target_pairs={{0,4},{4,0},{8,12},{12,8},{16,20},{20,16},{24,28},{28,24},{1,5},{5... | collective-permute-start | bytes 393224 | tf_op jit(solution)/shard_map/ppermute | solution.py:414
  24.2 27.3 %collective-permute-start.7 = (f32[72,8,128]{2,1,0:T(8,128)S(1)}, f32[72,8,128]{2,1,0:T(8,128)S(1)}, u32[]{:S(2)}, u32[]{:S(2)}) collective-permute-start(f32[72,8,128]{2,1,0:T(8,128)S(1)} %get-tuple-element.44), channel_id=1, source_target_pairs={{0,4},{4,8},{8,12},{12,16},{16,20},{20,24},{24,28},{1,5},{5,9},{9,... | collective-permute-start | bytes 884744 | tf_op jit(solution)/shard_map/ppermute | solution.py:419
  26.4 25.1 %collective-permute-start.8 = (f32[72,8,128]{2,1,0:T(8,128)S(1)}, f32[72,8,128]{2,1,0:T(8,128)S(1)}, u32[]{:S(2)}, u32[]{:S(2)}) collective-permute-start(f32[72,8,128]{2,1,0:T(8,128)S(1)} %get-tuple-element.45), channel_id=1, source_target_pairs={{4,0},{8,4},{12,8},{16,12},{20,16},{24,20},{28,24},{5,1},{9,5},{13... | collective-permute-start | bytes 884744 | tf_op jit(solution)/shard_map/ppermute | solution.py:419
  27.8 15.2 %collective-permute-start.5 = (f32[32,8,128]{2,1,0:T(8,128)S(1)}, f32[32,8,128]{2,1,0:T(8,128)S(1)}, u32[]{:S(2)}, u32[]{:S(2)}) collective-permute-start(f32[32,8,128]{2,1,0:T(8,128)S(1)} %bitcast_add_fusion), channel_id=1, source_target_pairs={{0,8},{4,12},{8,0},{12,4},{16,24},{20,28},{24,16},{28,20},{1,9},{5... | collective-permute-start | bytes 393224 | tf_op jit(solution)/shard_map/ppermute | solution.py:414
  43.0 8.5 %collective-permute-start.6 = (f32[32,8,128]{2,1,0:T(8,128)S(1)}, f32[32,8,128]{2,1,0:T(8,128)S(1)}, u32[]{:S(2)}, u32[]{:S(2)}) collective-permute-start(f32[32,8,128]{2,1,0:T(8,128)S(1)} %add.42), channel_id=1, source_target_pairs={{0,16},{4,20},{8,24},{12,28},{16,0},{20,4},{24,8},{28,12},{1,17},{... | collective-permute-start | bytes 393224 | tf_op jit(solution)/shard_map/ppermute | solution.py:414
  51.5 5.5 %collective-permute-start.9 = (f32[32,8,128]{2,1,0:T(8,128)S(1)}, f32[32,8,128]{2,1,0:T(8,128)S(1)}, u32[]{:S(2)}, u32[]{:S(2)}) collective-permute-start(f32[32,8,128]{2,1,0:T(8,128)S(1)} %add.43.mine_ref), channel_id=1, source_target_pairs={{0,4},{4,0},{8,12},{12,8},{16,20},{20,16},{24,28},{28,24},{1,5},{5... | collective-permute-start | bytes 393224 | tf_op jit(solution)/shard_map/ppermute | solution.py:414

commit v12 on v11

--- a/solution.py
+++ b/solution.py
@@ -340,15 +340,14 @@
                 swept_ref[f, n, :, one(j)] = value
                 for ref, field, step in ((forth_ref, 0, steps - 1), (back_ref, 1, 0)):
                     if (f, n) == (field, step):
-                        ref[j] = iterate_ref[f, n, :, one(j)]
-                        ref[columns + j] = value
-                        block, row = 2 * columns + j // depth, j % depth
+                        ref[j] = value
+                        block, row = columns + j // depth, j % depth
                         ref[block, row : row + 1] = from_above[k : k + 1]
                         block += columns // depth
                         ref[block, row : row + 1] = from_below[k : k + 1]
 
 
-def third_kernel(steps, ranks, place_ref, iterate_ref, forcing_ref, swept_ref, edge_ref, forth_ref, back_ref, out_ref):
+def third_kernel(steps, ranks, place_ref, iterate_ref, forcing_ref, swept_ref, edge_ref, last_ref, next_ref, forth_ref, back_ref, out_ref):
     _, _, _, along, across = level_terms(0)
     depth, cells = iterate_ref.shape[2:]
     columns = cells // LANES
@@ -364,7 +363,7 @@
     def loaded(j):
         if j >= columns:
             return {s: zero for s in slots}
-        near = {"forth": forth_ref[j], "back": back_ref[j]}
+        near = {"forth": last_ref[:, column(j)], "back": next_ref[:, column(j)]}
         values = {}
         for s in slots:
             values[s] = swept_ref[s[0], s[1], :, column(j)]
@@ -373,7 +372,7 @@
         return values
 
     def edges(j, side):
-        block, row = 2 * columns + side * (columns // depth) + j // depth, j % depth
+        block, row = columns + side * (columns // depth) + j // depth, j % depth
         near = {"forth": forth_ref[block, row : row + 1], "back": back_ref[block, row : row + 1]}
         values = {}
         for s in slots:
@@ -395,8 +394,8 @@
             above = jnp.where(sublane == 0, over[s], pltpu.roll(now[s], 1, 0))
             below = jnp.where(sublane == depth - 1, under[s], pltpu.roll(now[s], depth - 1, 0))
             around[s] = across_rows + beside(now[s], lane) + (above + below)
-        before = (forth_ref[columns + j] - across * iterate_ref[1, 0, :, column(j)]) * has_before
-        after = (back_ref[columns + j] + across * iterate_ref[0, steps - 1, :, column(j)]) * has_after
+        before = (forth_ref[j] - across * iterate_ref[1, 0, :, column(j)]) * has_before
+        after = (back_ref[j] + across * iterate_ref[0, steps - 1, :, column(j)]) * has_after
         for n in range(steps):
             values = relaxed(
                 (now[0, n], now[1, n]),
@@ -472,9 +471,11 @@
         return lax.dynamic_index_in_dim(array, index, 0, keepdims=False)
 
     half = chosen(own, 1 - field) + chosen(term, 1 - field)
-    half, above, below = lax.optimization_barrier((half, above, below))
+    last = shifted(iterate_after[0, -1], "tm", 1)
+    following = shifted(iterate_after[1, 0], "tm", -1)
+    half, above, below, last, following = lax.optimization_barrier((half, above, below, last, following))
     mine = chosen(own, field) + chosen(term, field) + swapped(half, "tm", 1)
-    payload = (2 * columns + 2 * columns // depth, depth, LANES)
+    payload = (columns + 2 * columns // depth, depth, LANES)
     swept, edge, forth, back = vmem_call(
         functools.partial(second_kernel, steps, slabs),
         (iterate.shape, (4 * steps, cells), payload, payload),
@@ -495,7 +496,7 @@
         functools.partial(third_kernel, steps, ranks),
         (iterate.shape,),
         (place,),
-        (iterate, forcing, swept, edge, forth, back),
+        (iterate, forcing, swept, edge, last, following, forth, back),
         cost=64 * 2**20,
     )
     return smoothed, coarse

time: 58.6 us -> 56.4 us (0.962)
  waiting for transfers between devices: 24.3 us -> 14.8 us
  starting transfers between devices: 19.4 us -> 26.6 us
    ppermute x5, waiting for transfers between devices: 23.3 us -> 11.1 us  [swapped(): lax.ppermute(value, axis, [(i, i ^ mask) for i in range(lax.axis_size(axi...]
    ppermute x4 -> x6, starting transfers between devices: 6.58 us -> 13.3 us  [shifted(): lax.ppermute(value, axis, [(i, i + by) for i in range(size) if 0 <= i + b...]
    ppermute x4 -> x6, waiting for transfers between devices: 0.01 us -> 2.73 us  [shifted(): lax.ppermute(value, axis, [(i, i + by) for i in range(size) if 0 <= i + b...]
  transfers between devices with their start and end apart: 10 -> 12, of which waited for: 5 -> 5; matrix products, arithmetic and copies ran while one was open for 0% -> 0% of each run, Pallas kernels for 6% -> 6%
where the time goes in v12:
time: 56.4 us; the launch traced here: 56.2 us
  starting transfers between devices  26.6 us (47%)
  waiting for transfers between devices  14.8 us (26%)
  Pallas kernels  13.8 us (24%)
  between operations  0.79 us (1%)
    pallas_call x6, Pallas kernels, vmem_call(): pl.pallas_call(kernel, out_shape=out_shape, in_specs=[smem] * len(smem_in...  13.8 us
    ppermute x6, starting transfers between devices, shifted(): lax.ppermute(value, axis, [(i, i + by) for i in range(size) if 0 <= i + b...  13.3 us
    ppermute x5, starting transfers between devices, swapped(): lax.ppermute(value, axis, [(i, i ^ mask) for i in range(lax.axis_size(axi...  12.7 us
    ppermute x5, waiting for transfers between devices, swapped(): lax.ppermute(value, axis, [(i, i ^ mask) for i in range(lax.axis_size(axi...  11.1 us
    ppermute x6, waiting for transfers between devices, shifted(): lax.ppermute(value, axis, [(i, i + by) for i in range(size) if 0 <= i + b...  2.73 us
  transfers between devices with their start and end apart: 12, of which 5 were waited for; matrix products, arithmetic and copies ran while one was open for 0% of the time, Pallas kernels for 6%

profile of v12, /device:TPU:0, one launch (start us, length us, event | category | flops | bytes accessed | tf_op | source)
XLA Modules:
  0.0 56.2 jit_solution(12019818061591749342)
XLA Ops:
  0.6 0.1 pad_add_fusion.place_ref
  0.7 7.8 %shard_map.50 = (f32[2,2,32,8,128]{4,3,2,1,0:T(8,128)S(1)}, f32[2,2,32,8,128]{4,3,2,1,0:T(8,128)S(1)}) custom-call(s32[3]{0:T(128)S(1)} %pad_add_fusion.place_ref, f32[8,88,128]{2,1,0:T(8,128)} %constant.35.clone.weights_hbm, f32[2,2,8,4096]{3,2,1,0:T(8,128)} %iterate_ref.4, f32[2,2,8,4096]{3,2,1,0:T(8,128)} %forcing_ref.2), custom_call_target="tpu_custom_call" | custom-call | flops 1000000 | bytes 25165824 | tf_op jit(solution)/shard_map/pallas_call | solution.py:205
  8.6 0.5 collective-permute-start
  9.1 0.5 shard_map.51
  9.6 1.0 %collective-permute-done.received_any = f32[2,2,32,8,128]{4,3,2,1,0:T(8,128)S(1)} collective-permute-done((f32[2,2,32,8,128]{4,3,2,1,0:T(8,128)S(1)}, f32[2,2,32,8,128]{4,3,2,1,0:T(8,128)S(1)}, u32[]{:S(2)}, u32[]{:S(2)}) %collective-permute-start) | collective-permute-done | bytes 524320 | tf_op jit(solution)/shard_map/ppermute | solution.py:450
  10.6 1.3 %shard_map.52 = (f32[2,32,8,128]{3,2,1,0:T(8,128)S(1)}, f32[2,32,8,128]{3,2,1,0:T(8,128)S(1)}) custom-call(s32[3]{0:T(128)S(1)} %pad_add_fusion.place_ref, f32[2,2,32,8,128]{4,3,2,1,0:T(8,128)S(1)} %get-tuple-element.32.keep_ref, f32[2,2,32,8,128]{4,3,2,1,0:T(8,128)S(1)} %collective-permute-done.received_any), custom_call_target="tpu_custom_call" | custom-call | flops 1000000 | bytes 1048576 | tf_op jit(solution)/shard_map/pallas_call | solution.py:205
  11.9 2.9 %collective-permute-start.1 = (f32[2,32,8,128]{3,2,1,0:T(8,128)S(1)}, f32[2,32,8,128]{3,2,1,0:T(8,128)S(1)}, u32[]{:S(2)}, u32[]{:S(2)}) collective-permute-start(f32[2,32,8,128]{3,2,1,0:T(8,128)S(1)} %get-tuple-element.40), channel_id=1, source_target_pairs={{0,2},{2,0},{1,3},{3,1},{4,6},{6,4},{5,7},{7,5},{8,10},{10,8},{9,1... | collective-permute-start | bytes 786440 | tf_op jit(solution)/shard_map/ppermute | solution.py:413
  14.9 3.4 %collective-permute-start.4 = (f32[8,4096]{1,0:T(8,128)S(1)}, f32[8,4096]{1,0:T(8,128)S(1)}, u32[]{:S(2)}, u32[]{:S(2)}) collective-permute-start(f32[8,4096]{1,0:T(8,128)S(1)} %get-tuple-element.55), channel_id=1, source_target_pairs={{0,4},{4,8},{8,12},{12,16},{16,20},{20,24},{24,28},{1,5},{5,9},{9,... | collective-permute-start | bytes 393224 | tf_op jit(solution)/shard_map/ppermute | solution.py:418
  18.3 1.3 %collective-permute-start.5 = (f32[8,4096]{1,0:T(8,128)S(1)}, f32[8,4096]{1,0:T(8,128)S(1)}, u32[]{:S(2)}, u32[]{:S(2)}) collective-permute-start(f32[8,4096]{1,0:T(8,128)S(1)} %get-tuple-element.54), channel_id=1, source_target_pairs={{4,0},{8,4},{12,8},{16,12},{20,16},{24,20},{28,24},{5,1},{9,5},{13... | collective-permute-start | bytes 393224 | tf_op jit(solution)/shard_map/ppermute | solution.py:418
  19.6 1.5 %collective-permute-start.2 = (f32[8,4096]{1,0:T(8,128)S(1)}, f32[8,4096]{1,0:T(8,128)S(1)}, u32[]{:S(2)}, u32[]{:S(2)}) collective-permute-start(f32[8,4096]{1,0:T(8,128)S(1)} %get-tuple-element.37.up_ref), channel_id=1, source_target_pairs={{0,1},{1,2},{2,3},{4,5},{5,6},{6,7},{8,9},{9,10},{10,11},{12,13},{... | collective-permute-start | bytes 393224 | tf_op jit(solution)/shard_map/ppermute | solution.py:418
  21.1 1.3 %collective-permute-start.3 = (f32[8,4096]{1,0:T(8,128)S(1)}, f32[8,4096]{1,0:T(8,128)S(1)}, u32[]{:S(2)}, u32[]{:S(2)}) collective-permute-start(f32[8,4096]{1,0:T(8,128)S(1)} %get-tuple-element.38.down_ref), channel_id=1, source_target_pairs={{1,0},{2,1},{3,2},{5,4},{6,5},{7,6},{9,8},{10,9},{11,10},{13,12},{... | collective-permute-start | bytes 393224 | tf_op jit(solution)/shard_map/ppermute | solution.py:418
  22.5 2.7 %collective-permute-done.5.next_ref = f32[8,4096]{1,0:T(8,128)S(1)} collective-permute-done((f32[8,4096]{1,0:T(8,128)S(1)}, f32[8,4096]{1,0:T(8,128)S(1)}, u32[]{:S(2)}, u32[]{:S(2)}) %collective-permute-start.5) | collective-permute-done | bytes 131104 | tf_op jit(solution)/shard_map/ppermute | solution.py:418
  25.2 2.4 %collective-permute-start.6 = (f32[32,8,128]{2,1,0:T(8,128)S(1)}, f32[32,8,128]{2,1,0:T(8,128)S(1)}, u32[]{:S(2)}, u32[]{:S(2)}) collective-permute-start(f32[32,8,128]{2,1,0:T(8,128)S(1)} %add_bitcast_fusion), channel_id=1, source_target_pairs={{0,4},{4,0},{8,12},{12,8},{16,20},{20,16},{24,28},{28,24},{1,5},{5... | collective-permute-start | bytes 393224 | tf_op jit(solution)/shard_map/ppermute | solution.py:413
  27.6 0.8 %shard_map.53 = (f32[2,2,8,4096]{3,2,1,0:T(8,128)S(1)}, f32[8,4096]{1,0:T(8,128)S(1)}, f32[40,8,128]{2,1,0:T(8,128)S(1)}, f32[40,8,128]{2,1,0:T(8,128)S(1)}) custom-call(s32[3]{0:T(128)S(1)} %pad_add_fusion.place_ref, f32[2,2,8,4096]{3,2,1,0:T(8,128)S(1)} %copy-done, f32[2,2,8,4096]{3,2,1,0:T(8,128)S(1)} %get-tuple-element.31.first_ref, ...), custom_call_target="tpu_custom_call" | custom-call | flops 1000000 | bytes 1048576 | tf_op jit(solution)/shard_map/pallas_call | solution.py:205
  28.5 2.1 %collective-permute-done.6 = f32[32,8,128]{2,1,0:T(8,128)S(1)} collective-permute-done((f32[32,8,128]{2,1,0:T(8,128)S(1)}, f32[32,8,128]{2,1,0:T(8,128)S(1)}, u32[]{:S(2)}, u32[]{:S(2)}) %collective-permute-start.6) | collective-permute-done | bytes 131104 | tf_op jit(solution)/shard_map/ppermute | solution.py:413
  30.6 3.0 %collective-permute-start.7 = (f32[32,8,128]{2,1,0:T(8,128)S(1)}, f32[32,8,128]{2,1,0:T(8,128)S(1)}, u32[]{:S(2)}, u32[]{:S(2)}) collective-permute-start(f32[32,8,128]{2,1,0:T(8,128)S(1)} %bitcast_add_fusion), channel_id=1, source_target_pairs={{0,8},{4,12},{8,0},{12,4},{16,24},{20,28},{24,16},{28,20},{1,9},{5... | collective-permute-start | bytes 393224 | tf_op jit(solution)/shard_map/ppermute | solution.py:413
  33.6 1.3 %collective-permute-start.10 = (f32[40,8,128]{2,1,0:T(8,128)S(1)}, f32[40,8,128]{2,1,0:T(8,128)S(1)}, u32[]{:S(2)}, u32[]{:S(2)}) collective-permute-start(f32[40,8,128]{2,1,0:T(8,128)S(1)} %get-tuple-element.49), channel_id=1, source_target_pairs={{4,0},{8,4},{12,8},{16,12},{20,16},{24,20},{28,24},{5,1},{9,5},{13... | collective-permute-start | bytes 491528 | tf_op jit(solution)/shard_map/ppermute | solution.py:418
  34.9 4.6 %collective-permute-start.9 = (f32[40,8,128]{2,1,0:T(8,128)S(1)}, f32[40,8,128]{2,1,0:T(8,128)S(1)}, u32[]{:S(2)}, u32[]{:S(2)}) collective-permute-start(f32[40,8,128]{2,1,0:T(8,128)S(1)} %get-tuple-element.48), channel_id=1, source_target_pairs={{0,4},{4,8},{8,12},{12,16},{16,20},{20,24},{24,28},{1,5},{5,9},{9,... | collective-permute-start | bytes 491528 | tf_op jit(solution)/shard_map/ppermute | solution.py:418
  39.5 2.6 %collective-permute-start.8 = (f32[32,8,128]{2,1,0:T(8,128)S(1)}, f32[32,8,128]{2,1,0:T(8,128)S(1)}, u32[]{:S(2)}, u32[]{:S(2)}) collective-permute-start(f32[32,8,128]{2,1,0:T(8,128)S(1)} %add.42), channel_id=1, source_target_pairs={{0,16},{4,20},{8,24},{12,28},{16,0},{20,4},{24,8},{28,12},{1,17},{... | collective-permute-start | bytes 393224 | tf_op jit(solution)/shard_map/ppermute | solution.py:413
  42.1 6.9 %collective-permute-done.8 = f32[32,8,128]{2,1,0:T(8,128)S(1)} collective-permute-done((f32[32,8,128]{2,1,0:T(8,128)S(1)}, f32[32,8,128]{2,1,0:T(8,128)S(1)}, u32[]{:S(2)}, u32[]{:S(2)}) %collective-permute-start.8) | collective-permute-done | bytes 131104 | tf_op jit(solution)/shard_map/ppermute | solution.py:413
  49.0 1.7 %collective-permute-start.11 = (f32[32,8,128]{2,1,0:T(8,128)S(1)}, f32[32,8,128]{2,1,0:T(8,128)S(1)}, u32[]{:S(2)}, u32[]{:S(2)}) collective-permute-start(f32[32,8,128]{2,1,0:T(8,128)S(1)} %add.43.mine_ref), channel_id=1, source_target_pairs={{0,4},{4,0},{8,12},{12,8},{16,20},{20,16},{24,28},{28,24},{1,5},{5... | collective-permute-start | bytes 393224 | tf_op jit(solution)/shard_map/ppermute | solution.py:413
  50.8 1.9 %shard_map.54 = f32[2,2,8,4096]{3,2,1,0:T(8,128)} custom-call(s32[3]{0:T(128)S(1)} %pad_add_fusion.place_ref, f32[2,2,8,4096]{3,2,1,0:T(8,128)S(1)} %copy-done, f32[2,2,8,4096]{3,2,1,0:T(8,128)S(1)} %copy-done.1, f32[2,2,8,4096]{3,2,1,0:T(8,128)S(1)} %get-tuple-element.43.swept_ref, f32[8,4096]{1,0:T(8,128)S(1)} %get-tuple-element.44.edge_ref, ...), custom_call_target="tpu_custom_call" | custom-call | flops 1000000 | bytes 67108864 | tf_op jit(solution)/shard_map/pallas_call | solution.py:205
  52.7 2.1 %collective-permute-done.11.given_ref = f32[32,8,128]{2,1,0:T(8,128)S(1)} collective-permute-done((f32[32,8,128]{2,1,0:T(8,128)S(1)}, f32[32,8,128]{2,1,0:T(8,128)S(1)}, u32[]{:S(2)}, u32[]{:S(2)}) %collective-permute-start.11) | collective-permute-done | bytes 131104 | tf_op jit(solution)/shard_map/ppermute | solution.py:413
  54.8 1.4 %shard_map.55 = f32[2,2,8,4096]{3,2,1,0:T(8,128)} custom-call(s32[3]{0:T(128)S(1)} %pad_add_fusion.place_ref, f32[32,8,128]{2,1,0:T(8,128)S(1)} %add.43.mine_ref, f32[32,8,128]{2,1,0:T(8,128)S(1)} %collective-permute-done.11.given_ref), custom_call_target="tpu_custom_call" | custom-call | flops 1000000 | bytes 1048576 | tf_op jit(solution)/shard_map/pallas_call | solution.py:205
  (16 shorter events, 0.1 us)
Async XLA Ops:
  0.7 8.4 %copy-start = (f32[2,2,8,4096]{3,2,1,0:T(8,128)S(1)}, f32[2,2,8,4096]{3,2,1,0:T(8,128)}, u32[]{:S(2)}) copy-start(f32[2,2,8,4096]{3,2,1,0:T(8,128)} %iterate_ref.4) | copy-start | bytes 1572868
  0.7 8.4 %copy-start.1 = (f32[2,2,8,4096]{3,2,1,0:T(8,128)S(1)}, f32[2,2,8,4096]{3,2,1,0:T(8,128)}, u32[]{:S(2)}) copy-start(f32[2,2,8,4096]{3,2,1,0:T(8,128)} %forcing_ref.2) | copy-start | bytes 1572868
  8.6 2.1 %collective-permute-start = (f32[2,2,32,8,128]{4,3,2,1,0:T(8,128)S(1)}, f32[2,2,32,8,128]{4,3,2,1,0:T(8,128)S(1)}, u32[]{:S(2)}, u32[]{:S(2)}) collective-permute-start(f32[2,2,32,8,128]{4,3,2,1,0:T(8,128)S(1)} %get-tuple-element.33), channel_id=1, source_target_pairs={{0,1},{1,0},{2,3},{3,2},{4,5},{5,4},{6,7},{7,6},{8,9},{9,8},{10,11... | collective-permute-start | bytes 1572872 | tf_op jit(solution)/shard_map/ppermute | solution.py:450
  11.9 10.5 %collective-permute-start.1 = (f32[2,32,8,128]{3,2,1,0:T(8,128)S(1)}, f32[2,32,8,128]{3,2,1,0:T(8,128)S(1)}, u32[]{:S(2)}, u32[]{:S(2)}) collective-permute-start(f32[2,32,8,128]{3,2,1,0:T(8,128)S(1)} %get-tuple-element.40), channel_id=1, source_target_pairs={{0,2},{2,0},{1,3},{3,1},{4,6},{6,4},{5,7},{7,5},{8,10},{10,8},{9,1... | collective-permute-start | bytes 786440 | tf_op jit(solution)/shard_map/ppermute | solution.py:413
  14.9 7.6 %collective-permute-start.4 = (f32[8,4096]{1,0:T(8,128)S(1)}, f32[8,4096]{1,0:T(8,128)S(1)}, u32[]{:S(2)}, u32[]{:S(2)}) collective-permute-start(f32[8,4096]{1,0:T(8,128)S(1)} %get-tuple-element.55), channel_id=1, source_target_pairs={{0,4},{4,8},{8,12},{12,16},{16,20},{20,24},{24,28},{1,5},{5,9},{9,... | collective-permute-start | bytes 393224 | tf_op jit(solution)/shard_map/ppermute | solution.py:418
  18.3 6.9 %collective-permute-start.5 = (f32[8,4096]{1,0:T(8,128)S(1)}, f32[8,4096]{1,0:T(8,128)S(1)}, u32[]{:S(2)}, u32[]{:S(2)}) collective-permute-start(f32[8,4096]{1,0:T(8,128)S(1)} %get-tuple-element.54), channel_id=1, source_target_pairs={{4,0},{8,4},{12,8},{16,12},{20,16},{24,20},{28,24},{5,1},{9,5},{13... | collective-permute-start | bytes 393224 | tf_op jit(solution)/shard_map/ppermute | solution.py:418
  19.6 5.6 %collective-permute-start.2 = (f32[8,4096]{1,0:T(8,128)S(1)}, f32[8,4096]{1,0:T(8,128)S(1)}, u32[]{:S(2)}, u32[]{:S(2)}) collective-permute-start(f32[8,4096]{1,0:T(8,128)S(1)} %get-tuple-element.37.up_ref), channel_id=1, source_target_pairs={{0,1},{1,2},{2,3},{4,5},{5,6},{6,7},{8,9},{9,10},{10,11},{12,13},{... | collective-permute-start | bytes 393224 | tf_op jit(solution)/shard_map/ppermute | solution.py:418
  21.1 4.1 %collective-permute-start.3 = (f32[8,4096]{1,0:T(8,128)S(1)}, f32[8,4096]{1,0:T(8,128)S(1)}, u32[]{:S(2)}, u32[]{:S(2)}) collective-permute-start(f32[8,4096]{1,0:T(8,128)S(1)} %get-tuple-element.38.down_ref), channel_id=1, source_target_pairs={{1,0},{2,1},{3,2},{5,4},{6,5},{7,6},{9,8},{10,9},{11,10},{13,12},{... | collective-permute-start | bytes 393224 | tf_op jit(solution)/shard_map/ppermute | solution.py:418
  25.2 5.4 %collective-permute-start.6 = (f32[32,8,128]{2,1,0:T(8,128)S(1)}, f32[32,8,128]{2,1,0:T(8,128)S(1)}, u32[]{:S(2)}, u32[]{:S(2)}) collective-permute-start(f32[32,8,128]{2,1,0:T(8,128)S(1)} %add_bitcast_fusion), channel_id=1, source_target_pairs={{0,4},{4,0},{8,12},{12,8},{16,20},{20,16},{24,28},{28,24},{1,5},{5... | collective-permute-start | bytes 393224 | tf_op jit(solution)/shard_map/ppermute | solution.py:413
  30.6 8.9 %collective-permute-start.7 = (f32[32,8,128]{2,1,0:T(8,128)S(1)}, f32[32,8,128]{2,1,0:T(8,128)S(1)}, u32[]{:S(2)}, u32[]{:S(2)}) collective-permute-start(f32[32,8,128]{2,1,0:T(8,128)S(1)} %bitcast_add_fusion), channel_id=1, source_target_pairs={{0,8},{4,12},{8,0},{12,4},{16,24},{20,28},{24,16},{28,20},{1,9},{5... | collective-permute-start | bytes 393224 | tf_op jit(solution)/shard_map/ppermute | solution.py:413
  33.6 15.4 %collective-permute-start.10 = (f32[40,8,128]{2,1,0:T(8,128)S(1)}, f32[40,8,128]{2,1,0:T(8,128)S(1)}, u32[]{:S(2)}, u32[]{:S(2)}) collective-permute-start(f32[40,8,128]{2,1,0:T(8,128)S(1)} %get-tuple-element.49), channel_id=1, source_target_pairs={{4,0},{8,4},{12,8},{16,12},{20,16},{24,20},{28,24},{5,1},{9,5},{13... | collective-permute-start | bytes 491528 | tf_op jit(solution)/shard_map/ppermute | solution.py:418
  34.9 14.1 %collective-permute-start.9 = (f32[40,8,128]{2,1,0:T(8,128)S(1)}, f32[40,8,128]{2,1,0:T(8,128)S(1)}, u32[]{:S(2)}, u32[]{:S(2)}) collective-permute-start(f32[40,8,128]{2,1,0:T(8,128)S(1)} %get-tuple-element.48), channel_id=1, source_target_pairs={{0,4},{4,8},{8,12},{12,16},{16,20},{20,24},{24,28},{1,5},{5,9},{9,... | collective-permute-start | bytes 491528 | tf_op jit(solution)/shard_map/ppermute | solution.py:418
  39.5 9.5 %collective-permute-start.8 = (f32[32,8,128]{2,1,0:T(8,128)S(1)}, f32[32,8,128]{2,1,0:T(8,128)S(1)}, u32[]{:S(2)}, u32[]{:S(2)}) collective-permute-start(f32[32,8,128]{2,1,0:T(8,128)S(1)} %add.42), channel_id=1, source_target_pairs={{0,16},{4,20},{8,24},{12,28},{16,0},{20,4},{24,8},{28,12},{1,17},{... | collective-permute-start | bytes 393224 | tf_op jit(solution)/shard_map/ppermute | solution.py:413
  49.0 5.7 %collective-permute-start.11 = (f32[32,8,128]{2,1,0:T(8,128)S(1)}, f32[32,8,128]{2,1,0:T(8,128)S(1)}, u32[]{:S(2)}, u32[]{:S(2)}) collective-permute-start(f32[32,8,128]{2,1,0:T(8,128)S(1)} %add.43.mine_ref), channel_id=1, source_target_pairs={{0,4},{4,0},{8,12},{12,8},{16,20},{20,16},{24,28},{28,24},{1,5},{5... | collective-permute-start | bytes 393224 | tf_op jit(solution)/shard_map/ppermute | solution.py:413

commit v13 on v12

--- a/solution.py
+++ b/solution.py
@@ -484,12 +484,13 @@
     )
     mine, _, _ = lax.optimization_barrier((mine, forth, back))
     mask = 2
+    forth = shifted(forth, "tm", 1)
+    back = shifted(back, "tm", -1)
     while mask < ranks:
+        if 2 * mask == ranks:
+            mine, forth, back = lax.optimization_barrier((mine, forth, back))
         mine = mine + swapped(mine, "tm", mask)
         mask *= 2
-    forth = shifted(forth, "tm", 1)
-    back = shifted(back, "tm", -1)
-    mine, forth, back = lax.optimization_barrier((mine, forth, back))
     given = swapped(mine, "tm", 1)
     (coarse,) = vmem_call(last_kernel, (iterate.shape,), (place,), (mine, given))
     (smoothed,) = vmem_call(

time: 56.4 us -> 59.5 us (1.055)
  waiting for transfers between devices: 14.8 us -> 20 us
  starting transfers between devices: 26.6 us -> 24.4 us
    ppermute x5, waiting for transfers between devices: 11.1 us -> 16.3 us  [swapped(): lax.ppermute(value, axis, [(i, i ^ mask) for i in range(lax.axis_size(axi...]
    ppermute x6, starting transfers between devices: 13.3 us -> 10.7 us  [shifted(): lax.ppermute(value, axis, [(i, i + by) for i in range(size) if 0 <= i + b...]
  transfers between devices with their start and end apart: 12 -> 12, of which waited for: 5 -> 5; matrix products, arithmetic and copies ran while one was open for 0% -> 0% of each run, Pallas kernels for 6% -> 5%
where the time goes in v13:
time: 59.5 us; the launch traced here: 59.2 us
  starting transfers between devices  24.4 us (41%)
  waiting for transfers between devices  20 us (34%)
  Pallas kernels  13.8 us (23%)
  between operations  0.79 us (1%)
    ppermute x5, waiting for transfers between devices, swapped(): lax.ppermute(value, axis, [(i, i ^ mask) for i in range(lax.axis_size(axi...  16.3 us
    pallas_call x6, Pallas kernels, vmem_call(): pl.pallas_call(kernel, out_shape=out_shape, in_specs=[smem] * len(smem_in...  13.8 us
    ppermute x5, starting transfers between devices, swapped(): lax.ppermute(value, axis, [(i, i ^ mask) for i in range(lax.axis_size(axi...  13.1 us
    ppermute x6, starting transfers between devices, shifted(): lax.ppermute(value, axis, [(i, i + by) for i in range(size) if 0 <= i + b...  10.7 us
    ppermute x6, waiting for transfers between devices, shifted(): lax.ppermute(value, axis, [(i, i + by) for i in range(size) if 0 <= i + b...  2.73 us
  transfers between devices with their start and end apart: 12, of which 5 were waited for; matrix products, arithmetic and copies ran while one was open for 0% of the time, Pallas kernels for 5%

profile of v13, /device:TPU:0, one launch (start us, length us, event | category | flops | bytes accessed | tf_op | source)
XLA Modules:
  0.0 59.2 jit_solution(11867951700450984157)
XLA Ops:
  0.6 0.1 pad_add_fusion.place_ref
  0.7 7.8 %shard_map.50 = (f32[2,2,32,8,128]{4,3,2,1,0:T(8,128)S(1)}, f32[2,2,32,8,128]{4,3,2,1,0:T(8,128)S(1)}) custom-call(s32[3]{0:T(128)S(1)} %pad_add_fusion.place_ref, f32[8,88,128]{2,1,0:T(8,128)} %constant.35.clone.weights_hbm, f32[2,2,8,4096]{3,2,1,0:T(8,128)} %iterate_ref.4, f32[2,2,8,4096]{3,2,1,0:T(8,128)} %forcing_ref.2), custom_call_target="tpu_custom_call" | custom-call | flops 1000000 | bytes 25165824 | tf_op jit(solution)/shard_map/pallas_call | solution.py:205
  8.6 0.5 collective-permute-start
  9.1 0.5 shard_map.51
  9.6 1.0 %collective-permute-done.received_any = f32[2,2,32,8,128]{4,3,2,1,0:T(8,128)S(1)} collective-permute-done((f32[2,2,32,8,128]{4,3,2,1,0:T(8,128)S(1)}, f32[2,2,32,8,128]{4,3,2,1,0:T(8,128)S(1)}, u32[]{:S(2)}, u32[]{:S(2)}) %collective-permute-start) | collective-permute-done | bytes 524320 | tf_op jit(solution)/shard_map/ppermute | solution.py:450
  10.6 1.3 %shard_map.52 = (f32[2,32,8,128]{3,2,1,0:T(8,128)S(1)}, f32[2,32,8,128]{3,2,1,0:T(8,128)S(1)}) custom-call(s32[3]{0:T(128)S(1)} %pad_add_fusion.place_ref, f32[2,2,32,8,128]{4,3,2,1,0:T(8,128)S(1)} %get-tuple-element.32.keep_ref, f32[2,2,32,8,128]{4,3,2,1,0:T(8,128)S(1)} %collective-permute-done.received_any), custom_call_target="tpu_custom_call" | custom-call | flops 1000000 | bytes 1048576 | tf_op jit(solution)/shard_map/pallas_call | solution.py:205
  11.9 2.9 %collective-permute-start.1 = (f32[2,32,8,128]{3,2,1,0:T(8,128)S(1)}, f32[2,32,8,128]{3,2,1,0:T(8,128)S(1)}, u32[]{:S(2)}, u32[]{:S(2)}) collective-permute-start(f32[2,32,8,128]{3,2,1,0:T(8,128)S(1)} %get-tuple-element.40), channel_id=1, source_target_pairs={{0,2},{2,0},{1,3},{3,1},{4,6},{6,4},{5,7},{7,5},{8,10},{10,8},{9,1... | collective-permute-start | bytes 786440 | tf_op jit(solution)/shard_map/ppermute | solution.py:413
  14.9 3.4 %collective-permute-start.4 = (f32[8,4096]{1,0:T(8,128)S(1)}, f32[8,4096]{1,0:T(8,128)S(1)}, u32[]{:S(2)}, u32[]{:S(2)}) collective-permute-start(f32[8,4096]{1,0:T(8,128)S(1)} %get-tuple-element.55), channel_id=1, source_target_pairs={{0,4},{4,8},{8,12},{12,16},{16,20},{20,24},{24,28},{1,5},{5,9},{9,... | collective-permute-start | bytes 393224 | tf_op jit(solution)/shard_map/ppermute | solution.py:418
  18.3 1.3 %collective-permute-start.5 = (f32[8,4096]{1,0:T(8,128)S(1)}, f32[8,4096]{1,0:T(8,128)S(1)}, u32[]{:S(2)}, u32[]{:S(2)}) collective-permute-start(f32[8,4096]{1,0:T(8,128)S(1)} %get-tuple-element.54), channel_id=1, source_target_pairs={{4,0},{8,4},{12,8},{16,12},{20,16},{24,20},{28,24},{5,1},{9,5},{13... | collective-permute-start | bytes 393224 | tf_op jit(solution)/shard_map/ppermute | solution.py:418
  19.6 1.5 %collective-permute-start.2 = (f32[8,4096]{1,0:T(8,128)S(1)}, f32[8,4096]{1,0:T(8,128)S(1)}, u32[]{:S(2)}, u32[]{:S(2)}) collective-permute-start(f32[8,4096]{1,0:T(8,128)S(1)} %get-tuple-element.37.up_ref), channel_id=1, source_target_pairs={{0,1},{1,2},{2,3},{4,5},{5,6},{6,7},{8,9},{9,10},{10,11},{12,13},{... | collective-permute-start | bytes 393224 | tf_op jit(solution)/shard_map/ppermute | solution.py:418
  21.1 1.3 %collective-permute-start.3 = (f32[8,4096]{1,0:T(8,128)S(1)}, f32[8,4096]{1,0:T(8,128)S(1)}, u32[]{:S(2)}, u32[]{:S(2)}) collective-permute-start(f32[8,4096]{1,0:T(8,128)S(1)} %get-tuple-element.38.down_ref), channel_id=1, source_target_pairs={{1,0},{2,1},{3,2},{5,4},{6,5},{7,6},{9,8},{10,9},{11,10},{13,12},{... | collective-permute-start | bytes 393224 | tf_op jit(solution)/shard_map/ppermute | solution.py:418
  22.5 2.7 %collective-permute-done.5.next_ref = f32[8,4096]{1,0:T(8,128)S(1)} collective-permute-done((f32[8,4096]{1,0:T(8,128)S(1)}, f32[8,4096]{1,0:T(8,128)S(1)}, u32[]{:S(2)}, u32[]{:S(2)}) %collective-permute-start.5) | collective-permute-done | bytes 131104 | tf_op jit(solution)/shard_map/ppermute | solution.py:418
  25.2 2.4 %collective-permute-start.6 = (f32[32,8,128]{2,1,0:T(8,128)S(1)}, f32[32,8,128]{2,1,0:T(8,128)S(1)}, u32[]{:S(2)}, u32[]{:S(2)}) collective-permute-start(f32[32,8,128]{2,1,0:T(8,128)S(1)} %add_bitcast_fusion), channel_id=1, source_target_pairs={{0,4},{4,0},{8,12},{12,8},{16,20},{20,16},{24,28},{28,24},{1,5},{5... | collective-permute-start | bytes 393224 | tf_op jit(solution)/shard_map/ppermute | solution.py:413
  27.6 0.8 %shard_map.53 = (f32[2,2,8,4096]{3,2,1,0:T(8,128)S(1)}, f32[8,4096]{1,0:T(8,128)S(1)}, f32[40,8,128]{2,1,0:T(8,128)S(1)}, f32[40,8,128]{2,1,0:T(8,128)S(1)}) custom-call(s32[3]{0:T(128)S(1)} %pad_add_fusion.place_ref, f32[2,2,8,4096]{3,2,1,0:T(8,128)S(1)} %copy-done, f32[2,2,8,4096]{3,2,1,0:T(8,128)S(1)} %get-tuple-element.31.first_ref, ...), custom_call_target="tpu_custom_call" | custom-call | flops 1000000 | bytes 1048576 | tf_op jit(solution)/shard_map/pallas_call | solution.py:205
  28.5 1.9 %collective-permute-start.8 = (f32[40,8,128]{2,1,0:T(8,128)S(1)}, f32[40,8,128]{2,1,0:T(8,128)S(1)}, u32[]{:S(2)}, u32[]{:S(2)}) collective-permute-start(f32[40,8,128]{2,1,0:T(8,128)S(1)} %get-tuple-element.48), channel_id=1, source_target_pairs={{0,4},{4,8},{8,12},{12,16},{16,20},{20,24},{24,28},{1,5},{5,9},{9,... | collective-permute-start | bytes 491528 | tf_op jit(solution)/shard_map/ppermute | solution.py:418
  30.4 1.3 %collective-permute-start.9 = (f32[40,8,128]{2,1,0:T(8,128)S(1)}, f32[40,8,128]{2,1,0:T(8,128)S(1)}, u32[]{:S(2)}, u32[]{:S(2)}) collective-permute-start(f32[40,8,128]{2,1,0:T(8,128)S(1)} %get-tuple-element.49), channel_id=1, source_target_pairs={{4,0},{8,4},{12,8},{16,12},{20,16},{24,20},{28,24},{5,1},{9,5},{13... | collective-permute-start | bytes 491528 | tf_op jit(solution)/shard_map/ppermute | solution.py:418
  31.7 5.2 %collective-permute-start.7 = (f32[32,8,128]{2,1,0:T(8,128)S(1)}, f32[32,8,128]{2,1,0:T(8,128)S(1)}, u32[]{:S(2)}, u32[]{:S(2)}) collective-permute-start(f32[32,8,128]{2,1,0:T(8,128)S(1)} %bitcast_add_fusion), channel_id=1, source_target_pairs={{0,8},{4,12},{8,0},{12,4},{16,24},{20,28},{24,16},{28,20},{1,9},{5... | collective-permute-start | bytes 393224 | tf_op jit(solution)/shard_map/ppermute | solution.py:413
  36.9 5.4 %collective-permute-done.7 = f32[32,8,128]{2,1,0:T(8,128)S(1)} collective-permute-done((f32[32,8,128]{2,1,0:T(8,128)S(1)}, f32[32,8,128]{2,1,0:T(8,128)S(1)}, u32[]{:S(2)}, u32[]{:S(2)}) %collective-permute-start.7) | collective-permute-done | bytes 131104 | tf_op jit(solution)/shard_map/ppermute | solution.py:413
  42.3 2.6 %collective-permute-start.10 = (f32[32,8,128]{2,1,0:T(8,128)S(1)}, f32[32,8,128]{2,1,0:T(8,128)S(1)}, u32[]{:S(2)}, u32[]{:S(2)}) collective-permute-start(f32[32,8,128]{2,1,0:T(8,128)S(1)} %add.42), channel_id=1, source_target_pairs={{0,16},{4,20},{8,24},{12,28},{16,0},{20,4},{24,8},{28,12},{1,17},{... | collective-permute-start | bytes 393224 | tf_op jit(solution)/shard_map/ppermute | solution.py:413
  44.9 7.0 %collective-permute-done.10 = f32[32,8,128]{2,1,0:T(8,128)S(1)} collective-permute-done((f32[32,8,128]{2,1,0:T(8,128)S(1)}, f32[32,8,128]{2,1,0:T(8,128)S(1)}, u32[]{:S(2)}, u32[]{:S(2)}) %collective-permute-start.10) | collective-permute-done | bytes 131104 | tf_op jit(solution)/shard_map/ppermute | solution.py:413
  51.9 0.1 collective-permute-start.11
  52.0 1.9 %shard_map.54 = f32[2,2,8,4096]{3,2,1,0:T(8,128)} custom-call(s32[3]{0:T(128)S(1)} %pad_add_fusion.place_ref, f32[2,2,8,4096]{3,2,1,0:T(8,128)S(1)} %copy-done, f32[2,2,8,4096]{3,2,1,0:T(8,128)S(1)} %copy-done.1, f32[2,2,8,4096]{3,2,1,0:T(8,128)S(1)} %get-tuple-element.43.swept_ref, f32[8,4096]{1,0:T(8,128)S(1)} %get-tuple-element.44.edge_ref, ...), custom_call_target="tpu_custom_call" | custom-call | flops 1000000 | bytes 67108864 | tf_op jit(solution)/shard_map/pallas_call | solution.py:205
  53.9 3.9 %collective-permute-done.11.given_ref = f32[32,8,128]{2,1,0:T(8,128)S(1)} collective-permute-done((f32[32,8,128]{2,1,0:T(8,128)S(1)}, f32[32,8,128]{2,1,0:T(8,128)S(1)}, u32[]{:S(2)}, u32[]{:S(2)}) %collective-permute-start.11) | collective-permute-done | bytes 131104 | tf_op jit(solution)/shard_map/ppermute | solution.py:413
  57.8 1.4 %shard_map.55 = f32[2,2,8,4096]{3,2,1,0:T(8,128)} custom-call(s32[3]{0:T(128)S(1)} %pad_add_fusion.place_ref, f32[32,8,128]{2,1,0:T(8,128)S(1)} %add.43.mine_ref, f32[32,8,128]{2,1,0:T(8,128)S(1)} %collective-permute-done.11.given_ref), custom_call_target="tpu_custom_call" | custom-call | flops 1000000 | bytes 1048576 | tf_op jit(solution)/shard_map/pallas_call | solution.py:205
  (16 shorter events, 0.1 us)
Async XLA Ops:
  0.7 8.4 %copy-start = (f32[2,2,8,4096]{3,2,1,0:T(8,128)S(1)}, f32[2,2,8,4096]{3,2,1,0:T(8,128)}, u32[]{:S(2)}) copy-start(f32[2,2,8,4096]{3,2,1,0:T(8,128)} %iterate_ref.4) | copy-start | bytes 1572868
  0.7 8.4 %copy-start.1 = (f32[2,2,8,4096]{3,2,1,0:T(8,128)S(1)}, f32[2,2,8,4096]{3,2,1,0:T(8,128)}, u32[]{:S(2)}) copy-start(f32[2,2,8,4096]{3,2,1,0:T(8,128)} %forcing_ref.2) | copy-start | bytes 1572868
  8.6 2.1 %collective-permute-start = (f32[2,2,32,8,128]{4,3,2,1,0:T(8,128)S(1)}, f32[2,2,32,8,128]{4,3,2,1,0:T(8,128)S(1)}, u32[]{:S(2)}, u32[]{:S(2)}) collective-permute-start(f32[2,2,32,8,128]{4,3,2,1,0:T(8,128)S(1)} %get-tuple-element.33), channel_id=1, source_target_pairs={{0,1},{1,0},{2,3},{3,2},{4,5},{5,4},{6,7},{7,6},{8,9},{9,8},{10,11... | collective-permute-start | bytes 1572872 | tf_op jit(solution)/shard_map/ppermute | solution.py:450
  11.9 10.5 %collective-permute-start.1 = (f32[2,32,8,128]{3,2,1,0:T(8,128)S(1)}, f32[2,32,8,128]{3,2,1,0:T(8,128)S(1)}, u32[]{:S(2)}, u32[]{:S(2)}) collective-permute-start(f32[2,32,8,128]{3,2,1,0:T(8,128)S(1)} %get-tuple-element.40), channel_id=1, source_target_pairs={{0,2},{2,0},{1,3},{3,1},{4,6},{6,4},{5,7},{7,5},{8,10},{10,8},{9,1... | collective-permute-start | bytes 786440 | tf_op jit(solution)/shard_map/ppermute | solution.py:413
  14.9 7.6 %collective-permute-start.4 = (f32[8,4096]{1,0:T(8,128)S(1)}, f32[8,4096]{1,0:T(8,128)S(1)}, u32[]{:S(2)}, u32[]{:S(2)}) collective-permute-start(f32[8,4096]{1,0:T(8,128)S(1)} %get-tuple-element.55), channel_id=1, source_target_pairs={{0,4},{4,8},{8,12},{12,16},{16,20},{20,24},{24,28},{1,5},{5,9},{9,... | collective-permute-start | bytes 393224 | tf_op jit(solution)/shard_map/ppermute | solution.py:418
  18.3 6.9 %collective-permute-start.5 = (f32[8,4096]{1,0:T(8,128)S(1)}, f32[8,4096]{1,0:T(8,128)S(1)}, u32[]{:S(2)}, u32[]{:S(2)}) collective-permute-start(f32[8,4096]{1,0:T(8,128)S(1)} %get-tuple-element.54), channel_id=1, source_target_pairs={{4,0},{8,4},{12,8},{16,12},{20,16},{24,20},{28,24},{5,1},{9,5},{13... | collective-permute-start | bytes 393224 | tf_op jit(solution)/shard_map/ppermute | solution.py:418
  19.6 5.6 %collective-permute-start.2 = (f32[8,4096]{1,0:T(8,128)S(1)}, f32[8,4096]{1,0:T(8,128)S(1)}, u32[]{:S(2)}, u32[]{:S(2)}) collective-permute-start(f32[8,4096]{1,0:T(8,128)S(1)} %get-tuple-element.37.up_ref), channel_id=1, source_target_pairs={{0,1},{1,2},{2,3},{4,5},{5,6},{6,7},{8,9},{9,10},{10,11},{12,13},{... | collective-permute-start | bytes 393224 | tf_op jit(solution)/shard_map/ppermute | solution.py:418
  21.1 4.1 %collective-permute-start.3 = (f32[8,4096]{1,0:T(8,128)S(1)}, f32[8,4096]{1,0:T(8,128)S(1)}, u32[]{:S(2)}, u32[]{:S(2)}) collective-permute-start(f32[8,4096]{1,0:T(8,128)S(1)} %get-tuple-element.38.down_ref), channel_id=1, source_target_pairs={{1,0},{2,1},{3,2},{5,4},{6,5},{7,6},{9,8},{10,9},{11,10},{13,12},{... | collective-permute-start | bytes 393224 | tf_op jit(solution)/shard_map/ppermute | solution.py:418
  25.2 6.5 %collective-permute-start.6 = (f32[32,8,128]{2,1,0:T(8,128)S(1)}, f32[32,8,128]{2,1,0:T(8,128)S(1)}, u32[]{:S(2)}, u32[]{:S(2)}) collective-permute-start(f32[32,8,128]{2,1,0:T(8,128)S(1)} %add_bitcast_fusion), channel_id=1, source_target_pairs={{0,4},{4,0},{8,12},{12,8},{16,20},{20,16},{24,28},{28,24},{1,5},{5... | collective-permute-start | bytes 393224 | tf_op jit(solution)/shard_map/ppermute | solution.py:413
  28.5 13.9 %collective-permute-start.8 = (f32[40,8,128]{2,1,0:T(8,128)S(1)}, f32[40,8,128]{2,1,0:T(8,128)S(1)}, u32[]{:S(2)}, u32[]{:S(2)}) collective-permute-start(f32[40,8,128]{2,1,0:T(8,128)S(1)} %get-tuple-element.48), channel_id=1, source_target_pairs={{0,4},{4,8},{8,12},{12,16},{16,20},{20,24},{24,28},{1,5},{5,9},{9,... | collective-permute-start | bytes 491528 | tf_op jit(solution)/shard_map/ppermute | solution.py:418
  30.4 11.9 %collective-permute-start.9 = (f32[40,8,128]{2,1,0:T(8,128)S(1)}, f32[40,8,128]{2,1,0:T(8,128)S(1)}, u32[]{:S(2)}, u32[]{:S(2)}) collective-permute-start(f32[40,8,128]{2,1,0:T(8,128)S(1)} %get-tuple-element.49), channel_id=1, source_target_pairs={{4,0},{8,4},{12,8},{16,12},{20,16},{24,20},{28,24},{5,1},{9,5},{13... | collective-permute-start | bytes 491528 | tf_op jit(solution)/shard_map/ppermute | solution.py:418
  31.7 10.5 %collective-permute-start.7 = (f32[32,8,128]{2,1,0:T(8,128)S(1)}, f32[32,8,128]{2,1,0:T(8,128)S(1)}, u32[]{:S(2)}, u32[]{:S(2)}) collective-permute-start(f32[32,8,128]{2,1,0:T(8,128)S(1)} %bitcast_add_fusion), channel_id=1, source_target_pairs={{0,8},{4,12},{8,0},{12,4},{16,24},{20,28},{24,16},{28,20},{1,9},{5... | collective-permute-start | bytes 393224 | tf_op jit(solution)/shard_map/ppermute | solution.py:413
  42.3 9.6 %collective-permute-start.10 = (f32[32,8,128]{2,1,0:T(8,128)S(1)}, f32[32,8,128]{2,1,0:T(8,128)S(1)}, u32[]{:S(2)}, u32[]{:S(2)}) collective-permute-start(f32[32,8,128]{2,1,0:T(8,128)S(1)} %add.42), channel_id=1, source_target_pairs={{0,16},{4,20},{8,24},{12,28},{16,0},{20,4},{24,8},{28,12},{1,17},{... | collective-permute-start | bytes 393224 | tf_op jit(solution)/shard_map/ppermute | solution.py:413
  51.9 5.9 %collective-permute-start.11 = (f32[32,8,128]{2,1,0:T(8,128)S(1)}, f32[32,8,128]{2,1,0:T(8,128)S(1)}, u32[]{:S(2)}, u32[]{:S(2)}) collective-permute-start(f32[32,8,128]{2,1,0:T(8,128)S(1)} %add.43.mine_ref), channel_id=1, source_target_pairs={{0,4},{4,0},{8,12},{12,8},{16,20},{20,16},{24,28},{28,24},{1,5},{5... | collective-permute-start | bytes 393224 | tf_op jit(solution)/shard_map/ppermute | solution.py:413
